TPU v7x, 32 devices: a whole 2x2x4 slice. The times are simulated.
32 devices in a mesh: groups: 2 (over x), tile: 16 (over z, y, core).
Axes of the slice: x: 2, y: 2, z: 4, core: 2. Of those that a mesh axis runs over, the one named last changes fastest.
Arguments:
- model_field: float32 [16, 524288], P(None, ('groups', 'tile')), parts along dimension 1, may hold values from -6 to 6
- direction: float32 [16, 524288], P(None, ('groups', 'tile')), parts along dimension 1, may hold values from -100 to 100
- old_grad: float32 [16, 524288], P(None, ('groups', 'tile')), parts along dimension 1, may hold values from -100 to 100
- residual: float32 [16, 65536], P(None, ('groups', 'tile')), parts along dimension 1, may hold values from -6 to 6
- block_pairs: int32 [256, 8], P(('groups', 'tile')), parts along dimension 0, may hold values from 0 to 159, as said below
- depth_band: int32 [524288], P(('groups', 'tile')), parts along dimension 0, may hold values from 0 to 15
- station_offsets: float32 [2, 65536], P(None, ('groups', 'tile')), parts along dimension 1, may hold values from -1.25 to 2.25, as said below
Outputs:
- new_model: float32 [16, 524288], P(None, ('groups', 'tile')), parts along dimension 1
- new_residual: float32 [16, 65536], P(None, ('groups', 'tile')), parts along dimension 1
- new_direction: float32 [16, 524288], P(None, ('groups', 'tile')), parts along dimension 1
There are 2 independent parts, one for each index of `groups`. A program takes and returns all parts, laid end to end along the dimension named above; each array names one. Nothing has to cross between parts.
Inputs may be any that keep to these rules, and one draw needn't show every extreme that they name: `block_pairs`: each row lists 8 different codes. `station_offsets`: row 1 (along) lies between 0 and 1.
All inputs are finite; a program needn't handle non-finite values.
Results may differ from a plain program's by a relative error of at most 0.0003.
Values sent between devices are 32-bit elements; how exact they have to be, the bound alone decides.
No kernel may reach another device: no remote copies, remote signals or barrier semaphores. Data moves between devices by JAX's collectives and lax.ppermute only.
A program may use at most 128 MiB of HBM per device.

v0:
```python
import functools
import math

import jax
import jax.numpy as jnp
from jax import lax
from jax.experimental import pallas as pl
from jax.experimental.pallas import tpu as pltpu
from jax.sharding import PartitionSpec as P

CBLOCK = 512
SBLOCK = 256
REACH = 2
BANDS = 16
COL_SIDE = 32
DEPTH_RANGE = 2.0
DEPTH_SHIFT = 0.25
DAMPING = 1.0
GUARD = 1e-06

F32 = jnp.float32
BF16 = jnp.bfloat16
LANES = 128
TILE = 256
HALF = TILE // 2

SMEM = pl.BlockSpec(memory_space=pltpu.SMEM)
VMEM = pl.BlockSpec(memory_space=pltpu.VMEM)


def params():
    return pltpu.CompilerParams(vmem_limit_bytes=48 * 2**20)


def split(values):
    high = values.astype(BF16)
    return high, (values - high.astype(F32)).astype(BF16)


def dot(left, right):
    return jnp.dot(left, right, preferred_element_type=F32)


def pack_kernel(offsets_ref, pairs_ref, message_ref):
    stations = offsets_ref.shape[1]
    message_ref[...] = jnp.zeros_like(message_ref)
    message_ref[pl.ds(0, 2), pl.ds(0, stations)] = offsets_ref[...]
    message_ref[:, pl.ds(stations, pairs_ref.shape[1])] = pairs_ref[...].astype(F32) + 1.0


def pack(station_offsets, block_pairs):
    rows, stations = block_pairs.shape[0], station_offsets.shape[1]
    return pl.pallas_call(
        pack_kernel,
        out_shape=jax.ShapeDtypeStruct((rows, stations + LANES), F32),
        in_specs=[VMEM] * 2,
        out_specs=VMEM,
        name="pack",
    )(station_offsets, block_pairs)


def prepare_kernel(scale, band_ref, band_row_ref, direction_ref, old_ref, values_ref, cells_ref, turned_ref, sums_ref):
    blocks = values_ref.shape[0]
    epochs = direction_ref.shape[0]
    depth = (band_ref[...].astype(F32) + 0.5) * (DEPTH_RANGE / BANDS)
    turned_ref[...] = (depth * depth).T

    def block(w, sums):
        at = pl.ds(pl.multiple_of(w * CBLOCK, CBLOCK), CBLOCK)
        row = (band_row_ref[:, at].astype(F32) + 0.5) * (DEPTH_RANGE / BANDS)
        shifted = row + DEPTH_SHIFT
        factor = row * scale * (shifted * jnp.sqrt(shifted))
        cells_ref[pl.ds(0, 1), at] = row * row
        cells_ref[pl.ds(1, 1), at] = factor
        values = direction_ref[:, at]
        old = old_ref[:, at]
        high, low = split(values * factor)
        values_ref[w, pl.ds(0, epochs), :] = high
        values_ref[w, pl.ds(epochs, epochs), :] = low
        return sums[0] + old * old, sums[1] + values * values

    zero = jnp.zeros((epochs, CBLOCK), F32)
    old_sum, direction_sum = lax.fori_loop(0, blocks, block, (zero, zero), unroll=2)
    sums_ref[pl.ds(0, 1), :] = jnp.broadcast_to(jnp.sum(old_sum).reshape(1, 1), (1, LANES))
    sums_ref[pl.ds(1, 1), :] = jnp.broadcast_to(jnp.sum(direction_sum).reshape(1, 1), (1, LANES))


def prepare(scale, depth_band, direction, old_grad):
    epochs, cells = direction.shape
    blocks = cells // CBLOCK
    return pl.pallas_call(
        functools.partial(prepare_kernel, scale),
        out_shape=(
            jax.ShapeDtypeStruct((blocks, 2 * epochs, CBLOCK), BF16),
            jax.ShapeDtypeStruct((2, cells), F32),
            jax.ShapeDtypeStruct((cells // LANES, LANES), F32),
            jax.ShapeDtypeStruct((2, LANES), F32),
        ),
        in_specs=[VMEM] * 4,
        out_specs=(VMEM,) * 4,
        compiler_params=params(),
        cost_estimate=pl.CostEstimate(flops=8 * epochs * cells, bytes_accessed=12 * epochs * cells, transcendentals=0),
        name="prepare",
    )(depth_band.reshape(cells // LANES, LANES), depth_band.reshape(1, cells), direction, old_grad)


def list_pairs(sizes, first_ref, codes, list_ref):
    cell_blocks, station_blocks, pairs = sizes[:3]
    count = jnp.int32(0)
    for slot, codes_ref in enumerate(codes):
        first = first_ref[slot]
        for q in range(station_blocks):
            for i in range(pairs):
                within = codes_ref[q, i].astype(jnp.int32) - first
                hit = jnp.logical_and(within >= 0, within < cell_blocks)
                list_ref[count] = (slot * station_blocks + q) * cell_blocks + within
                count = count + hit.astype(jnp.int32)
    for i in range(UNROLL + 4):
        list_ref[count + i] = len(codes) * station_blocks * cell_blocks
    return count


def pair_list(sizes):
    cell_blocks, station_blocks, pairs, epochs, slots = sizes
    return pltpu.SMEM((slots * station_blocks * pairs + UNROLL + 4,), jnp.int32)


def codes_spec(stations):
    return pl.BlockSpec((8, LANES), lambda i: (0, stations // LANES), memory_space=pltpu.SMEM)


UNROLL = 4


def pipelined(count, stage, issue, collect):
    stage(0, 0)
    stage(1, 1)
    issue(0, 0)

    def step(j, unused):
        for k in range(UNROLL):
            i, now, later = UNROLL * j + k, k % 2, 1 - k % 2
            issue(i + 1, later)
            stage(i + 2, now)
            collect(i, now)
        return 0

    rounds = (count + UNROLL - 2) // UNROLL
    lax.fori_loop(0, rounds, step, 0)
    collect(UNROLL * rounds, 0)


def multiply_add(sums_ref, left, pieces, unit, register):
    high, low = zip(*pieces)
    pltpu.matmul_push_rhs(jnp.concatenate(high + low, axis=0), register, unit)
    pltpu.matmul_acc_lhs(sums_ref, jnp.concatenate([left, left], axis=1), load_staged_rhs=register)


def accumulators(rows):
    return [pltpu.ACC(unit)((rows, TILE), F32) for unit in (0, 1)] * 2


def inverse_cube(squared):
    return lax.rsqrt(squared * squared * squared)


def forward_kernel(sizes, first_ref, shift_ref, *refs):
    cell_blocks, station_blocks, pairs, epochs, slots = sizes
    codes = refs[:slots]
    messages = refs[slots : 2 * slots]
    values_ref, turned_ref = refs[2 * slots : 2 * slots + 2]
    images = refs[2 * slots + 2 : 3 * slots + 2]
    list_ref, across_ref, along_ref, image_ref, gaps_ref, lines_ref, depths_ref = refs[3 * slots + 2 :]
    dummy = slots * station_blocks
    across_ref[pl.ds(dummy, 1), :] = jnp.zeros((1, SBLOCK), F32)
    along_ref[pl.ds(dummy, 1), :] = jnp.zeros((1, SBLOCK), F32)
    image_ref[...] = jnp.zeros_like(image_ref)
    for slot in range(slots):
        for q in range(station_blocks):
            at = pl.ds(q * SBLOCK, SBLOCK)
            row = pl.ds(slot * station_blocks + q, 1)
            across_ref[row, :] = messages[slot][pl.ds(0, 1), at] + shift_ref[slot]
            along_ref[row, :] = messages[slot][pl.ds(1, 1), at]
    count = list_pairs(sizes, first_ref, codes, list_ref)
    column = lax.broadcasted_iota(jnp.int32, (COL_SIDE, SBLOCK), 0).astype(F32)
    column = (column + 0.5) / COL_SIDE
    rows = CBLOCK // COL_SIDE

    def stage(i, k):
        code = list_ref[i]
        q, w = code // cell_blocks, code % cell_blocks
        across = across_ref[pl.ds(q, 1), :] - column
        gaps_ref[k] = across * across
        lines_ref[k] = along_ref[pl.ds(q, 1), :] - (w % 2).astype(F32) * (rows / COL_SIDE)
        turned = pltpu.roll(turned_ref[...], (LANES - w * (CBLOCK // LANES)) % LANES, 1)
        for part in range(CBLOCK // LANES):
            depths_ref[k, pl.ds(part * LANES, LANES), :] = jnp.broadcast_to(turned[:, part : part + 1], (LANES, LANES))

    def issue(sums, i, k):
        w = list_ref[i] % cell_blocks
        across = gaps_ref[k]
        along = lines_ref[k]
        for tile in range(CBLOCK // HALF):
            pieces = []
            for at in range(0, HALF, COL_SIDE):
                y = (tile * HALF + at) // COL_SIDE
                depth = depths_ref[k, pl.ds(y * COL_SIDE, COL_SIDE), :]
                depth = jnp.concatenate([depth] * (SBLOCK // LANES), axis=1)
                gap = along - (y + 0.5) / COL_SIDE
                pieces.append(split(inverse_cube((across + gap * gap) + depth)))
            left = values_ref[w, :, pl.ds(tile * HALF, HALF)]
            multiply_add(sums[2 * k + tile % 2], left, pieces, tile % 2, tile // 2)

    def collect(sums, i, k):
        q = list_ref[i] // cell_blocks
        both = pltpu.matmul_pop(sums[2 * k]) + pltpu.matmul_pop(sums[2 * k + 1])
        image_ref[q] += both[:epochs] + both[epochs:]

    def run(*sums):
        pipelined(count, stage, functools.partial(issue, sums), functools.partial(collect, sums))

    pl.run_scoped(run, *accumulators(2 * epochs))
    for slot in range(slots):
        images[slot][...] = image_ref[pl.ds(slot * station_blocks, station_blocks)]


def forward(sizes, first, shift, messages, values, turned):
    cell_blocks, station_blocks, pairs, epochs, slots = sizes
    stations = station_blocks * SBLOCK
    rows = (slots * station_blocks + 8) // 8 * 8
    return pl.pallas_call(
        functools.partial(forward_kernel, sizes),
        grid=(1,),
        out_shape=(jax.ShapeDtypeStruct((station_blocks, epochs, SBLOCK), F32),) * slots,
        in_specs=[SMEM, SMEM] + [codes_spec(stations)] * slots + [VMEM] * (slots + 2),
        out_specs=(VMEM,) * slots,
        scratch_shapes=[
            pair_list(sizes),
            pltpu.VMEM((rows, SBLOCK), F32),
            pltpu.VMEM((rows, SBLOCK), F32),
            pltpu.VMEM((slots * station_blocks + 1, epochs, SBLOCK), F32),
            pltpu.VMEM((2, COL_SIDE, SBLOCK), F32),
            pltpu.VMEM((2, 1, SBLOCK), F32),
            pltpu.VMEM((2, CBLOCK, LANES), F32),
        ],
        compiler_params=params(),
        cost_estimate=estimate(sizes),
        name="forward",
    )(first, shift, *messages, *messages, values, turned)


def estimate(sizes):
    cell_blocks, station_blocks, pairs, epochs, slots = sizes
    entries = station_blocks * pairs * slots // (2 * REACH + 1) * SBLOCK * CBLOCK
    return pl.CostEstimate(flops=2 * 1200 * entries, bytes_accessed=2**20, transcendentals=entries)


def adjoint_sums(sizes, first_ref, shift_ref, codes, messages, residuals, images, cells_ref, total_ref, scratch):
    cell_blocks, station_blocks, pairs, epochs, slots = sizes
    list_ref, stations_ref, terms_ref, depths_ref, gaps_ref, lines_ref = scratch
    dummy = slots * station_blocks
    terms_ref[dummy] = jnp.zeros(terms_ref.shape[1:], BF16)
    stations_ref[slots] = jnp.zeros(stations_ref.shape[1:], F32)
    total_ref[...] = jnp.zeros_like(total_ref)
    per_block = SBLOCK // LANES
    lane_rows = station_blocks * per_block
    for slot in range(slots):
        parts = [messages[slot][pl.ds(0, 1), pl.ds(i * LANES, LANES)] + shift_ref[slot] for i in range(lane_rows)]
        parts += [messages[slot][pl.ds(1, 1), pl.ds(i * LANES, LANES)] for i in range(lane_rows)]
        parts.append(jnp.zeros((LANES - 2 * lane_rows, LANES), F32))
        stations_ref[slot] = jnp.concatenate(parts, axis=0).T
        for q in range(station_blocks):
            stacked = jnp.concatenate([residuals[slot][:, pl.ds(q * SBLOCK, SBLOCK)], images[slot][q]], axis=0)
            high, low = split(stacked)
            terms_ref[slot * station_blocks + q, pl.ds(0, 2 * epochs), :] = high
            terms_ref[slot * station_blocks + q, pl.ds(2 * epochs, 2 * epochs), :] = low
    count = list_pairs(sizes, first_ref, codes, list_ref)
    lane = lax.broadcasted_iota(jnp.int32, (1, LANES), 1)
    column = ((lane % COL_SIDE).astype(F32) + 0.5) / COL_SIDE
    line = ((lane // COL_SIDE).astype(F32) + 0.5) / COL_SIDE
    rows = CBLOCK // COL_SIDE
    chunks = CBLOCK // LANES

    def stage(i, k):
        code = list_ref[i]
        q, w = code // cell_blocks, code % cell_blocks
        slot, within = q // station_blocks, q % station_blocks
        depths_ref[k] = cells_ref[pl.ds(0, 1), pl.ds(pl.multiple_of(w * CBLOCK, CBLOCK), CBLOCK)]
        lines = line + (w % 2).astype(F32) * (rows / COL_SIDE)
        places = pltpu.roll(stations_ref[slot], (LANES - within * per_block) % LANES, 1)
        for part in range(per_block):
            at = pl.ds(part * LANES, LANES)
            across = jnp.broadcast_to(places[:, part : part + 1], (LANES, LANES)) - column
            gaps_ref[k, at, :] = across * across
            along = jnp.broadcast_to(places[:, lane_rows + part : lane_rows + part + 1], (LANES, LANES))
            lines_ref[k, at, :] = along - lines

    def issue(sums, i, k):
        q = list_ref[i] // cell_blocks
        depth = depths_ref[k]
        for part in range(per_block):
            pieces = ([], [])
            for at in range(part * LANES, (part + 1) * LANES, 16):
                across = gaps_ref[k, pl.ds(at, 16), :]
                along = lines_ref[k, pl.ds(at, 16), :]
                for unit in range(2):
                    near = []
                    for chunk in range(unit * chunks // 2, (unit + 1) * chunks // 2):
                        gap = along - chunk * (LANES // COL_SIDE) / COL_SIDE
                        squared = (across + gap * gap) + depth[:, chunk * LANES : (chunk + 1) * LANES]
                        near.append(split(inverse_cube(squared)))
                    pieces[unit].append([jnp.concatenate(terms, axis=1) for terms in zip(*near)])
            left = terms_ref[q, :, pl.ds(part * HALF, HALF)]
            for unit in range(2):
                multiply_add(sums[2 * k + unit], left, pieces[unit], unit, part)

    def collect(sums, i, k):
        w = list_ref[i] % cell_blocks
        for unit in range(2):
            both = pltpu.matmul_pop(sums[2 * k + unit])
            total_ref[w, :, pl.ds(unit * TILE, TILE)] += both[: 2 * epochs] + both[2 * epochs :]

    def run(*sums):
        pipelined(count, stage, functools.partial(issue, sums), functools.partial(collect, sums))

    pl.run_scoped(run, *accumulators(4 * epochs))


def adjoint_refs(slots, refs):
    codes, messages, residuals, images = (refs[i * slots : (i + 1) * slots] for i in range(4))
    return codes, messages, residuals, images, refs[4 * slots :]


def near_kernel(sizes, first_ref, shift_ref, *refs):
    codes, messages, residuals, images, rest = adjoint_refs(sizes[-1], refs)
    cells_ref, total_ref, *scratch = rest
    adjoint_sums(sizes, first_ref, shift_ref, codes, messages, residuals, images, cells_ref, total_ref, scratch)


def far_kernel(sizes, first_ref, shift_ref, *refs):
    cell_blocks, station_blocks, pairs, epochs, slots = sizes
    codes, messages, residuals, images, rest = adjoint_refs(slots, refs)
    cells_ref, near_ref, model_ref, direction_ref, sums_ref, image_ref = rest[:6]
    constant_ref, slope_ref, stats_ref = rest[6:9]
    total_ref, *scratch = rest[9:]
    adjoint_sums(sizes, first_ref, shift_ref, codes, messages, residuals, images, cells_ref, total_ref, scratch)
    zero = jnp.zeros((epochs, CBLOCK), F32)

    def combine(w, sums):
        at = pl.ds(pl.multiple_of(w * CBLOCK, CBLOCK), CBLOCK)
        total = (near_ref[w] + total_ref[w]) * cells_ref[pl.ds(1, 1), at]
        constant = total[:epochs] - DAMPING * model_ref[:, at]
        slope = total[epochs:] + DAMPING * direction_ref[:, at]
        constant_ref[:, at] = constant
        slope_ref[:, at] = slope
        return sums[0] + constant * slope, sums[1] + slope * slope

    cross, square = lax.fori_loop(0, cell_blocks, combine, (zero, zero), unroll=2)
    square = jnp.sum(square).reshape(1, 1)
    cross = jnp.sum(cross).reshape(1, 1)
    local_step = jnp.where(square > 0, cross / jnp.where(square > 0, square, 1.0), 0.0)

    def remainder(w, sums):
        at = pl.ds(pl.multiple_of(w * CBLOCK, CBLOCK), CBLOCK)
        slope = slope_ref[:, at]
        left = constant_ref[:, at] - local_step * slope
        return sums[0] + left * left, sums[1] + left * slope

    left_square, left_cross = lax.fori_loop(0, cell_blocks, remainder, (zero, zero), unroll=2)
    image = image_ref[...]
    stats = [
        sums_ref[pl.ds(0, 1), pl.ds(0, 1)],
        sums_ref[pl.ds(1, 1), pl.ds(0, 1)],
        jnp.sum(image * image).reshape(1, 1),
        local_step,
        jnp.sum(left_square).reshape(1, 1),
        jnp.sum(left_cross).reshape(1, 1),
        jnp.sqrt(square),
    ]
    lane = lax.broadcasted_iota(jnp.int32, (1, LANES), 1)
    row = jnp.zeros((1, LANES), F32)
    for i, value in enumerate(stats):
        row = jnp.where(lane == i, value, row)
    for i in range(stats_ref.shape[0]):
        stats_ref[i] = row


def adjoint(sizes, first, shift, messages, residuals, images, cell_rows, last=()):
    cell_blocks, station_blocks, pairs, epochs, slots = sizes
    total = (cell_blocks, 2 * epochs, CBLOCK)
    scratch = [
        pair_list(sizes),
        pltpu.VMEM((slots + 1, LANES, LANES), F32),
        pltpu.VMEM((slots * station_blocks + 1, 4 * epochs, SBLOCK), BF16),
        pltpu.VMEM((2, 1, CBLOCK), F32),
        pltpu.VMEM((2, SBLOCK, LANES), F32),
        pltpu.VMEM((2, SBLOCK, LANES), F32),
    ]
    if last:
        ranks, *last = last
        kernel, cells = far_kernel, (epochs, cell_blocks * CBLOCK)
        shapes = [cells, cells, (ranks, 1, LANES)]
        scratch = [pltpu.VMEM(total, F32)] + scratch
    else:
        kernel, shapes = near_kernel, [total]
    return pl.pallas_call(
        functools.partial(kernel, sizes),
        grid=(1,),
        out_shape=tuple(jax.ShapeDtypeStruct(shape, F32) for shape in shapes),
        in_specs=[SMEM, SMEM]
        + [codes_spec(station_blocks * SBLOCK)] * slots
        + [VMEM] * (3 * slots + 1 + len(last)),
        out_specs=(VMEM,) * len(shapes),
        scratch_shapes=scratch,
        compiler_params=params(),
        cost_estimate=estimate(sizes),
        name="far" if last else "near",
    )(first, shift, *messages, *messages, *residuals, *images, cell_rows, *last)


def finish_kernel(
    stats_ref, constant_ref, slope_ref, model_ref, direction_ref, residual_ref, image_ref, model_out, residual_out, direction_out
):
    stats = stats_ref[...][:, 0, :]
    gamma_old, direction_square, image_square = (
        jnp.sum(stats[:, i : i + 1], axis=0, keepdims=True) for i in range(3)
    )
    step = gamma_old / (image_square + DAMPING * direction_square + GUARD)
    ahead = step - stats[:, 3:4]
    reach = ahead * stats[:, 6:7]
    gamma_new = jnp.sum(stats[:, 4:5] - 2.0 * ahead * stats[:, 5:6] + reach * reach, axis=0, keepdims=True)
    ratio = gamma_new / (gamma_old + GUARD)
    blocks = model_ref.shape[1] // CBLOCK

    def block(w, unused):
        at = pl.ds(pl.multiple_of(w * CBLOCK, CBLOCK), CBLOCK)
        direction = direction_ref[:, at]
        model_out[:, at] = model_ref[:, at] + step * direction
        direction_out[:, at] = (constant_ref[:, at] - step * slope_ref[:, at]) + ratio * direction
        return 0

    lax.fori_loop(0, blocks, block, 0, unroll=2)
    for q in range(image_ref.shape[0]):
        at = pl.ds(q * SBLOCK, SBLOCK)
        residual_out[:, at] = residual_ref[:, at] - step * image_ref[q]


def finish(stats, constant, slope, model_field, direction, residual, image):
    return pl.pallas_call(
        finish_kernel,
        out_shape=(
            jax.ShapeDtypeStruct(model_field.shape, F32),
            jax.ShapeDtypeStruct(residual.shape, F32),
            jax.ShapeDtypeStruct(direction.shape, F32),
        ),
        in_specs=[VMEM] * 7,
        out_specs=(VMEM,) * 3,
        compiler_params=params(),
        name="finish",
    )(stats, constant, slope, model_field, direction, residual, image)


def after(arrays, others):
    return lax.optimization_barrier((arrays, others))[0]


def shards(model_field, direction, old_grad, residual, block_pairs, depth_band, station_offsets):
    ranks = lax.axis_size("tile")
    tile_id = lax.axis_index("tile")
    epochs, cells = model_field.shape
    station_blocks, pairs = block_pairs.shape
    cell_blocks = cells // CBLOCK
    side = 2 * (tile_id % 2) - 1

    def to_partner(array):
        return lax.ppermute(array, "tile", [(i, i ^ 1) for i in range(ranks)])

    def across(first, second):
        ends = [(i, i + 1) for i in range(1, ranks - 1, 2)]
        both = lax.ppermute(jnp.stack([first, second]), "tile", ends + [(j, i) for i, j in ends])
        return both[0], both[1]

    def slots(*places):
        offsets = jnp.stack([multiple * side for multiple in places]).astype(jnp.int32)
        sizes = (cell_blocks, station_blocks, pairs, epochs, len(places))
        return sizes, cell_blocks * (REACH - offsets) + 1, offsets.astype(F32)

    own_slot, partner_slot, near_slots, far_slots = slots(0), slots(-1), slots(0, -1), slots(1, 2, -2)

    own = pack(station_offsets, block_pairs)
    values, cell_rows, turned, sums = prepare(2.0 / math.sqrt(cells), depth_band, direction, old_grad)
    partner = to_partner(own)
    first_far, second_far = across(own, partner)
    (to_return,) = forward(*partner_slot, [partner], values, turned)
    third_far = to_partner(first_far)

    own_residual = after(residual, third_far)
    partner_residual = to_partner(own_residual)
    far_residuals = across(own_residual, partner_residual)
    far_residuals = [*far_residuals, to_partner(far_residuals[0])]

    far = [first_far, second_far, third_far]
    to_first, to_second, to_third = forward(*far_slots, far, values, turned)
    to_first = to_first + to_partner(to_third)
    (image,) = forward(*own_slot, [after(own, to_first)], values, turned)
    given, to_pass = across(to_first, to_second)
    image = image + given + to_partner(to_return + to_pass)

    partner_image = to_partner(image)
    first_image, second_image = across(image, partner_image)
    (near_total,) = adjoint(
        *near_slots, [own, partner], [residual, partner_residual], [image, partner_image], cell_rows
    )
    far_images = [first_image, second_image, to_partner(first_image)]
    constant, slope, stats = adjoint(
        *far_slots, far, far_residuals, far_images, cell_rows,
        (ranks, near_total, model_field, direction, sums, image),
    )
    stats = lax.all_to_all(stats, "tile", 0, 0)
    return finish(stats, constant, slope, model_field, direction, residual, image)


def solution(mesh):
    wide = P(None, ("groups", "tile"))
    mapped = jax.shard_map(
        shards,
        mesh=mesh,
        in_specs=(wide, wide, wide, wide, P(("groups", "tile"), None), P(("groups", "tile")), wide),
        out_specs=(wide, wide, wide),
        check_vma=False,
    )

    def step(*arrays):
        with jax.sharding.use_abstract_mesh(mesh.abstract_mesh):
            return mapped(*arrays)

    return step
```

profile of v0, /device:TPU:0, one launch (start us, length us, event | category | flops | bytes accessed | tf_op | source)
XLA Modules:
  0.0 97.1 jit_solution(8449355435241864385)
XLA Ops:
  0.6 1.4 %pack.1.refs_0_.refs_1_.refs_2_ = f32[8,2176]{1,0:T(8,128)} custom-call(f32[2,2048]{1,0:T(2,128)} %offsets_ref.1, s32[8,8]{1,0:T(8,128)} %pairs_ref.1), custom_call_target="tpu_custom_call" | custom-call | tf_op jit(solution)/shard_map/pack/pallas_call | solution.py:53
  2.0 0.5 collective-permute-start
  2.4 1.1 %collective-permute-done.refs_0_.refs_1_.refs_3_ = f32[8,2176]{1,0:T(8,128)S(1)} collective-permute-done((f32[8,2176]{1,0:T(8,128)}, f32[8,2176]{1,0:T(8,128)S(1)}, u32[]{:S(2)}, u32[]{:S(2)}) %collective-permute-start) | collective-permute-done | bytes 69664 | tf_op jit(solution)/shard_map/ppermute | solution.py:476
  3.6 0.9 pad_maximum_fusion.3
  4.5 0.7 collective-permute-start.1
  5.2 0.1 fusion.4
  5.2 6.9 %collective-permute-start.2 = (f32[8,2176]{1,0:T(8,128)S(1)}, f32[8,2176]{1,0:T(8,128)S(1)}, u32[]{:S(2)}, u32[]{:S(2)}) collective-permute-start(f32[8,2176]{1,0:T(8,128)S(1)} %get-tuple-element.34.refs_0_.refs_3_), channel_id=1, source_target_pairs={{0,1},{1,0},{2,3},{3,2},{4,5},{5,4},{6,7},{7,6},{8,9},{9,8},{10,11... | collective-permute-start | bytes 208904 | tf_op jit(solution)/shard_map/ppermute | solution.py:476
  12.2 1.2 %copy-done = f32[16,16384]{1,0:T(8,128)S(1)} copy-done((f32[16,16384]{1,0:T(8,128)S(1)}, f32[16,16384]{1,0:T(8,128)}, u32[]{:S(2)}) %copy-start) | copy-done | bytes 1048600
  13.4 1.2 %copy-done.3 = f32[16,16384]{1,0:T(8,128)S(1)} copy-done((f32[16,16384]{1,0:T(8,128)S(1)}, f32[16,16384]{1,0:T(8,128)}, u32[]{:S(2)}) %copy-start.3) | copy-done | bytes 1048600
  14.6 0.8 copy-done.6
  15.5 0.7 prepare.1
  16.2 5.5 %forward.3 = (f32[8,16,256]{2,1,0:T(8,128)S(1)}, f32[8,16,256]{2,1,0:T(8,128)S(1)}, f32[8,16,256]{2,1,0:T(8,128)S(1)}) custom-call(s32[3]{0:T(128)S(1)} %multiply_add_fusion.1.first_ref, f32[3]{0:T(128)S(1)} %get-tuple-element.27.shift_ref, f32[8,2176]{1,0:T(8,128)S(1)} %get-tuple-element.34.refs_0_.refs_3_, ...), custom_call_target="tpu_custom_call" | custom-call | flops 11953766400 | bytes 1048576 | tf_op jit(solution)/shard_map/forward/pallas_call | solution.py:231
  21.8 0.1 collective-permute-start.6
  21.9 0.5 collective-permute-start.3
  22.4 0.8 collective-permute-done.6
  23.3 0.0 copy-start.5
  23.3 0.8 collective-permute-start.7
  24.1 4.1 %forward.5 = f32[8,16,256]{2,1,0:T(8,128)S(1)} custom-call(s32[1]{0:T(128)S(6)} %add.30.first_ref, f32[1]{0:T(128)S(6)} %convert_element_type.10.shift_ref, f32[8,2176]{1,0:T(8,128)S(1)} %collective-permute-done.refs_0_.refs_1_.refs_3_, f32[8,2176]{1,0:T(8,128)S(1)} %collective-permute-done.refs_0_.refs_1_.refs_3_, ...), custom_call_target="tpu_custom_call" | custom-call | flops 3774873600 | bytes 1048576 | tf_op jit(solution)/shard_map/forward/pallas_call | solution.py:231
  28.3 0.7 collective-permute-start.4
  29.0 10.1 %collective-permute-start.8 = (f32[8,16,256]{2,1,0:T(8,128)S(1)}, f32[8,16,256]{2,1,0:T(8,128)S(1)}, u32[]{:S(2)}, u32[]{:S(2)}) collective-permute-start(f32[8,16,256]{2,1,0:T(8,128)S(1)} %fusion), channel_id=1, source_target_pairs={{0,1},{1,0},{2,3},{3,2},{4,5},{5,4},{6,7},{7,6},{8,9},{9,8},{10,11... | collective-permute-start | bytes 393224 | tf_op jit(solution)/shard_map/ppermute | solution.py:476
  39.1 2.7 %forward.4 = f32[8,16,256]{2,1,0:T(8,128)S(1)} custom-call(s32[1]{0:T(128)} %constant.9.clone.1.first_ref, f32[1]{0:T(128)} %constant.10.clone.1.shift_ref, f32[8,2176]{1,0:T(8,128)S(1)} %copy-done.5, f32[8,2176]{1,0:T(8,128)S(1)} %copy-done.5, bf16[32,32,512]{2,1,0:T(8,128)(2,1)S(1)} %get-tuple-element.16.refs_6_.refs_2_, ...), custom_call_target="tpu_custom_call" | custom-call | flops 3774873600 | bytes 1048576 | tf_op jit(solution)/shard_map/forward/pallas_call | solution.py:231
  41.8 0.8 collective-permute-start.9
  42.6 0.1 multiply_add_fusion
  42.7 0.9 collective-permute-done.9.refs_7_
  43.6 0.7 collective-permute-start.10
  44.4 4.2 %collective-permute-start.5 = (f32[16,2048]{1,0:T(8,128)S(1)}, f32[16,2048]{1,0:T(8,128)S(1)}, u32[]{:S(2)}, u32[]{:S(2)}) collective-permute-start(f32[16,2048]{1,0:T(8,128)S(1)} %get-tuple-element.32.refs_6_), channel_id=1, source_target_pairs={{0,1},{1,0},{2,3},{3,2},{4,5},{5,4},{6,7},{7,6},{8,9},{9,8},{10,11... | collective-permute-start | bytes 393224 | tf_op jit(solution)/shard_map/ppermute | solution.py:476
  48.6 6.1 %collective-permute-start.11 = (f32[8,16,256]{2,1,0:T(8,128)S(1)}, f32[8,16,256]{2,1,0:T(8,128)S(1)}, u32[]{:S(2)}, u32[]{:S(2)}) collective-permute-start(f32[8,16,256]{2,1,0:T(8,128)S(1)} %get-tuple-element.30.refs_9_), channel_id=1, source_target_pairs={{0,1},{1,0},{2,3},{3,2},{4,5},{5,4},{6,7},{7,6},{8,9},{9,8},{10,11... | collective-permute-start | bytes 393224 | tf_op jit(solution)/shard_map/ppermute | solution.py:476
  54.7 7.3 %near.1.refs_13_ = f32[32,32,512]{2,1,0:T(8,128)S(1)} custom-call(s32[2]{0:T(128)S(1)} %get-tuple-element.35.first_ref, f32[2]{0:T(128)S(1)} %get-tuple-element.36.shift_ref, f32[8,2176]{1,0:T(8,128)S(1)} %copy-done.5, f32[8,2176]{1,0:T(8,128)S(1)} %collective-permute-done.refs_0_.refs_1_.refs_3_, f32[8,2176]{1,0:T(8,128)S(1)} %copy-done.5, ...), custom_call_target="tpu_custom_call" | custom-call | flops 7864320000 | bytes 1048576 | tf_op jit(solution)/shard_map/near/pallas_call | solution.py:406
  62.0 1.3 %copy-done.7 = f32[32,32,512]{2,1,0:T(8,128)} copy-done((f32[32,32,512]{2,1,0:T(8,128)}, f32[32,32,512]{2,1,0:T(8,128)S(1)}, u32[]{:S(2)}) %copy-start.7) | copy-done | bytes 2097176
  63.4 8.8 %far.1 = (f32[16,16384]{1,0:T(8,128)S(1)}, f32[16,16384]{1,0:T(8,128)S(1)}, f32[16,1,128]{2,1,0:T(1,128)S(1)}) custom-call(s32[3]{0:T(128)S(1)} %multiply_add_fusion.1.first_ref, f32[3]{0:T(128)S(1)} %get-tuple-element.27.shift_ref, f32[8,2176]{1,0:T(8,128)S(1)} %get-tuple-element.34.refs_0_.refs_3_, f32[8,2176]{1,0:T(8,128)S(1)} %get-tuple-element.33.refs_1_.refs_4_, ...), custom_call_target="tpu_custom_call" | custom-call | flops 11953766400 | bytes 1048576 | tf_op jit(solution)/shard_map/far/pallas_call | solution.py:406
  72.2 22.1 %all_to_all.5.stats_ref = f32[16,1,128]{2,1,0:T(1,128)S(1)} all-to-all(f32[16,1,128]{2,1,0:T(1,128)S(1)} %get-tuple-element.24), channel_id=1, replica_groups=mesh['groups'=2,'tile'=16] {'tile'}, dimensions={0} | all-to-all | bytes 16384 | tf_op jit(solution)/shard_map/all_to_all | solution.py:519
  94.3 2.8 %finish.1 = (f32[16,16384]{1,0:T(8,128)}, f32[16,2048]{1,0:T(8,128)}, f32[16,16384]{1,0:T(8,128)}) custom-call(f32[16,1,128]{2,1,0:T(1,128)S(1)} %all_to_all.5.stats_ref, f32[16,16384]{1,0:T(8,128)S(1)} %get-tuple-element.25.constant_ref, f32[16,16384]{1,0:T(8,128)S(1)} %get-tuple-element.26.slope_ref, f32[16,16384]{1,0:T(8,128)S(1)} %copy-done.2, ...), custom_call_target="tpu_custom_call" | custom-call | tf_op jit(solution)/shard_map/finish/pallas_call | solution.py:449
  (30 shorter events, 0.2 us)
Async XLA Ops:
  2.0 1.6 %collective-permute-start = (f32[8,2176]{1,0:T(8,128)}, f32[8,2176]{1,0:T(8,128)S(1)}, u32[]{:S(2)}, u32[]{:S(2)}) collective-permute-start(f32[8,2176]{1,0:T(8,128)} %pack.1.refs_0_.refs_1_.refs_2_), channel_id=1, source_target_pairs={{0,1},{1,0},{2,3},{3,2},{4,5},{5,4},{6,7},{7,6},{8,9},{9,8},{10,11... | collective-permute-start | bytes 208904 | tf_op jit(solution)/shard_map/ppermute | solution.py:476
  4.5 0.8 collective-permute-start.1
  5.2 11.0 %collective-permute-start.2 = (f32[8,2176]{1,0:T(8,128)S(1)}, f32[8,2176]{1,0:T(8,128)S(1)}, u32[]{:S(2)}, u32[]{:S(2)}) collective-permute-start(f32[8,2176]{1,0:T(8,128)S(1)} %get-tuple-element.34.refs_0_.refs_3_), channel_id=1, source_target_pairs={{0,1},{1,0},{2,3},{3,2},{4,5},{5,4},{6,7},{7,6},{8,9},{9,8},{10,11... | collective-permute-start | bytes 208904 | tf_op jit(solution)/shard_map/ppermute | solution.py:476
  12.2 1.2 %copy-start = (f32[16,16384]{1,0:T(8,128)S(1)}, f32[16,16384]{1,0:T(8,128)}, u32[]{:S(2)}) copy-start(f32[16,16384]{1,0:T(8,128)} %direction_ref.3) | copy-start | bytes 3145732
  13.4 1.2 %copy-start.3 = (f32[16,16384]{1,0:T(8,128)S(1)}, f32[16,16384]{1,0:T(8,128)}, u32[]{:S(2)}) copy-start(f32[16,16384]{1,0:T(8,128)} %old_ref.1) | copy-start | bytes 3145732
  14.6 0.8 copy-start.6
  16.2 5.7 %copy-start.4 = (f32[16,2048]{1,0:T(8,128)S(1)}, f32[16,2048]{1,0:T(8,128)}, u32[]{:S(2)}) copy-start(f32[16,2048]{1,0:T(8,128)} %residual_ref.1) | copy-start | bytes 393220
  21.8 1.4 %collective-permute-start.6 = (f32[8,16,256]{2,1,0:T(8,128)S(1)}, f32[8,16,256]{2,1,0:T(8,128)S(1)}, u32[]{:S(2)}, u32[]{:S(2)}) collective-permute-start(f32[8,16,256]{2,1,0:T(8,128)S(1)} %get-tuple-element.19), channel_id=1, source_target_pairs={{0,1},{1,0},{2,3},{3,2},{4,5},{5,4},{6,7},{7,6},{8,9},{9,8},{10,11... | collective-permute-start | bytes 393224 | tf_op jit(solution)/shard_map/ppermute | solution.py:476
  21.9 6.3 %collective-permute-start.3 = (f32[16,2048]{1,0:T(8,128)S(1)}, f32[16,2048]{1,0:T(8,128)S(1)}, u32[]{:S(2)}, u32[]{:S(2)}) collective-permute-start(f32[16,2048]{1,0:T(8,128)S(1)} %copy-done.4), channel_id=1, source_target_pairs={{0,1},{1,0},{2,3},{3,2},{4,5},{5,4},{6,7},{7,6},{8,9},{9,8},{10,11... | collective-permute-start | bytes 393224 | tf_op jit(solution)/shard_map/ppermute | solution.py:476
  23.3 15.8 %copy-start.5 = (f32[8,2176]{1,0:T(8,128)S(1)}, f32[8,2176]{1,0:T(8,128)}, u32[]{:S(2)}) copy-start(f32[8,2176]{1,0:T(8,128)} %pack.1.refs_0_.refs_1_.refs_2_) | copy-start | bytes 208900
  23.3 5.7 %collective-permute-start.7 = (f32[2,8,16,256]{3,2,1,0:T(8,128)S(1)}, f32[2,8,16,256]{3,2,1,0:T(8,128)S(1)}, u32[]{:S(2)}, u32[]{:S(2)}) collective-permute-start(f32[2,8,16,256]{3,2,1,0:T(8,128)S(1)} %pad_maximum_fusion.1), channel_id=1, source_target_pairs={{1,2},{3,4},{5,6},{7,8},{9,10},{11,12},{13,14},{2,1},{4,3},{6,5},{... | collective-permute-start | bytes 786440 | tf_op jit(solution)/shard_map/ppermute | solution.py:480
  28.3 16.0 %collective-permute-start.4 = (f32[2,16,2048]{2,1,0:T(8,128)S(1)}, f32[2,16,2048]{2,1,0:T(8,128)S(1)}, u32[]{:S(2)}, u32[]{:S(2)}) collective-permute-start(f32[2,16,2048]{2,1,0:T(8,128)S(1)} %pad_maximum_fusion), channel_id=1, source_target_pairs={{1,2},{3,4},{5,6},{7,8},{9,10},{11,12},{13,14},{2,1},{4,3},{6,5},{... | collective-permute-start | bytes 786440 | tf_op jit(solution)/shard_map/ppermute | solution.py:480
  29.0 12.8 %collective-permute-start.8 = (f32[8,16,256]{2,1,0:T(8,128)S(1)}, f32[8,16,256]{2,1,0:T(8,128)S(1)}, u32[]{:S(2)}, u32[]{:S(2)}) collective-permute-start(f32[8,16,256]{2,1,0:T(8,128)S(1)} %fusion), channel_id=1, source_target_pairs={{0,1},{1,0},{2,3},{3,2},{4,5},{5,4},{6,7},{7,6},{8,9},{9,8},{10,11... | collective-permute-start | bytes 393224 | tf_op jit(solution)/shard_map/ppermute | solution.py:476
  41.8 1.8 %collective-permute-start.9 = (f32[8,16,256]{2,1,0:T(8,128)S(1)}, f32[8,16,256]{2,1,0:T(8,128)S(1)}, u32[]{:S(2)}, u32[]{:S(2)}) collective-permute-start(f32[8,16,256]{2,1,0:T(8,128)S(1)} %fusion.2.refs_6_.refs_17_.image_ref), channel_id=1, source_target_pairs={{0,1},{1,0},{2,3},{3,2},{4,5},{5,4},{6,7},{7,6},{8,9},{9,8},{10,11... | collective-permute-start | bytes 393224 | tf_op jit(solution)/shard_map/ppermute | solution.py:476
  43.6 5.0 %collective-permute-start.10 = (f32[2,8,16,256]{3,2,1,0:T(8,128)S(1)}, f32[2,8,16,256]{3,2,1,0:T(8,128)S(1)}, u32[]{:S(2)}, u32[]{:S(2)}) collective-permute-start(f32[2,8,16,256]{3,2,1,0:T(8,128)S(1)} %pad_maximum_fusion.2), channel_id=1, source_target_pairs={{1,2},{3,4},{5,6},{7,8},{9,10},{11,12},{13,14},{2,1},{4,3},{6,5},{... | collective-permute-start | bytes 786440 | tf_op jit(solution)/shard_map/ppermute | solution.py:480
  44.4 19.0 %collective-permute-start.5 = (f32[16,2048]{1,0:T(8,128)S(1)}, f32[16,2048]{1,0:T(8,128)S(1)}, u32[]{:S(2)}, u32[]{:S(2)}) collective-permute-start(f32[16,2048]{1,0:T(8,128)S(1)} %get-tuple-element.32.refs_6_), channel_id=1, source_target_pairs={{0,1},{1,0},{2,3},{3,2},{4,5},{5,4},{6,7},{7,6},{8,9},{9,8},{10,11... | collective-permute-start | bytes 393224 | tf_op jit(solution)/shard_map/ppermute | solution.py:476
  48.6 14.7 %collective-permute-start.11 = (f32[8,16,256]{2,1,0:T(8,128)S(1)}, f32[8,16,256]{2,1,0:T(8,128)S(1)}, u32[]{:S(2)}, u32[]{:S(2)}) collective-permute-start(f32[8,16,256]{2,1,0:T(8,128)S(1)} %get-tuple-element.30.refs_9_), channel_id=1, source_target_pairs={{0,1},{1,0},{2,3},{3,2},{4,5},{5,4},{6,7},{7,6},{8,9},{9,8},{10,11... | collective-permute-start | bytes 393224 | tf_op jit(solution)/shard_map/ppermute | solution.py:476
  54.7 8.7 %copy-start.1 = (f32[16,16384]{1,0:T(8,128)S(1)}, f32[16,16384]{1,0:T(8,128)}, u32[]{:S(2)}) copy-start(f32[16,16384]{1,0:T(8,128)} %direction_ref.3) | copy-start | bytes 3145732
  54.7 8.7 %copy-start.2 = (f32[16,16384]{1,0:T(8,128)S(1)}, f32[16,16384]{1,0:T(8,128)}, u32[]{:S(2)}) copy-start(f32[16,16384]{1,0:T(8,128)} %model_ref.1) | copy-start | bytes 3145732
  62.0 1.3 %copy-start.7 = (f32[32,32,512]{2,1,0:T(8,128)}, f32[32,32,512]{2,1,0:T(8,128)S(1)}, u32[]{:S(2)}) copy-start(f32[32,32,512]{2,1,0:T(8,128)S(1)} %near.1.refs_13_) | copy-start | bytes 6291460
where the time goes:
time: 96.4 us; the launch traced here: 97.1 us
  Pallas kernels  33.4 us (35%)
  starting transfers between devices  31.9 us (33%)
  blocking collectives  22.1 us (23%)
  local copies, waits for them, and re-layouts  4.69 us (5%)
  waiting for transfers between devices  2.88 us (3%)
  other arithmetic  1.19 us (1%)
    ppermute x8, starting transfers between devices, to_partner(): return lax.ppermute(array, 'tile', [(i, i ^ 1) for i in range(ranks)])  29.1 us
    all_to_all x1, blocking collectives, shards(): stats = lax.all_to_all(stats, 'tile', 0, 0)  22.1 us
    pallas_call x2, Pallas kernels, adjoint(): pl.pallas_call(functools.partial(kernel, sizes), grid=(1,), out_shape=tup...  16.1 us
    pallas_call x3, Pallas kernels, forward(): pl.pallas_call(functools.partial(forward_kernel, sizes), grid=(1,), out_s...  12.4 us
    unnamed x16, local copies, waits for them, and re-layouts  4.64 us
    ppermute x8, waiting for transfers between devices, to_partner(): return lax.ppermute(array, 'tile', [(i, i ^ 1) for i in range(ranks)])  2.87 us
    ppermute x4, starting transfers between devices, across(): lax.ppermute(jnp.stack([first, second]), 'tile', ends + [(j, i) for i, j...  2.83 us
    pallas_call x1, Pallas kernels, finish(): pl.pallas_call(finish_kernel, out_shape=(jax.ShapeDtypeStruct(model_field...  2.78 us
  transfers between devices with their start and end apart: 12, of which 3 were waited for; matrix products, arithmetic and copies ran while one was open for 0% of the time, Pallas kernels for 15%

commit v1 on v0

--- a/solution.py
+++ b/solution.py
@@ -29,7 +29,7 @@
 
 
 def params():
-    return pltpu.CompilerParams(vmem_limit_bytes=48 * 2**20)
+    return pltpu.CompilerParams(vmem_limit_bytes=24 * 2**20)
 
 
 def split(values):
@@ -59,11 +59,34 @@
     )(station_offsets, block_pairs)
 
 
+def pair_kernel(*refs):
+    first_ref, second_ref, *added_refs, message_ref = refs
+    first = first_ref[...]
+    for added_ref in added_refs:
+        first = first + added_ref[...]
+    message_ref[0] = first
+    message_ref[1] = second_ref[...]
+
+
+def pair_up(first, second, *added):
+    return pl.pallas_call(
+        pair_kernel,
+        out_shape=jax.ShapeDtypeStruct((2, *first.shape), F32),
+        in_specs=[VMEM] * (2 + len(added)),
+        out_specs=VMEM,
+        name="pair",
+    )(first, second, *added)
+
+
 def prepare_kernel(scale, band_ref, band_row_ref, direction_ref, old_ref, values_ref, cells_ref, turned_ref, sums_ref):
     blocks = values_ref.shape[0]
     epochs = direction_ref.shape[0]
-    depth = (band_ref[...].astype(F32) + 0.5) * (DEPTH_RANGE / BANDS)
-    turned_ref[...] = (depth * depth).T
+
+    @pl.when(pl.program_id(0) == 0)
+    def first():
+        depth = (band_ref[...].astype(F32) + 0.5) * (DEPTH_RANGE / BANDS)
+        turned_ref[...] = (depth * depth).T
+        sums_ref[...] = jnp.zeros_like(sums_ref)
 
     def block(w, sums):
         at = pl.ds(pl.multiple_of(w * CBLOCK, CBLOCK), CBLOCK)
@@ -81,23 +104,34 @@
 
     zero = jnp.zeros((epochs, CBLOCK), F32)
     old_sum, direction_sum = lax.fori_loop(0, blocks, block, (zero, zero), unroll=2)
-    sums_ref[pl.ds(0, 1), :] = jnp.broadcast_to(jnp.sum(old_sum).reshape(1, 1), (1, LANES))
-    sums_ref[pl.ds(1, 1), :] = jnp.broadcast_to(jnp.sum(direction_sum).reshape(1, 1), (1, LANES))
+    sums_ref[pl.ds(0, 1), :] += jnp.broadcast_to(jnp.sum(old_sum).reshape(1, 1), (1, LANES))
+    sums_ref[pl.ds(1, 1), :] += jnp.broadcast_to(jnp.sum(direction_sum).reshape(1, 1), (1, LANES))
+
+
+PARTS = 4
 
 
 def prepare(scale, depth_band, direction, old_grad):
     epochs, cells = direction.shape
     blocks = cells // CBLOCK
+    direction, old_grad = (pltpu.with_memory_space_constraint(array, pltpu.HBM) for array in (direction, old_grad))
+    wide = pl.BlockSpec((epochs, cells // PARTS), lambda i: (0, i))
     return pl.pallas_call(
         functools.partial(prepare_kernel, scale),
+        grid=(PARTS,),
         out_shape=(
             jax.ShapeDtypeStruct((blocks, 2 * epochs, CBLOCK), BF16),
             jax.ShapeDtypeStruct((2, cells), F32),
             jax.ShapeDtypeStruct((cells // LANES, LANES), F32),
             jax.ShapeDtypeStruct((2, LANES), F32),
         ),
-        in_specs=[VMEM] * 4,
-        out_specs=(VMEM,) * 4,
+        in_specs=[VMEM, pl.BlockSpec((1, cells // PARTS), lambda i: (0, i)), wide, wide],
+        out_specs=(
+            pl.BlockSpec((blocks // PARTS, 2 * epochs, CBLOCK), lambda i: (i, 0, 0)),
+            pl.BlockSpec((2, cells // PARTS), lambda i: (0, i)),
+            VMEM,
+            VMEM,
+        ),
         compiler_params=params(),
         cost_estimate=pl.CostEstimate(flops=8 * epochs * cells, bytes_accessed=12 * epochs * cells, transcendentals=0),
         name="prepare",
@@ -475,10 +509,9 @@
     def to_partner(array):
         return lax.ppermute(array, "tile", [(i, i ^ 1) for i in range(ranks)])
 
-    def across(first, second):
+    def across(message):
         ends = [(i, i + 1) for i in range(1, ranks - 1, 2)]
-        both = lax.ppermute(jnp.stack([first, second]), "tile", ends + [(j, i) for i, j in ends])
-        return both[0], both[1]
+        return lax.ppermute(message, "tile", ends + [(j, i) for i, j in ends])
 
     def slots(*places):
         offsets = jnp.stack([multiple * side for multiple in places]).astype(jnp.int32)
@@ -488,30 +521,35 @@
     own_slot, partner_slot, near_slots, far_slots = slots(0), slots(-1), slots(0, -1), slots(1, 2, -2)
 
     own = pack(station_offsets, block_pairs)
-    values, cell_rows, turned, sums = prepare(2.0 / math.sqrt(cells), depth_band, direction, old_grad)
     partner = to_partner(own)
-    first_far, second_far = across(own, partner)
+    arrived = across(pair_up(own, partner))
+    partner_residual = to_partner(after(residual, partner))
+    values, cell_rows, turned, sums = prepare(
+        2.0 / math.sqrt(cells), after(depth_band, partner), direction, old_grad
+    )
     (to_return,) = forward(*partner_slot, [partner], values, turned)
+    arrived = after(arrived, (to_return, partner_residual))
+    first_far, second_far = arrived[0], arrived[1]
     third_far = to_partner(first_far)
-
-    own_residual = after(residual, third_far)
-    partner_residual = to_partner(own_residual)
-    far_residuals = across(own_residual, partner_residual)
-    far_residuals = [*far_residuals, to_partner(far_residuals[0])]
-
     far = [first_far, second_far, third_far]
+
+    arrived = across(pair_up(after(residual, first_far), partner_residual))
     to_first, to_second, to_third = forward(*far_slots, far, values, turned)
-    to_first = to_first + to_partner(to_third)
-    (image,) = forward(*own_slot, [after(own, to_first)], values, turned)
-    given, to_pass = across(to_first, to_second)
-    image = image + given + to_partner(to_return + to_pass)
+    to_third, arrived = after((to_third, arrived), (arrived, to_third))
+    far_residuals = [arrived[0], arrived[1], to_partner(arrived[0])]
+    returned = to_partner(to_third)
+    given = across(pair_up(to_first, to_second, returned))
+    (image,) = forward(*own_slot, [after(own, (far_residuals[2], returned))], values, turned)
+    given = after(given, image)
+    image = image + given[0] + to_partner(to_return + given[1])
 
     partner_image = to_partner(image)
-    first_image, second_image = across(image, partner_image)
+    arrived = across(pair_up(image, partner_image))
     (near_total,) = adjoint(
         *near_slots, [own, partner], [residual, partner_residual], [image, partner_image], cell_rows
     )
-    far_images = [first_image, second_image, to_partner(first_image)]
+    arrived = after(arrived, near_total)
+    far_images = [arrived[0], arrived[1], to_partner(arrived[0])]
     constant, slope, stats = adjoint(
         *far_slots, far, far_residuals, far_images, cell_rows,
         (ranks, near_total, model_field, direction, sums, image),

time: 96.4 us -> 98.5 us (1.022); the launches traced: 97.1 us -> 97 us
  Pallas kernels: 33.4 us -> 40 us
  blocking collectives: 22.1 us -> 17.3 us
  starting transfers between devices: 31.9 us -> 27.9 us
  waiting for transfers between devices: 2.88 us -> 5.21 us
    pallas_call x1 -> x5, Pallas kernels: 0.75 us -> 9.78 us  [the longest x4 6.71 us: pair_up(): pl.pallas_call(pair_kernel, out_shape=jax.ShapeDtypeStruct((2, *first.sha...]
    all_to_all x1, blocking collectives: 22.1 us -> 17.3 us  [shards(): stats = lax.all_to_all(stats, 'tile', 0, 0)]
    ppermute x8, starting transfers between devices: 29.1 us -> 25.2 us  [to_partner(): return lax.ppermute(array, 'tile', [(i, i ^ 1) for i in range(ranks)])]
    ppermute x8, waiting for transfers between devices: 2.87 us -> 5.2 us  [to_partner(): return lax.ppermute(array, 'tile', [(i, i ^ 1) for i in range(ranks)])]
    pallas_call x2, Pallas kernels: 16.1 us -> 14.3 us  [adjoint(): pl.pallas_call(functools.partial(kernel, sizes), grid=(1,), out_shape=tup...]
    unnamed x16 -> x32, local copies, waits for them, and re-layouts: 4.64 us -> 5.52 us
  transfers between devices with their start and end apart: 12 -> 12, of which waited for: 3 -> 6; matrix products, arithmetic and copies ran while one was open for 0% -> 0% of each run, Pallas kernels for 15% -> 27%
where the time goes in v1:
time: 98.5 us; the launch traced here: 97 us
  Pallas kernels  40 us (41%)
  starting transfers between devices  27.9 us (28%)
  blocking collectives  17.3 us (18%)
  local copies, waits for them, and re-layouts  5.57 us (6%)
  waiting for transfers between devices  5.21 us (5%)
    ppermute x8, starting transfers between devices, to_partner(): return lax.ppermute(array, 'tile', [(i, i ^ 1) for i in range(ranks)])  25.2 us
    all_to_all x1, blocking collectives, shards(): stats = lax.all_to_all(stats, 'tile', 0, 0)  17.3 us
    pallas_call x2, Pallas kernels, adjoint(): pl.pallas_call(functools.partial(kernel, sizes), grid=(1,), out_shape=tup...  14.3 us
    pallas_call x3, Pallas kernels, forward(): pl.pallas_call(functools.partial(forward_kernel, sizes), grid=(1,), out_s...  11.7 us
    pallas_call x4, Pallas kernels, pair_up(): pl.pallas_call(pair_kernel, out_shape=jax.ShapeDtypeStruct((2, *first.sha...  6.71 us
    unnamed x32, local copies, waits for them, and re-layouts  5.52 us
    ppermute x8, waiting for transfers between devices, to_partner(): return lax.ppermute(array, 'tile', [(i, i ^ 1) for i in range(ranks)])  5.2 us
    pallas_call x1, Pallas kernels, prepare(): pl.pallas_call(functools.partial(prepare_kernel, scale), grid=(PARTS,), o...  3.07 us
  transfers between devices with their start and end apart: 12, of which 6 were waited for; matrix products, arithmetic and copies ran while one was open for 0% of the time, Pallas kernels for 27%

profile of v1, /device:TPU:0, one launch (start us, length us, event | category | flops | bytes accessed | tf_op | source)
XLA Modules:
  0.0 97.0 jit_solution(820733696585207757)
XLA Ops:
  0.6 1.4 %pack.1.refs_0_.refs_1_.refs_2_ = f32[8,2176]{1,0:T(8,128)} custom-call(f32[2,2048]{1,0:T(2,128)} %offsets_ref.1, s32[8,8]{1,0:T(8,128)} %pairs_ref.1), custom_call_target="tpu_custom_call" | custom-call | tf_op jit(solution)/shard_map/pack/pallas_call | solution.py:53
  2.5 1.0 %collective-permute-done.refs_1_.refs_0_.refs_3_ = f32[8,2176]{1,0:T(8,128)S(1)} collective-permute-done((f32[8,2176]{1,0:T(8,128)}, f32[8,2176]{1,0:T(8,128)S(1)}, u32[]{:S(2)}, u32[]{:S(2)}) %collective-permute-start) | collective-permute-done | bytes 69664 | tf_op jit(solution)/shard_map/ppermute | solution.py:510
  4.2 1.6 %pair.4 = f32[2,8,2176]{2,1,0:T(8,128)} custom-call(f32[8,2176]{1,0:T(8,128)} %pack.1.refs_0_.refs_1_.refs_2_, f32[8,2176]{1,0:T(8,128)} %copy-done.13), custom_call_target="tpu_custom_call" | custom-call | tf_op jit(solution)/shard_map/pair/pallas_call | solution.py:72
  5.8 0.7 collective-permute-start.1
  6.5 0.8 copy-done.6
  7.3 3.1 %prepare.1 = (bf16[32,32,512]{2,1,0:T(8,128)(2,1)S(1)}, f32[2,16384]{1,0:T(2,128)S(1)}, f32[128,128]{1,0:T(8,128)S(1)}, f32[2,128]{1,0:T(2,128)S(1)}) custom-call(s32[128,128]{1,0:T(8,128)S(1)} %bitcast.24, s32[1,16384]{1,0:T(1,128)S(1)} %bitcast.25, f32[16,16384]{1,0:T(8,128)} %direction_ref.3, f32[16,16384]{1,0:T(8,128)} %old_ref.1), custom_call_target="tpu_custom_call" | custom-call | flops 2097152 | bytes 3145728 | tf_op jit(solution)/shard_map/prepare/pallas_call | solution.py:119
  10.4 2.7 %forward.3 = f32[8,16,256]{2,1,0:T(8,128)S(1)} custom-call(s32[1]{0:T(128)S(6)} %add.25.first_ref, f32[1]{0:T(128)S(6)} %convert_element_type.10.shift_ref, f32[8,2176]{1,0:T(8,128)S(1)} %copy-done.14, f32[8,2176]{1,0:T(8,128)S(1)} %copy-done.14, bf16[32,32,512]{2,1,0:T(8,128)(2,1)S(1)} %get-tuple-element.23.refs_2_.refs_6_, ...), custom_call_target="tpu_custom_call" | custom-call | flops 3774873600 | bytes 1048576 | tf_op jit(solution)/shard_map/forward/pallas_call | solution.py:265
  13.1 5.0 %collective-permute-start.3 = (f32[8,2176]{1,0:T(8,128)S(1)}, f32[8,2176]{1,0:T(8,128)S(1)}, u32[]{:S(2)}, u32[]{:S(2)}) collective-permute-start(f32[8,2176]{1,0:T(8,128)S(1)} %get-tuple-element.48.refs_0_.refs_3_), channel_id=1, source_target_pairs={{0,1},{1,0},{2,3},{3,2},{4,5},{5,4},{6,7},{7,6},{8,9},{9,8},{10,11... | collective-permute-start | bytes 208904 | tf_op jit(solution)/shard_map/ppermute | solution.py:510
  18.2 1.7 %pair.5 = f32[2,16,2048]{2,1,0:T(8,128)} custom-call(f32[16,2048]{1,0:T(8,128)} %residual_ref.1, f32[16,2048]{1,0:T(8,128)} %copy-done.9), custom_call_target="tpu_custom_call" | custom-call | tf_op jit(solution)/shard_map/pair/pallas_call | solution.py:72
  19.8 0.7 collective-permute-start.4
  20.5 4.1 %forward.4 = (f32[8,16,256]{2,1,0:T(8,128)S(1)}, f32[8,16,256]{2,1,0:T(8,128)S(1)}, f32[8,16,256]{2,1,0:T(8,128)S(1)}) custom-call(s32[3]{0:T(128)S(1)} %multiply_add_fusion.1.first_ref, f32[3]{0:T(128)S(1)} %get-tuple-element.41.shift_ref, f32[8,2176]{1,0:T(8,128)S(1)} %get-tuple-element.48.refs_0_.refs_3_, ...), custom_call_target="tpu_custom_call" | custom-call | flops 11953766400 | bytes 1048576 | tf_op jit(solution)/shard_map/forward/pallas_call | solution.py:265
  24.7 0.6 copy-done.7
  26.0 5.1 %collective-permute-start.5 = (f32[16,2048]{1,0:T(8,128)S(1)}, f32[16,2048]{1,0:T(8,128)S(1)}, u32[]{:S(2)}, u32[]{:S(2)}) collective-permute-start(f32[16,2048]{1,0:T(8,128)S(1)} %get-tuple-element.46.refs_6_), channel_id=1, source_target_pairs={{0,1},{1,0},{2,3},{3,2},{4,5},{5,4},{6,7},{7,6},{8,9},{9,8},{10,11... | collective-permute-start | bytes 393224 | tf_op jit(solution)/shard_map/ppermute | solution.py:510
  31.2 0.9 collective-permute-done.5.refs_8_
  32.4 0.6 copy-done.15
  33.1 1.8 %pair.6 = f32[2,8,16,256]{3,2,1,0:T(8,128)} custom-call(f32[8,16,256]{2,1,0:T(8,128)} %copy-done.7, f32[8,16,256]{2,1,0:T(8,128)} %copy-done.8, f32[8,16,256]{2,1,0:T(8,128)} %copy-done.15), custom_call_target="tpu_custom_call" | custom-call | tf_op jit(solution)/shard_map/pair/pallas_call | solution.py:72
  34.8 0.8 collective-permute-start.7
  35.6 4.9 %forward.5 = f32[8,16,256]{2,1,0:T(8,128)S(1)} custom-call(s32[1]{0:T(128)} %constant.12.clone.1.first_ref, f32[1]{0:T(128)} %constant.40.clone.1.shift_ref, f32[8,2176]{1,0:T(8,128)S(1)} %copy-done.5, f32[8,2176]{1,0:T(8,128)S(1)} %copy-done.5, bf16[32,32,512]{2,1,0:T(8,128)(2,1)S(1)} %get-tuple-element.23.refs_2_.refs_6_, ...), custom_call_target="tpu_custom_call" | custom-call | flops 3774873600 | bytes 1048576 | tf_op jit(solution)/shard_map/forward/pallas_call | solution.py:265
  40.5 8.8 %collective-permute-start.8 = (f32[8,16,256]{2,1,0:T(8,128)S(1)}, f32[8,16,256]{2,1,0:T(8,128)S(1)}, u32[]{:S(2)}, u32[]{:S(2)}) collective-permute-start(f32[8,16,256]{2,1,0:T(8,128)S(1)} %bitcast_add_fusion), channel_id=1, source_target_pairs={{0,1},{1,0},{2,3},{3,2},{4,5},{5,4},{6,7},{7,6},{8,9},{9,8},{10,11... | collective-permute-start | bytes 393224 | tf_op jit(solution)/shard_map/ppermute | solution.py:510
  49.4 1.0 %collective-permute-done.8 = f32[8,16,256]{2,1,0:T(8,128)S(1)} collective-permute-done((f32[8,16,256]{2,1,0:T(8,128)S(1)}, f32[8,16,256]{2,1,0:T(8,128)S(1)}, u32[]{:S(2)}, u32[]{:S(2)}) %collective-permute-start.8) | collective-permute-done | bytes 131104 | tf_op jit(solution)/shard_map/ppermute | solution.py:510
  50.9 0.9 collective-permute-done.9.refs_1_.refs_7_
  51.8 0.6 copy-done.11
  52.5 1.7 %pair.7 = f32[2,8,16,256]{3,2,1,0:T(8,128)} custom-call(f32[8,16,256]{2,1,0:T(8,128)} %copy-done.1, f32[8,16,256]{2,1,0:T(8,128)} %copy-done.11), custom_call_target="tpu_custom_call" | custom-call | tf_op jit(solution)/shard_map/pair/pallas_call | solution.py:72
  54.1 0.7 collective-permute-start.10
  54.8 0.9 copy-done.2
  55.7 0.9 copy-done.12
  56.7 8.2 %near.1.refs_13_ = f32[32,32,512]{2,1,0:T(8,128)S(1)} custom-call(s32[2]{0:T(128)S(1)} %get-tuple-element.49.first_ref, f32[2]{0:T(128)S(1)} %get-tuple-element.50.shift_ref, f32[8,2176]{1,0:T(8,128)S(1)} %copy-done.5, f32[8,2176]{1,0:T(8,128)S(1)} %copy-done.14, f32[8,2176]{1,0:T(8,128)S(1)} %copy-done.5, f32[8,2176]{1,0:T(8,128)S(1)} %copy-done.14, ...), custom_call_target="tpu_custom_call" | custom-call | flops 7864320000 | bytes 1048576 | tf_op jit(solution)/shard_map/near/pallas_call | solution.py:440
  64.9 4.9 %collective-permute-start.11 = (f32[8,16,256]{2,1,0:T(8,128)S(1)}, f32[8,16,256]{2,1,0:T(8,128)S(1)}, u32[]{:S(2)}, u32[]{:S(2)}) collective-permute-start(f32[8,16,256]{2,1,0:T(8,128)S(1)} %get-tuple-element.44.refs_9_), channel_id=1, source_target_pairs={{0,1},{1,0},{2,3},{3,2},{4,5},{5,4},{6,7},{7,6},{8,9},{9,8},{10,11... | collective-permute-start | bytes 393224 | tf_op jit(solution)/shard_map/ppermute | solution.py:510
  69.9 1.0 %collective-permute-done.11.refs_11_ = f32[8,16,256]{2,1,0:T(8,128)S(1)} collective-permute-done((f32[8,16,256]{2,1,0:T(8,128)S(1)}, f32[8,16,256]{2,1,0:T(8,128)S(1)}, u32[]{:S(2)}, u32[]{:S(2)}) %collective-permute-start.11) | collective-permute-done | bytes 131104 | tf_op jit(solution)/shard_map/ppermute | solution.py:510
  70.9 6.1 %far.1 = (f32[16,16384]{1,0:T(8,128)S(1)}, f32[16,16384]{1,0:T(8,128)S(1)}, f32[16,1,128]{2,1,0:T(1,128)S(1)}) custom-call(s32[3]{0:T(128)S(1)} %multiply_add_fusion.1.first_ref, f32[3]{0:T(128)S(1)} %get-tuple-element.41.shift_ref, f32[8,2176]{1,0:T(8,128)S(1)} %get-tuple-element.48.refs_0_.refs_3_, f32[8,2176]{1,0:T(8,128)S(1)} %get-tuple-element.47.refs_1_.refs_4_, ...), custom_call_target="tpu_custom_call" | custom-call | flops 11953766400 | bytes 1048576 | tf_op jit(solution)/shard_map/far/pallas_call | solution.py:440
  77.0 17.3 %all_to_all.5.stats_ref = f32[16,1,128]{2,1,0:T(1,128)S(1)} all-to-all(f32[16,1,128]{2,1,0:T(1,128)S(1)} %get-tuple-element.38), channel_id=1, replica_groups=mesh['groups'=2,'tile'=16] {'tile'}, dimensions={0} | all-to-all | bytes 16384 | tf_op jit(solution)/shard_map/all_to_all | solution.py:557
  94.2 2.8 %finish.1 = (f32[16,16384]{1,0:T(8,128)}, f32[16,2048]{1,0:T(8,128)}, f32[16,16384]{1,0:T(8,128)}) custom-call(f32[16,1,128]{2,1,0:T(1,128)S(1)} %all_to_all.5.stats_ref, f32[16,16384]{1,0:T(8,128)S(1)} %get-tuple-element.39.constant_ref, f32[16,16384]{1,0:T(8,128)S(1)} %get-tuple-element.40.slope_ref, f32[16,16384]{1,0:T(8,128)S(1)} %copy-done.3, ...), custom_call_target="tpu_custom_call" | custom-call | tf_op jit(solution)/shard_map/finish/pallas_call | solution.py:483
  (45 shorter events, 2.9 us)
Async XLA Ops:
  2.0 1.6 %collective-permute-start = (f32[8,2176]{1,0:T(8,128)}, f32[8,2176]{1,0:T(8,128)S(1)}, u32[]{:S(2)}, u32[]{:S(2)}) collective-permute-start(f32[8,2176]{1,0:T(8,128)} %pack.1.refs_0_.refs_1_.refs_2_), channel_id=1, source_target_pairs={{0,1},{1,0},{2,3},{3,2},{4,5},{5,4},{6,7},{7,6},{8,9},{9,8},{10,11... | collective-permute-start | bytes 208904 | tf_op jit(solution)/shard_map/ppermute | solution.py:510
  3.6 0.6 copy-start.13
  3.6 9.5 %collective-permute-start.2 = (f32[16,2048]{1,0:T(8,128)}, f32[16,2048]{1,0:T(8,128)S(1)}, u32[]{:S(2)}, u32[]{:S(2)}) collective-permute-start(f32[16,2048]{1,0:T(8,128)} %residual_ref.1), channel_id=1, source_target_pairs={{0,1},{1,0},{2,3},{3,2},{4,5},{5,4},{6,7},{7,6},{8,9},{9,8},{10,11... | collective-permute-start | bytes 393224 | tf_op jit(solution)/shard_map/ppermute | solution.py:510
  5.8 7.3 %collective-permute-start.1 = (f32[2,8,2176]{2,1,0:T(8,128)}, f32[2,8,2176]{2,1,0:T(8,128)S(1)}, u32[]{:S(2)}, u32[]{:S(2)}) collective-permute-start(f32[2,8,2176]{2,1,0:T(8,128)} %pair.4), channel_id=1, source_target_pairs={{1,2},{3,4},{5,6},{7,8},{9,10},{11,12},{13,14},{2,1},{4,3},{6,5},{... | collective-permute-start | bytes 417800 | tf_op jit(solution)/shard_map/ppermute | solution.py:514
  6.4 0.8 copy-start.6
  7.3 3.1 %copy-start.14 = (f32[8,2176]{1,0:T(8,128)S(1)}, f32[8,2176]{1,0:T(8,128)}, u32[]{:S(2)}) copy-start(f32[8,2176]{1,0:T(8,128)} %copy-done.13) | copy-start | bytes 208900
  13.1 5.1 %copy-start.9 = (f32[16,2048]{1,0:T(8,128)}, f32[16,2048]{1,0:T(8,128)S(1)}, u32[]{:S(2)}) copy-start(f32[16,2048]{1,0:T(8,128)S(1)} %collective-permute-done.2.refs_1_.refs_5_) | copy-start | bytes 393220
  13.1 7.4 %collective-permute-start.3 = (f32[8,2176]{1,0:T(8,128)S(1)}, f32[8,2176]{1,0:T(8,128)S(1)}, u32[]{:S(2)}, u32[]{:S(2)}) collective-permute-start(f32[8,2176]{1,0:T(8,128)S(1)} %get-tuple-element.48.refs_0_.refs_3_), channel_id=1, source_target_pairs={{0,1},{1,0},{2,3},{3,2},{4,5},{5,4},{6,7},{7,6},{8,9},{9,8},{10,11... | collective-permute-start | bytes 208904 | tf_op jit(solution)/shard_map/ppermute | solution.py:510
  19.8 6.1 %collective-permute-start.4 = (f32[2,16,2048]{2,1,0:T(8,128)}, f32[2,16,2048]{2,1,0:T(8,128)S(1)}, u32[]{:S(2)}, u32[]{:S(2)}) collective-permute-start(f32[2,16,2048]{2,1,0:T(8,128)} %pair.5), channel_id=1, source_target_pairs={{1,2},{3,4},{5,6},{7,8},{9,10},{11,12},{13,14},{2,1},{4,3},{6,5},{... | collective-permute-start | bytes 786440 | tf_op jit(solution)/shard_map/ppermute | solution.py:514
  20.5 15.1 %copy-start.5 = (f32[8,2176]{1,0:T(8,128)S(1)}, f32[8,2176]{1,0:T(8,128)}, u32[]{:S(2)}) copy-start(f32[8,2176]{1,0:T(8,128)} %pack.1.refs_0_.refs_1_.refs_2_) | copy-start | bytes 208900
  24.7 0.7 copy-start.7
  25.3 0.6 copy-start.8
  26.0 6.1 %collective-permute-start.5 = (f32[16,2048]{1,0:T(8,128)S(1)}, f32[16,2048]{1,0:T(8,128)S(1)}, u32[]{:S(2)}, u32[]{:S(2)}) collective-permute-start(f32[16,2048]{1,0:T(8,128)S(1)} %get-tuple-element.46.refs_6_), channel_id=1, source_target_pairs={{0,1},{1,0},{2,3},{3,2},{4,5},{5,4},{6,7},{7,6},{8,9},{9,8},{10,11... | collective-permute-start | bytes 393224 | tf_op jit(solution)/shard_map/ppermute | solution.py:510
  31.1 1.3 %collective-permute-start.6 = (f32[8,16,256]{2,1,0:T(8,128)S(1)}, f32[8,16,256]{2,1,0:T(8,128)S(1)}, u32[]{:S(2)}, u32[]{:S(2)}) collective-permute-start(f32[8,16,256]{2,1,0:T(8,128)S(1)} %get-tuple-element.30), channel_id=1, source_target_pairs={{0,1},{1,0},{2,3},{3,2},{4,5},{5,4},{6,7},{7,6},{8,9},{9,8},{10,11... | collective-permute-start | bytes 393224 | tf_op jit(solution)/shard_map/ppermute | solution.py:510
  32.4 0.6 copy-start.15
  34.8 20.0 %copy-start.4 = (f32[16,2048]{1,0:T(8,128)S(1)}, f32[16,2048]{1,0:T(8,128)}, u32[]{:S(2)}) copy-start(f32[16,2048]{1,0:T(8,128)} %residual_ref.1) | copy-start | bytes 393220
  34.8 20.0 %copy-start.10 = (f32[16,2048]{1,0:T(8,128)S(1)}, f32[16,2048]{1,0:T(8,128)}, u32[]{:S(2)}) copy-start(f32[16,2048]{1,0:T(8,128)} %copy-done.9) | copy-start | bytes 393220
  34.8 5.7 %collective-permute-start.7 = (f32[2,8,16,256]{3,2,1,0:T(8,128)}, f32[2,8,16,256]{3,2,1,0:T(8,128)S(1)}, u32[]{:S(2)}, u32[]{:S(2)}) collective-permute-start(f32[2,8,16,256]{3,2,1,0:T(8,128)} %pair.6), channel_id=1, source_target_pairs={{1,2},{3,4},{5,6},{7,8},{9,10},{11,12},{13,14},{2,1},{4,3},{6,5},{... | collective-permute-start | bytes 786440 | tf_op jit(solution)/shard_map/ppermute | solution.py:514
  40.5 9.8 %collective-permute-start.8 = (f32[8,16,256]{2,1,0:T(8,128)S(1)}, f32[8,16,256]{2,1,0:T(8,128)S(1)}, u32[]{:S(2)}, u32[]{:S(2)}) collective-permute-start(f32[8,16,256]{2,1,0:T(8,128)S(1)} %bitcast_add_fusion), channel_id=1, source_target_pairs={{0,1},{1,0},{2,3},{3,2},{4,5},{5,4},{6,7},{7,6},{8,9},{9,8},{10,11... | collective-permute-start | bytes 393224 | tf_op jit(solution)/shard_map/ppermute | solution.py:510
  50.4 1.4 %copy-start.1 = (f32[8,16,256]{2,1,0:T(8,128)}, f32[8,16,256]{2,1,0:T(8,128)S(1)}, u32[]{:S(2)}) copy-start(f32[8,16,256]{2,1,0:T(8,128)S(1)} %fusion.refs_0_.refs_6_.refs_17_.image_ref) | copy-start | bytes 393220
  50.4 1.4 %collective-permute-start.9 = (f32[8,16,256]{2,1,0:T(8,128)S(1)}, f32[8,16,256]{2,1,0:T(8,128)S(1)}, u32[]{:S(2)}, u32[]{:S(2)}) collective-permute-start(f32[8,16,256]{2,1,0:T(8,128)S(1)} %fusion.refs_0_.refs_6_.refs_17_.image_ref), channel_id=1, source_target_pairs={{0,1},{1,0},{2,3},{3,2},{4,5},{5,4},{6,7},{7,6},{8,9},{9,8},{10,11... | collective-permute-start | bytes 393224 | tf_op jit(solution)/shard_map/ppermute | solution.py:510
  51.8 0.6 copy-start.11
  54.1 10.8 %collective-permute-start.10 = (f32[2,8,16,256]{3,2,1,0:T(8,128)}, f32[2,8,16,256]{3,2,1,0:T(8,128)S(1)}, u32[]{:S(2)}, u32[]{:S(2)}) collective-permute-start(f32[2,8,16,256]{3,2,1,0:T(8,128)} %pair.7), channel_id=1, source_target_pairs={{1,2},{3,4},{5,6},{7,8},{9,10},{11,12},{13,14},{2,1},{4,3},{6,5},{... | collective-permute-start | bytes 786440 | tf_op jit(solution)/shard_map/ppermute | solution.py:514
  54.8 0.9 copy-start.2
  55.7 0.9 copy-start.12
  56.6 14.2 %copy-start = (f32[16,16384]{1,0:T(8,128)S(1)}, f32[16,16384]{1,0:T(8,128)}, u32[]{:S(2)}) copy-start(f32[16,16384]{1,0:T(8,128)} %direction_ref.3) | copy-start | bytes 3145732
  56.6 14.2 %copy-start.3 = (f32[16,16384]{1,0:T(8,128)S(1)}, f32[16,16384]{1,0:T(8,128)}, u32[]{:S(2)}) copy-start(f32[16,16384]{1,0:T(8,128)} %model_ref.1) | copy-start | bytes 3145732
  64.9 5.9 %collective-permute-start.11 = (f32[8,16,256]{2,1,0:T(8,128)S(1)}, f32[8,16,256]{2,1,0:T(8,128)S(1)}, u32[]{:S(2)}, u32[]{:S(2)}) collective-permute-start(f32[8,16,256]{2,1,0:T(8,128)S(1)} %get-tuple-element.44.refs_9_), channel_id=1, source_target_pairs={{0,1},{1,0},{2,3},{3,2},{4,5},{5,4},{6,7},{7,6},{8,9},{9,8},{10,11... | collective-permute-start | bytes 393224 | tf_op jit(solution)/shard_map/ppermute | solution.py:510

commit v2 on v1

--- a/solution.py
+++ b/solution.py
@@ -28,8 +28,8 @@
 VMEM = pl.BlockSpec(memory_space=pltpu.VMEM)
 
 
-def params():
-    return pltpu.CompilerParams(vmem_limit_bytes=24 * 2**20)
+def params(mebibytes=16):
+    return pltpu.CompilerParams(vmem_limit_bytes=mebibytes * 2**20)
 
 
 def split(values):
@@ -42,19 +42,24 @@
 
 
 def pack_kernel(offsets_ref, pairs_ref, message_ref):
-    stations = offsets_ref.shape[1]
+    lines = offsets_ref.shape[1] // LANES
     message_ref[...] = jnp.zeros_like(message_ref)
-    message_ref[pl.ds(0, 2), pl.ds(0, stations)] = offsets_ref[...]
-    message_ref[:, pl.ds(stations, pairs_ref.shape[1])] = pairs_ref[...].astype(F32) + 1.0
+    for i in range(lines):
+        at = pl.ds(i * LANES, LANES)
+        message_ref[pl.ds(i, 1), :] = offsets_ref[pl.ds(0, 1), at]
+        message_ref[pl.ds(lines + i, 1), :] = offsets_ref[pl.ds(1, 1), at]
+    rows, pairs = pairs_ref.shape
+    message_ref[pl.ds(2 * lines, rows), pl.ds(0, pairs)] = pairs_ref[...].astype(F32) + 1.0
 
 
 def pack(station_offsets, block_pairs):
-    rows, stations = block_pairs.shape[0], station_offsets.shape[1]
+    rows = 2 * station_offsets.shape[1] // LANES + block_pairs.shape[0]
     return pl.pallas_call(
         pack_kernel,
-        out_shape=jax.ShapeDtypeStruct((rows, stations + LANES), F32),
+        out_shape=jax.ShapeDtypeStruct((rows, LANES), F32),
         in_specs=[VMEM] * 2,
         out_specs=VMEM,
+        compiler_params=params(2),
         name="pack",
     )(station_offsets, block_pairs)
 
@@ -74,11 +79,12 @@
         out_shape=jax.ShapeDtypeStruct((2, *first.shape), F32),
         in_specs=[VMEM] * (2 + len(added)),
         out_specs=VMEM,
+        compiler_params=params(2),
         name="pair",
     )(first, second, *added)
 
 
-def prepare_kernel(scale, band_ref, band_row_ref, direction_ref, old_ref, values_ref, cells_ref, turned_ref, sums_ref):
+def prepare_kernel(scale, band_ref, band_row_ref, direction_ref, values_ref, cells_ref, turned_ref):
     blocks = values_ref.shape[0]
     epochs = direction_ref.shape[0]
 
@@ -86,36 +92,28 @@
     def first():
         depth = (band_ref[...].astype(F32) + 0.5) * (DEPTH_RANGE / BANDS)
         turned_ref[...] = (depth * depth).T
-        sums_ref[...] = jnp.zeros_like(sums_ref)
-
-    def block(w, sums):
+
+    def block(w, unused):
         at = pl.ds(pl.multiple_of(w * CBLOCK, CBLOCK), CBLOCK)
         row = (band_row_ref[:, at].astype(F32) + 0.5) * (DEPTH_RANGE / BANDS)
         shifted = row + DEPTH_SHIFT
         factor = row * scale * (shifted * jnp.sqrt(shifted))
         cells_ref[pl.ds(0, 1), at] = row * row
         cells_ref[pl.ds(1, 1), at] = factor
-        values = direction_ref[:, at]
-        old = old_ref[:, at]
-        high, low = split(values * factor)
+        high, low = split(direction_ref[:, at] * factor)
         values_ref[w, pl.ds(0, epochs), :] = high
         values_ref[w, pl.ds(epochs, epochs), :] = low
-        return sums[0] + old * old, sums[1] + values * values
-
-    zero = jnp.zeros((epochs, CBLOCK), F32)
-    old_sum, direction_sum = lax.fori_loop(0, blocks, block, (zero, zero), unroll=2)
-    sums_ref[pl.ds(0, 1), :] += jnp.broadcast_to(jnp.sum(old_sum).reshape(1, 1), (1, LANES))
-    sums_ref[pl.ds(1, 1), :] += jnp.broadcast_to(jnp.sum(direction_sum).reshape(1, 1), (1, LANES))
-
-
-PARTS = 4
-
-
-def prepare(scale, depth_band, direction, old_grad):
+        return 0
+
+    lax.fori_loop(0, blocks, block, 0, unroll=4)
+
+
+PARTS = 2
+
+
+def prepare(scale, depth_band, direction):
     epochs, cells = direction.shape
     blocks = cells // CBLOCK
-    direction, old_grad = (pltpu.with_memory_space_constraint(array, pltpu.HBM) for array in (direction, old_grad))
-    wide = pl.BlockSpec((epochs, cells // PARTS), lambda i: (0, i))
     return pl.pallas_call(
         functools.partial(prepare_kernel, scale),
         grid=(PARTS,),
@@ -123,44 +121,63 @@
             jax.ShapeDtypeStruct((blocks, 2 * epochs, CBLOCK), BF16),
             jax.ShapeDtypeStruct((2, cells), F32),
             jax.ShapeDtypeStruct((cells // LANES, LANES), F32),
-            jax.ShapeDtypeStruct((2, LANES), F32),
         ),
-        in_specs=[VMEM, pl.BlockSpec((1, cells // PARTS), lambda i: (0, i)), wide, wide],
+        in_specs=[
+            VMEM,
+            pl.BlockSpec((1, cells // PARTS), lambda i: (0, i)),
+            pl.BlockSpec((epochs, cells // PARTS), lambda i: (0, i)),
+        ],
         out_specs=(
             pl.BlockSpec((blocks // PARTS, 2 * epochs, CBLOCK), lambda i: (i, 0, 0)),
             pl.BlockSpec((2, cells // PARTS), lambda i: (0, i)),
             VMEM,
-            VMEM,
         ),
-        compiler_params=params(),
+        compiler_params=params(8),
         cost_estimate=pl.CostEstimate(flops=8 * epochs * cells, bytes_accessed=12 * epochs * cells, transcendentals=0),
         name="prepare",
-    )(depth_band.reshape(cells // LANES, LANES), depth_band.reshape(1, cells), direction, old_grad)
-
-
-def list_pairs(sizes, first_ref, codes, list_ref):
-    cell_blocks, station_blocks, pairs = sizes[:3]
+    )(
+        depth_band.reshape(cells // LANES, LANES),
+        depth_band.reshape(1, cells),
+        pltpu.with_memory_space_constraint(direction, pltpu.HBM),
+    )
+
+
+def send_codes(sizes, first_ref, messages, codes_ref, scalars_ref, sent):
+    cell_blocks, station_blocks, pairs, epochs, slots = sizes
+    q = lax.broadcasted_iota(jnp.int32, (station_blocks, LANES), 0)
+    for slot, message_ref in enumerate(messages):
+        codes = message_ref[pl.ds(message_ref.shape[0] - station_blocks, station_blocks), :]
+        within = codes.astype(jnp.int32) - first_ref[slot]
+        hit = jnp.logical_and(within >= 0, within < cell_blocks)
+        code = (slot * station_blocks + q) * cell_blocks + within
+        codes_ref[pl.ds(slot * station_blocks, station_blocks), :] = jnp.where(hit, code, -1)
+    copy = pltpu.make_async_copy(codes_ref, scalars_ref, sent)
+    copy.start()
+    return copy
+
+
+def list_pairs(sizes, copy, scalars_ref, list_ref):
+    cell_blocks, station_blocks, pairs, epochs, slots = sizes
+    copy.wait()
     count = jnp.int32(0)
-    for slot, codes_ref in enumerate(codes):
-        first = first_ref[slot]
-        for q in range(station_blocks):
-            for i in range(pairs):
-                within = codes_ref[q, i].astype(jnp.int32) - first
-                hit = jnp.logical_and(within >= 0, within < cell_blocks)
-                list_ref[count] = (slot * station_blocks + q) * cell_blocks + within
-                count = count + hit.astype(jnp.int32)
+    for row in range(slots * station_blocks):
+        for i in range(pairs):
+            code = scalars_ref[row, i]
+            list_ref[count] = code
+            count = count + (code >= 0).astype(jnp.int32)
     for i in range(UNROLL + 4):
-        list_ref[count + i] = len(codes) * station_blocks * cell_blocks
+        list_ref[count + i] = slots * station_blocks * cell_blocks
     return count
 
 
-def pair_list(sizes):
-    cell_blocks, station_blocks, pairs, epochs, slots = sizes
-    return pltpu.SMEM((slots * station_blocks * pairs + UNROLL + 4,), jnp.int32)
-
-
-def codes_spec(stations):
-    return pl.BlockSpec((8, LANES), lambda i: (0, stations // LANES), memory_space=pltpu.SMEM)
+def list_scratch(sizes):
+    cell_blocks, station_blocks, pairs, epochs, slots = sizes
+    return [
+        pltpu.SMEM((slots * station_blocks * pairs + UNROLL + 4,), jnp.int32),
+        pltpu.VMEM((slots * station_blocks, LANES), jnp.int32),
+        pltpu.SMEM((slots * station_blocks, LANES), jnp.int32),
+        pltpu.SemaphoreType.DMA(()),
+    ]
 
 
 UNROLL = 4
@@ -200,22 +217,24 @@
 
 def forward_kernel(sizes, first_ref, shift_ref, *refs):
     cell_blocks, station_blocks, pairs, epochs, slots = sizes
-    codes = refs[:slots]
-    messages = refs[slots : 2 * slots]
-    values_ref, turned_ref = refs[2 * slots : 2 * slots + 2]
-    images = refs[2 * slots + 2 : 3 * slots + 2]
-    list_ref, across_ref, along_ref, image_ref, gaps_ref, lines_ref, depths_ref = refs[3 * slots + 2 :]
+    messages = refs[:slots]
+    values_ref, turned_ref = refs[slots : slots + 2]
+    images = refs[slots + 2 : 2 * slots + 2]
+    list_ref, codes_ref, scalars_ref, sent, *scratch = refs[2 * slots + 2 :]
+    across_ref, along_ref, image_ref, gaps_ref, lines_ref, depths_ref = scratch
+    copy = send_codes(sizes, first_ref, messages, codes_ref, scalars_ref, sent)
     dummy = slots * station_blocks
+    per_block = SBLOCK // LANES
+    lines = station_blocks * per_block
     across_ref[pl.ds(dummy, 1), :] = jnp.zeros((1, SBLOCK), F32)
     along_ref[pl.ds(dummy, 1), :] = jnp.zeros((1, SBLOCK), F32)
     image_ref[...] = jnp.zeros_like(image_ref)
     for slot in range(slots):
-        for q in range(station_blocks):
-            at = pl.ds(q * SBLOCK, SBLOCK)
-            row = pl.ds(slot * station_blocks + q, 1)
-            across_ref[row, :] = messages[slot][pl.ds(0, 1), at] + shift_ref[slot]
-            along_ref[row, :] = messages[slot][pl.ds(1, 1), at]
-    count = list_pairs(sizes, first_ref, codes, list_ref)
+        for i in range(lines):
+            place = (pl.ds(slot * station_blocks + i // per_block, 1), pl.ds(i % per_block * LANES, LANES))
+            across_ref[place] = messages[slot][pl.ds(i, 1), :] + shift_ref[slot]
+            along_ref[place] = messages[slot][pl.ds(lines + i, 1), :]
+    count = list_pairs(sizes, copy, scalars_ref, list_ref)
     column = lax.broadcasted_iota(jnp.int32, (COL_SIDE, SBLOCK), 0).astype(F32)
     column = (column + 0.5) / COL_SIDE
     rows = CBLOCK // COL_SIDE
@@ -260,16 +279,14 @@
 
 def forward(sizes, first, shift, messages, values, turned):
     cell_blocks, station_blocks, pairs, epochs, slots = sizes
-    stations = station_blocks * SBLOCK
     rows = (slots * station_blocks + 8) // 8 * 8
     return pl.pallas_call(
         functools.partial(forward_kernel, sizes),
-        grid=(1,),
         out_shape=(jax.ShapeDtypeStruct((station_blocks, epochs, SBLOCK), F32),) * slots,
-        in_specs=[SMEM, SMEM] + [codes_spec(stations)] * slots + [VMEM] * (slots + 2),
+        in_specs=[SMEM, SMEM] + [VMEM] * (slots + 2),
         out_specs=(VMEM,) * slots,
-        scratch_shapes=[
-            pair_list(sizes),
+        scratch_shapes=list_scratch(sizes)
+        + [
             pltpu.VMEM((rows, SBLOCK), F32),
             pltpu.VMEM((rows, SBLOCK), F32),
             pltpu.VMEM((slots * station_blocks + 1, epochs, SBLOCK), F32),
@@ -280,7 +297,7 @@
         compiler_params=params(),
         cost_estimate=estimate(sizes),
         name="forward",
-    )(first, shift, *messages, *messages, values, turned)
+    )(first, shift, *messages, values, turned)
 
 
 def estimate(sizes):
@@ -289,9 +306,10 @@
     return pl.CostEstimate(flops=2 * 1200 * entries, bytes_accessed=2**20, transcendentals=entries)
 
 
-def adjoint_sums(sizes, first_ref, shift_ref, codes, messages, residuals, images, cells_ref, total_ref, scratch):
-    cell_blocks, station_blocks, pairs, epochs, slots = sizes
-    list_ref, stations_ref, terms_ref, depths_ref, gaps_ref, lines_ref = scratch
+def adjoint_sums(sizes, first_ref, shift_ref, messages, residuals, images, cells_ref, total_ref, scratch):
+    cell_blocks, station_blocks, pairs, epochs, slots = sizes
+    list_ref, codes_ref, scalars_ref, sent, stations_ref, terms_ref, depths_ref, gaps_ref, lines_ref = scratch
+    copy = send_codes(sizes, first_ref, messages, codes_ref, scalars_ref, sent)
     dummy = slots * station_blocks
     terms_ref[dummy] = jnp.zeros(terms_ref.shape[1:], BF16)
     stations_ref[slots] = jnp.zeros(stations_ref.shape[1:], F32)
@@ -299,16 +317,15 @@
     per_block = SBLOCK // LANES
     lane_rows = station_blocks * per_block
     for slot in range(slots):
-        parts = [messages[slot][pl.ds(0, 1), pl.ds(i * LANES, LANES)] + shift_ref[slot] for i in range(lane_rows)]
-        parts += [messages[slot][pl.ds(1, 1), pl.ds(i * LANES, LANES)] for i in range(lane_rows)]
-        parts.append(jnp.zeros((LANES - 2 * lane_rows, LANES), F32))
-        stations_ref[slot] = jnp.concatenate(parts, axis=0).T
+        places = [messages[slot][pl.ds(0, lane_rows), :] + shift_ref[slot], messages[slot][pl.ds(lane_rows, lane_rows), :]]
+        places.append(jnp.zeros((LANES - 2 * lane_rows, LANES), F32))
+        stations_ref[slot] = jnp.concatenate(places, axis=0).T
         for q in range(station_blocks):
             stacked = jnp.concatenate([residuals[slot][:, pl.ds(q * SBLOCK, SBLOCK)], images[slot][q]], axis=0)
             high, low = split(stacked)
             terms_ref[slot * station_blocks + q, pl.ds(0, 2 * epochs), :] = high
             terms_ref[slot * station_blocks + q, pl.ds(2 * epochs, 2 * epochs), :] = low
-    count = list_pairs(sizes, first_ref, codes, list_ref)
+    count = list_pairs(sizes, copy, scalars_ref, list_ref)
     lane = lax.broadcasted_iota(jnp.int32, (1, LANES), 1)
     column = ((lane % COL_SIDE).astype(F32) + 0.5) / COL_SIDE
     line = ((lane // COL_SIDE).astype(F32) + 0.5) / COL_SIDE
@@ -360,24 +377,30 @@
     pl.run_scoped(run, *accumulators(4 * epochs))
 
 
-def adjoint_refs(slots, refs):
-    codes, messages, residuals, images = (refs[i * slots : (i + 1) * slots] for i in range(4))
-    return codes, messages, residuals, images, refs[4 * slots :]
-
-
 def near_kernel(sizes, first_ref, shift_ref, *refs):
-    codes, messages, residuals, images, rest = adjoint_refs(sizes[-1], refs)
-    cells_ref, total_ref, *scratch = rest
-    adjoint_sums(sizes, first_ref, shift_ref, codes, messages, residuals, images, cells_ref, total_ref, scratch)
+    cell_blocks, station_blocks, pairs, epochs, slots = sizes
+    messages, residuals, images = (refs[i * slots : (i + 1) * slots] for i in range(3))
+    cells_ref, direction_ref, old_ref, total_ref, sums_ref, *scratch = refs[3 * slots :]
+    adjoint_sums(sizes, first_ref, shift_ref, messages, residuals, images, cells_ref, total_ref, scratch)
+
+    def add(w, sums):
+        at = pl.ds(pl.multiple_of(w * CBLOCK, CBLOCK), CBLOCK)
+        direction, old = direction_ref[:, at], old_ref[:, at]
+        return sums[0] + old * old, sums[1] + direction * direction
+
+    zero = jnp.zeros((epochs, CBLOCK), F32)
+    for i, total in enumerate(lax.fori_loop(0, cell_blocks, add, (zero, zero), unroll=4)):
+        sums_ref[pl.ds(i, 1), :] = jnp.broadcast_to(jnp.sum(total).reshape(1, 1), (1, LANES))
 
 
 def far_kernel(sizes, first_ref, shift_ref, *refs):
     cell_blocks, station_blocks, pairs, epochs, slots = sizes
-    codes, messages, residuals, images, rest = adjoint_refs(slots, refs)
-    cells_ref, near_ref, model_ref, direction_ref, sums_ref, image_ref = rest[:6]
+    messages, residuals, images = (refs[i * slots : (i + 1) * slots] for i in range(3))
+    rest = refs[3 * slots :]
+    cells_ref, near_ref, sums_ref, model_ref, direction_ref, image_ref = rest[:6]
     constant_ref, slope_ref, stats_ref = rest[6:9]
     total_ref, *scratch = rest[9:]
-    adjoint_sums(sizes, first_ref, shift_ref, codes, messages, residuals, images, cells_ref, total_ref, scratch)
+    adjoint_sums(sizes, first_ref, shift_ref, messages, residuals, images, cells_ref, total_ref, scratch)
     zero = jnp.zeros((epochs, CBLOCK), F32)
 
     def combine(w, sums):
@@ -419,41 +442,37 @@
         stats_ref[i] = row
 
 
-def adjoint(sizes, first, shift, messages, residuals, images, cell_rows, last=()):
+def adjoint(sizes, first, shift, messages, residuals, images, cell_rows, *others, ranks=None):
     cell_blocks, station_blocks, pairs, epochs, slots = sizes
     total = (cell_blocks, 2 * epochs, CBLOCK)
-    scratch = [
-        pair_list(sizes),
+    scratch = list_scratch(sizes) + [
         pltpu.VMEM((slots + 1, LANES, LANES), F32),
         pltpu.VMEM((slots * station_blocks + 1, 4 * epochs, SBLOCK), BF16),
         pltpu.VMEM((2, 1, CBLOCK), F32),
         pltpu.VMEM((2, SBLOCK, LANES), F32),
         pltpu.VMEM((2, SBLOCK, LANES), F32),
     ]
-    if last:
-        ranks, *last = last
+    if ranks is None:
+        kernel, shapes = near_kernel, [total, (2, LANES)]
+    else:
         kernel, cells = far_kernel, (epochs, cell_blocks * CBLOCK)
         shapes = [cells, cells, (ranks, 1, LANES)]
         scratch = [pltpu.VMEM(total, F32)] + scratch
-    else:
-        kernel, shapes = near_kernel, [total]
     return pl.pallas_call(
         functools.partial(kernel, sizes),
-        grid=(1,),
         out_shape=tuple(jax.ShapeDtypeStruct(shape, F32) for shape in shapes),
-        in_specs=[SMEM, SMEM]
-        + [codes_spec(station_blocks * SBLOCK)] * slots
-        + [VMEM] * (3 * slots + 1 + len(last)),
+        in_specs=[SMEM, SMEM] + [VMEM] * (3 * slots + 1 + len(others)),
         out_specs=(VMEM,) * len(shapes),
         scratch_shapes=scratch,
         compiler_params=params(),
         cost_estimate=estimate(sizes),
-        name="far" if last else "near",
-    )(first, shift, *messages, *messages, *residuals, *images, cell_rows, *last)
+        name="near" if ranks is None else "far",
+    )(first, shift, *messages, *residuals, *images, cell_rows, *others)
 
 
 def finish_kernel(
-    stats_ref, constant_ref, slope_ref, model_ref, direction_ref, residual_ref, image_ref, model_out, residual_out, direction_out
+    stats_ref, constant_ref, slope_ref, model_ref, direction_ref, residual_ref, image_ref,
+    model_out, residual_out, direction_out, new_model, new_residual, new_direction, sent,
 ):
     stats = stats_ref[...][:, 0, :]
     gamma_old, direction_square, image_square = (
@@ -464,31 +483,45 @@
     reach = ahead * stats[:, 6:7]
     gamma_new = jnp.sum(stats[:, 4:5] - 2.0 * ahead * stats[:, 5:6] + reach * reach, axis=0, keepdims=True)
     ratio = gamma_new / (gamma_old + GUARD)
-    blocks = model_ref.shape[1] // CBLOCK
-
-    def block(w, unused):
-        at = pl.ds(pl.multiple_of(w * CBLOCK, CBLOCK), CBLOCK)
-        direction = direction_ref[:, at]
-        model_out[:, at] = model_ref[:, at] + step * direction
-        direction_out[:, at] = (constant_ref[:, at] - step * slope_ref[:, at]) + ratio * direction
-        return 0
-
-    lax.fori_loop(0, blocks, block, 0, unroll=2)
+    copies = []
+
+    def send(i, source, target, at):
+        copies.append(pltpu.make_async_copy(source.at[:, at], target.at[:, at], sent.at[i]))
+        copies[-1].start()
+
     for q in range(image_ref.shape[0]):
         at = pl.ds(q * SBLOCK, SBLOCK)
-        residual_out[:, at] = residual_ref[:, at] - step * image_ref[q]
+        new_residual[:, at] = residual_ref[:, at] - step * image_ref[q]
+    send(0, new_residual, residual_out, pl.ds(0, residual_ref.shape[1]))
+    cells = model_ref.shape[1] // FINISH_PARTS
+    for part in range(FINISH_PARTS):
+
+        def block(w, unused):
+            at = pl.ds(pl.multiple_of(part * cells + w * CBLOCK, CBLOCK), CBLOCK)
+            direction = direction_ref[:, at]
+            new_model[:, at] = model_ref[:, at] + step * direction
+            new_direction[:, at] = (constant_ref[:, at] - step * slope_ref[:, at]) + ratio * direction
+            return 0
+
+        lax.fori_loop(0, cells // CBLOCK, block, 0, unroll=2)
+        send(1 + 2 * part, new_model, model_out, pl.ds(part * cells, cells))
+        send(2 + 2 * part, new_direction, direction_out, pl.ds(part * cells, cells))
+    for copy in copies:
+        copy.wait()
+
+
+FINISH_PARTS = 4
 
 
 def finish(stats, constant, slope, model_field, direction, residual, image):
+    outs = (model_field.shape, residual.shape, direction.shape)
     return pl.pallas_call(
         finish_kernel,
-        out_shape=(
-            jax.ShapeDtypeStruct(model_field.shape, F32),
-            jax.ShapeDtypeStruct(residual.shape, F32),
-            jax.ShapeDtypeStruct(direction.shape, F32),
-        ),
+        out_shape=tuple(jax.ShapeDtypeStruct(shape, F32) for shape in outs),
         in_specs=[VMEM] * 7,
-        out_specs=(VMEM,) * 3,
+        out_specs=(pl.BlockSpec(memory_space=pl.ANY),) * 3,
+        scratch_shapes=[pltpu.VMEM(shape, F32) for shape in outs]
+        + [pltpu.SemaphoreType.DMA((1 + 2 * FINISH_PARTS,))],
         compiler_params=params(),
         name="finish",
     )(stats, constant, slope, model_field, direction, residual, image)
@@ -518,41 +551,36 @@
         sizes = (cell_blocks, station_blocks, pairs, epochs, len(places))
         return sizes, cell_blocks * (REACH - offsets) + 1, offsets.astype(F32)
 
-    own_slot, partner_slot, near_slots, far_slots = slots(0), slots(-1), slots(0, -1), slots(1, 2, -2)
+    near_slots, far_slots = slots(0, -1), slots(1, 2, -2)
 
     own = pack(station_offsets, block_pairs)
     partner = to_partner(own)
-    arrived = across(pair_up(own, partner))
-    partner_residual = to_partner(after(residual, partner))
-    values, cell_rows, turned, sums = prepare(
-        2.0 / math.sqrt(cells), after(depth_band, partner), direction, old_grad
-    )
-    (to_return,) = forward(*partner_slot, [partner], values, turned)
-    arrived = after(arrived, (to_return, partner_residual))
-    first_far, second_far = arrived[0], arrived[1]
-    third_far = to_partner(first_far)
-    far = [first_far, second_far, third_far]
-
-    arrived = across(pair_up(after(residual, first_far), partner_residual))
+    near = [own, partner]
+    partner_residual = to_partner(after(residual, own))
+    arrived = across(pair_up(*near))
+    values, cell_rows, turned = prepare(2.0 / math.sqrt(cells), after(depth_band, partner), direction)
+    arrived = after(arrived, (values, partner_residual))
+    far = [arrived[0], arrived[1], to_partner(arrived[0])]
+
+    arrived = across(pair_up(residual, partner_residual))
     to_first, to_second, to_third = forward(*far_slots, far, values, turned)
     to_third, arrived = after((to_third, arrived), (arrived, to_third))
     far_residuals = [arrived[0], arrived[1], to_partner(arrived[0])]
     returned = to_partner(to_third)
     given = across(pair_up(to_first, to_second, returned))
-    (image,) = forward(*own_slot, [after(own, (far_residuals[2], returned))], values, turned)
+    image, to_return = forward(*near_slots, after(near, (far_residuals[2], returned)), values, turned)
     given = after(given, image)
     image = image + given[0] + to_partner(to_return + given[1])
 
-    partner_image = to_partner(image)
-    arrived = across(pair_up(image, partner_image))
-    (near_total,) = adjoint(
-        *near_slots, [own, partner], [residual, partner_residual], [image, partner_image], cell_rows
+    near_images = [image, to_partner(image)]
+    arrived = across(pair_up(*near_images))
+    near_total, sums = adjoint(
+        *near_slots, near, [residual, partner_residual], near_images, cell_rows, direction, old_grad
     )
     arrived = after(arrived, near_total)
     far_images = [arrived[0], arrived[1], to_partner(arrived[0])]
     constant, slope, stats = adjoint(
-        *far_slots, far, far_residuals, far_images, cell_rows,
-        (ranks, near_total, model_field, direction, sums, image),
+        *far_slots, far, far_residuals, far_images, cell_rows, near_total, sums, model_field, direction, image, ranks=ranks
     )
     stats = lax.all_to_all(stats, "tile", 0, 0)
     return finish(stats, constant, slope, model_field, direction, residual, image)

time: 98.5 us -> 81.4 us (0.83); the launches traced: 97 us -> 82 us
  Pallas kernels: 40 us -> 29.9 us
  starting transfers between devices: 27.9 us -> 22.4 us
  blocking collectives: 17.3 us -> 20.5 us
  local copies, waits for them, and re-layouts: 5.57 us -> 3.21 us
    pallas_call x4, Pallas kernels: 6.71 us -> 0.06 us  [pair_up(): pl.pallas_call(pair_kernel, out_shape=jax.ShapeDtypeStruct((2, *first.sha...]
    ppermute x8, starting transfers between devices: 25.2 us -> 19.7 us  [to_partner(): return lax.ppermute(array, 'tile', [(i, i ^ 1) for i in range(ranks)])]
    all_to_all x1, blocking collectives: 17.3 us -> 20.5 us  [shards(): stats = lax.all_to_all(stats, 'tile', 0, 0)]
    unnamed x32 -> x16, local copies, waits for them, and re-layouts: 5.52 us -> 3.17 us
    pallas_call x7 -> x6, Pallas kernels: 30.2 us -> 28.3 us  [the longest x2 14.9 us: adjoint(): pl.pallas_call(functools.partial(kernel, sizes), out_shape=tuple((jax.Sha...]
    pallas_call x1, Pallas kernels: 3.07 us -> 1.51 us  [prepare(): pl.pallas_call(functools.partial(prepare_kernel, scale), grid=(PARTS,), o...]
  transfers between devices with their start and end apart: 12 -> 12, of which waited for: 6 -> 6; matrix products, arithmetic and copies ran while one was open for 0% -> 0% of each run, Pallas kernels for 27% -> 25%
where the time goes in v2:
time: 81.4 us; the launch traced here: 82 us
  Pallas kernels  29.9 us (37%)
  starting transfers between devices  22.4 us (28%)
  blocking collectives  20.5 us (25%)
  waiting for transfers between devices  4.93 us (6%)
  local copies, waits for them, and re-layouts  3.21 us (4%)
  between operations  0.87 us (1%)
    all_to_all x1, blocking collectives, shards(): stats = lax.all_to_all(stats, 'tile', 0, 0)  20.5 us
    ppermute x8, starting transfers between devices, to_partner(): return lax.ppermute(array, 'tile', [(i, i ^ 1) for i in range(ranks)])  19.7 us
    pallas_call x2, Pallas kernels, adjoint(): pl.pallas_call(functools.partial(kernel, sizes), out_shape=tuple((jax.Sha...  14.9 us
    pallas_call x2, Pallas kernels, forward(): pl.pallas_call(functools.partial(forward_kernel, sizes), out_shape=(jax.S...  11.2 us
    ppermute x8, waiting for transfers between devices, to_partner(): return lax.ppermute(array, 'tile', [(i, i ^ 1) for i in range(ranks)])  4.92 us
    unnamed x16, local copies, waits for them, and re-layouts  3.17 us
    ppermute x4, starting transfers between devices, across(): return lax.ppermute(message, 'tile', ends + [(j, i) for i, j in ends])  2.68 us
    pallas_call x1, Pallas kernels, finish(): pl.pallas_call(finish_kernel, out_shape=tuple((jax.ShapeDtypeStruct(shape...  2.22 us
  transfers between devices with their start and end apart: 12, of which 6 were waited for; matrix products, arithmetic and copies ran while one was open for 0% of the time, Pallas kernels for 25%

profile of v2, /device:TPU:0, one launch (start us, length us, event | category | flops | bytes accessed | tf_op | source)
XLA Modules:
  0.0 82.0 jit_solution(18116086246803803703)
XLA Ops:
  0.6 0.7 copy-done.5
  1.4 0.7 copy-done.6
  2.1 0.5 collective-permute-start
  2.6 0.1 collective-permute-start.2
  2.7 0.8 collective-permute-done.refs_1_
  3.4 0.7 collective-permute-start.1
  4.1 0.1 fusion.2
  4.2 0.8 %copy-done.4 = s32[16384]{0:T(1024)S(1)} copy-done((s32[16384]{0:T(1024)S(1)}, s32[16384]{0:T(1024)}, u32[]{:S(2)}) %copy-start.4) | copy-done | bytes 65560
  5.0 1.5 %prepare.1 = (bf16[32,32,512]{2,1,0:T(8,128)(2,1)S(1)}, f32[2,16384]{1,0:T(2,128)S(1)}, f32[128,128]{1,0:T(8,128)S(1)}) custom-call(s32[128,128]{1,0:T(8,128)S(1)} %bitcast.24, s32[1,16384]{1,0:T(1,128)S(1)} %bitcast.25, f32[16,16384]{1,0:T(8,128)} %direction_ref.3), custom_call_target="tpu_custom_call" | custom-call | flops 2097152 | bytes 3145728 | tf_op jit(solution)/shard_map/prepare/pallas_call | solution.py:117
  6.6 4.3 %collective-permute-start.3 = (f32[40,128]{1,0:T(8,128)S(1)}, f32[40,128]{1,0:T(8,128)S(1)}, u32[]{:S(2)}, u32[]{:S(2)}) collective-permute-start(f32[40,128]{1,0:T(8,128)S(1)} %get-tuple-element.54.refs_0_), channel_id=1, source_target_pairs={{0,1},{1,0},{2,3},{3,2},{4,5},{5,4},{6,7},{7,6},{8,9},{9,8},{10,11... | collective-permute-start | bytes 61448 | tf_op jit(solution)/shard_map/ppermute | solution.py:543
  10.9 0.9 %copy-done.2 = f32[16,2048]{1,0:T(8,128)S(1)} copy-done((f32[16,2048]{1,0:T(8,128)S(1)}, f32[16,2048]{1,0:T(8,128)}, u32[]{:S(2)}) %copy-start.2) | copy-done | bytes 131096
  11.8 0.7 collective-permute-start.4
  12.5 5.0 %forward.2 = (f32[8,16,256]{2,1,0:T(8,128)S(1)}, f32[8,16,256]{2,1,0:T(8,128)S(1)}, f32[8,16,256]{2,1,0:T(8,128)S(1)}) custom-call(s32[3]{0:T(128)S(1)} %multiply_add_fusion.1.first_ref, f32[3]{0:T(128)S(1)} %get-tuple-element.47.shift_ref, f32[40,128]{1,0:T(8,128)S(1)} %get-tuple-element.54.refs_0_, f32[40,128]{1,0:T(8,128)S(1)} %get-tuple-element.53.refs_1_, ...), custom_call_target="tpu_custom_call" | custom-call | flops 11953766400 | bytes 1048576 | tf_op jit(solution)/shard_map/forward/pallas_call | solution.py:283
  17.5 4.7 %collective-permute-start.5 = (f32[16,2048]{1,0:T(8,128)S(1)}, f32[16,2048]{1,0:T(8,128)S(1)}, u32[]{:S(2)}, u32[]{:S(2)}) collective-permute-start(f32[16,2048]{1,0:T(8,128)S(1)} %get-tuple-element.52.refs_3_), channel_id=1, source_target_pairs={{0,1},{1,0},{2,3},{3,2},{4,5},{5,4},{6,7},{7,6},{8,9},{9,8},{10,11... | collective-permute-start | bytes 393224 | tf_op jit(solution)/shard_map/ppermute | solution.py:543
  22.2 0.1 collective-permute-start.6
  22.3 0.1 multiply_add_fusion
  22.4 0.8 %collective-permute-done.5.refs_5_ = f32[16,2048]{1,0:T(8,128)S(1)} collective-permute-done((f32[16,2048]{1,0:T(8,128)S(1)}, f32[16,2048]{1,0:T(8,128)S(1)}, u32[]{:S(2)}, u32[]{:S(2)}) %collective-permute-start.5) | collective-permute-done | bytes 131104 | tf_op jit(solution)/shard_map/ppermute | solution.py:543
  23.2 0.4 collective-permute-done.6.refs_2_
  23.6 0.7 collective-permute-start.7
  24.3 0.0 copy-start
  24.3 6.2 %forward.3 = (f32[8,16,256]{2,1,0:T(8,128)S(1)}, f32[8,16,256]{2,1,0:T(8,128)S(1)}) custom-call(s32[2]{0:T(128)S(1)} %get-tuple-element.55.first_ref, f32[2]{0:T(128)S(1)} %get-tuple-element.56.shift_ref, f32[40,128]{1,0:T(8,128)S(1)} %pack.1.refs_0_, f32[40,128]{1,0:T(8,128)S(1)} %collective-permute-done.refs_1_, ...), custom_call_target="tpu_custom_call" | custom-call | flops 7864320000 | bytes 1048576 | tf_op jit(solution)/shard_map/forward/pallas_call | solution.py:283
  30.6 5.7 %collective-permute-start.8 = (f32[8,16,256]{2,1,0:T(8,128)S(1)}, f32[8,16,256]{2,1,0:T(8,128)S(1)}, u32[]{:S(2)}, u32[]{:S(2)}) collective-permute-start(f32[8,16,256]{2,1,0:T(8,128)S(1)} %bitcast_add_fusion), channel_id=1, source_target_pairs={{0,1},{1,0},{2,3},{3,2},{4,5},{5,4},{6,7},{7,6},{8,9},{9,8},{10,11... | collective-permute-start | bytes 393224 | tf_op jit(solution)/shard_map/ppermute | solution.py:543
  36.2 1.0 %collective-permute-done.8 = f32[8,16,256]{2,1,0:T(8,128)S(1)} collective-permute-done((f32[8,16,256]{2,1,0:T(8,128)S(1)}, f32[8,16,256]{2,1,0:T(8,128)S(1)}, u32[]{:S(2)}, u32[]{:S(2)}) %collective-permute-start.8) | collective-permute-done | bytes 131104 | tf_op jit(solution)/shard_map/ppermute | solution.py:543
  37.2 0.4 collective-permute-start.9
  37.7 1.0 %collective-permute-done.9.refs_1_.refs_5_ = f32[8,16,256]{2,1,0:T(8,128)S(1)} collective-permute-done((f32[8,16,256]{2,1,0:T(8,128)S(1)}, f32[8,16,256]{2,1,0:T(8,128)S(1)}, u32[]{:S(2)}, u32[]{:S(2)}) %collective-permute-start.9) | collective-permute-done | bytes 131104 | tf_op jit(solution)/shard_map/ppermute | solution.py:543
  38.7 0.7 collective-permute-start.10
  39.4 7.8 %near.1 = (f32[32,32,512]{2,1,0:T(8,128)S(1)}, f32[2,128]{1,0:T(2,128)S(1)}) custom-call(s32[2]{0:T(128)S(1)} %get-tuple-element.55.first_ref, f32[2]{0:T(128)S(1)} %get-tuple-element.56.shift_ref, f32[40,128]{1,0:T(8,128)S(1)} %pack.1.refs_0_, f32[40,128]{1,0:T(8,128)S(1)} %collective-permute-done.refs_1_, f32[16,2048]{1,0:T(8,128)S(1)} %copy-done.3, ...), custom_call_target="tpu_custom_call" | custom-call | flops 7864320000 | bytes 1048576 | tf_op jit(solution)/shard_map/near/pallas_call | solution.py:461
  47.3 4.0 %collective-permute-start.11 = (f32[8,16,256]{2,1,0:T(8,128)S(1)}, f32[8,16,256]{2,1,0:T(8,128)S(1)}, u32[]{:S(2)}, u32[]{:S(2)}) collective-permute-start(f32[8,16,256]{2,1,0:T(8,128)S(1)} %get-tuple-element.50.refs_6_), channel_id=1, source_target_pairs={{0,1},{1,0},{2,3},{3,2},{4,5},{5,4},{6,7},{7,6},{8,9},{9,8},{10,11... | collective-permute-start | bytes 393224 | tf_op jit(solution)/shard_map/ppermute | solution.py:543
  51.2 1.0 %collective-permute-done.11.refs_8_ = f32[8,16,256]{2,1,0:T(8,128)S(1)} collective-permute-done((f32[8,16,256]{2,1,0:T(8,128)S(1)}, f32[8,16,256]{2,1,0:T(8,128)S(1)}, u32[]{:S(2)}, u32[]{:S(2)}) %collective-permute-start.11) | collective-permute-done | bytes 131104 | tf_op jit(solution)/shard_map/ppermute | solution.py:543
  52.2 7.1 %far.1 = (f32[16,16384]{1,0:T(8,128)S(1)}, f32[16,16384]{1,0:T(8,128)S(1)}, f32[16,1,128]{2,1,0:T(1,128)S(1)}) custom-call(s32[3]{0:T(128)S(1)} %multiply_add_fusion.1.first_ref, f32[3]{0:T(128)S(1)} %get-tuple-element.47.shift_ref, f32[40,128]{1,0:T(8,128)S(1)} %get-tuple-element.54.refs_0_, f32[40,128]{1,0:T(8,128)S(1)} %get-tuple-element.53.refs_1_, ...), custom_call_target="tpu_custom_call" | custom-call | flops 11953766400 | bytes 1048576 | tf_op jit(solution)/shard_map/far/pallas_call | solution.py:461
  59.3 20.5 %all_to_all.5.stats_ref = f32[16,1,128]{2,1,0:T(1,128)S(1)} all-to-all(f32[16,1,128]{2,1,0:T(1,128)S(1)} %get-tuple-element.44), channel_id=1, replica_groups=mesh['groups'=2,'tile'=16] {'tile'}, dimensions={0} | all-to-all | bytes 16384 | tf_op jit(solution)/shard_map/all_to_all | solution.py:585
  79.8 2.2 %finish.1 = (f32[16,16384]{1,0:T(8,128)}, f32[16,2048]{1,0:T(8,128)}, f32[16,16384]{1,0:T(8,128)}) custom-call(f32[16,1,128]{2,1,0:T(1,128)S(1)} %all_to_all.5.stats_ref, f32[16,16384]{1,0:T(8,128)S(1)} %get-tuple-element.45.constant_ref, f32[16,16384]{1,0:T(8,128)S(1)} %get-tuple-element.46.slope_ref, f32[16,16384]{1,0:T(8,128)S(1)} %copy-done.1, ...), custom_call_target="tpu_custom_call" | custom-call | tf_op jit(solution)/shard_map/finish/pallas_call | solution.py:518
  (28 shorter events, 0.2 us)
Async XLA Ops:
  0.6 0.7 copy-start.5
  1.3 0.7 copy-start.6
  2.1 1.4 %collective-permute-start = (f32[40,128]{1,0:T(8,128)S(1)}, f32[40,128]{1,0:T(8,128)S(1)}, u32[]{:S(2)}, u32[]{:S(2)}) collective-permute-start(f32[40,128]{1,0:T(8,128)S(1)} %pack.1.refs_0_), channel_id=1, source_target_pairs={{0,1},{1,0},{2,3},{3,2},{4,5},{5,4},{6,7},{7,6},{8,9},{9,8},{10,11... | collective-permute-start | bytes 61448 | tf_op jit(solution)/shard_map/ppermute | solution.py:543
  2.6 4.0 %collective-permute-start.2 = (f32[16,2048]{1,0:T(8,128)}, f32[16,2048]{1,0:T(8,128)S(1)}, u32[]{:S(2)}, u32[]{:S(2)}) collective-permute-start(f32[16,2048]{1,0:T(8,128)} %residual_ref.1), channel_id=1, source_target_pairs={{0,1},{1,0},{2,3},{3,2},{4,5},{5,4},{6,7},{7,6},{8,9},{9,8},{10,11... | collective-permute-start | bytes 393224 | tf_op jit(solution)/shard_map/ppermute | solution.py:543
  3.4 3.1 %collective-permute-start.1 = (f32[2,40,128]{2,1,0:T(8,128)S(1)}, f32[2,40,128]{2,1,0:T(8,128)S(1)}, u32[]{:S(2)}, u32[]{:S(2)}) collective-permute-start(f32[2,40,128]{2,1,0:T(8,128)S(1)} %pair.4), channel_id=1, source_target_pairs={{1,2},{3,4},{5,6},{7,8},{9,10},{11,12},{13,14},{2,1},{4,3},{6,5},{... | collective-permute-start | bytes 122888 | tf_op jit(solution)/shard_map/ppermute | solution.py:547
  4.2 0.8 %copy-start.4 = (s32[16384]{0:T(1024)S(1)}, s32[16384]{0:T(1024)}, u32[]{:S(2)}) copy-start(s32[16384]{0:T(1024)} %param.12) | copy-start | bytes 196612
  6.6 5.9 %collective-permute-start.3 = (f32[40,128]{1,0:T(8,128)S(1)}, f32[40,128]{1,0:T(8,128)S(1)}, u32[]{:S(2)}, u32[]{:S(2)}) collective-permute-start(f32[40,128]{1,0:T(8,128)S(1)} %get-tuple-element.54.refs_0_), channel_id=1, source_target_pairs={{0,1},{1,0},{2,3},{3,2},{4,5},{5,4},{6,7},{7,6},{8,9},{9,8},{10,11... | collective-permute-start | bytes 61448 | tf_op jit(solution)/shard_map/ppermute | solution.py:543
  10.8 0.9 %copy-start.2 = (f32[16,2048]{1,0:T(8,128)S(1)}, f32[16,2048]{1,0:T(8,128)}, u32[]{:S(2)}) copy-start(f32[16,2048]{1,0:T(8,128)} %residual_ref.1) | copy-start | bytes 393220
  11.8 5.7 %collective-permute-start.4 = (f32[2,16,2048]{2,1,0:T(8,128)S(1)}, f32[2,16,2048]{2,1,0:T(8,128)S(1)}, u32[]{:S(2)}, u32[]{:S(2)}) collective-permute-start(f32[2,16,2048]{2,1,0:T(8,128)S(1)} %pair.5), channel_id=1, source_target_pairs={{1,2},{3,4},{5,6},{7,8},{9,10},{11,12},{13,14},{2,1},{4,3},{6,5},{... | collective-permute-start | bytes 786440 | tf_op jit(solution)/shard_map/ppermute | solution.py:547
  17.5 5.7 %collective-permute-start.5 = (f32[16,2048]{1,0:T(8,128)S(1)}, f32[16,2048]{1,0:T(8,128)S(1)}, u32[]{:S(2)}, u32[]{:S(2)}) collective-permute-start(f32[16,2048]{1,0:T(8,128)S(1)} %get-tuple-element.52.refs_3_), channel_id=1, source_target_pairs={{0,1},{1,0},{2,3},{3,2},{4,5},{5,4},{6,7},{7,6},{8,9},{9,8},{10,11... | collective-permute-start | bytes 393224 | tf_op jit(solution)/shard_map/ppermute | solution.py:543
  22.2 1.3 %collective-permute-start.6 = (f32[8,16,256]{2,1,0:T(8,128)S(1)}, f32[8,16,256]{2,1,0:T(8,128)S(1)}, u32[]{:S(2)}, u32[]{:S(2)}) collective-permute-start(f32[8,16,256]{2,1,0:T(8,128)S(1)} %get-tuple-element.32), channel_id=1, source_target_pairs={{0,1},{1,0},{2,3},{3,2},{4,5},{5,4},{6,7},{7,6},{8,9},{9,8},{10,11... | collective-permute-start | bytes 393224 | tf_op jit(solution)/shard_map/ppermute | solution.py:543
  23.6 6.9 %collective-permute-start.7 = (f32[2,8,16,256]{3,2,1,0:T(8,128)S(1)}, f32[2,8,16,256]{3,2,1,0:T(8,128)S(1)}, u32[]{:S(2)}, u32[]{:S(2)}) collective-permute-start(f32[2,8,16,256]{3,2,1,0:T(8,128)S(1)} %pair.6), channel_id=1, source_target_pairs={{1,2},{3,4},{5,6},{7,8},{9,10},{11,12},{13,14},{2,1},{4,3},{6,5},{... | collective-permute-start | bytes 786440 | tf_op jit(solution)/shard_map/ppermute | solution.py:547
  24.3 15.1 %copy-start = (f32[16,16384]{1,0:T(8,128)S(1)}, f32[16,16384]{1,0:T(8,128)}, u32[]{:S(2)}) copy-start(f32[16,16384]{1,0:T(8,128)} %direction_ref.3) | copy-start | bytes 3145732
  24.3 15.1 %copy-start.3 = (f32[16,2048]{1,0:T(8,128)S(1)}, f32[16,2048]{1,0:T(8,128)}, u32[]{:S(2)}) copy-start(f32[16,2048]{1,0:T(8,128)} %residual_ref.1) | copy-start | bytes 393220
  24.3 15.1 %copy-start.7 = (f32[16,16384]{1,0:T(8,128)S(1)}, f32[16,16384]{1,0:T(8,128)}, u32[]{:S(2)}) copy-start(f32[16,16384]{1,0:T(8,128)} %refs_8_.1) | copy-start | bytes 3145732
  30.6 6.6 %collective-permute-start.8 = (f32[8,16,256]{2,1,0:T(8,128)S(1)}, f32[8,16,256]{2,1,0:T(8,128)S(1)}, u32[]{:S(2)}, u32[]{:S(2)}) collective-permute-start(f32[8,16,256]{2,1,0:T(8,128)S(1)} %bitcast_add_fusion), channel_id=1, source_target_pairs={{0,1},{1,0},{2,3},{3,2},{4,5},{5,4},{6,7},{7,6},{8,9},{9,8},{10,11... | collective-permute-start | bytes 393224 | tf_op jit(solution)/shard_map/ppermute | solution.py:543
  37.2 1.4 %collective-permute-start.9 = (f32[8,16,256]{2,1,0:T(8,128)S(1)}, f32[8,16,256]{2,1,0:T(8,128)S(1)}, u32[]{:S(2)}, u32[]{:S(2)}) collective-permute-start(f32[8,16,256]{2,1,0:T(8,128)S(1)} %fusion.refs_0_.refs_4_.refs_14_.image_ref), channel_id=1, source_target_pairs={{0,1},{1,0},{2,3},{3,2},{4,5},{5,4},{6,7},{7,6},{8,9},{9,8},{10,11... | collective-permute-start | bytes 393224 | tf_op jit(solution)/shard_map/ppermute | solution.py:543
  38.7 8.5 %collective-permute-start.10 = (f32[2,8,16,256]{3,2,1,0:T(8,128)S(1)}, f32[2,8,16,256]{3,2,1,0:T(8,128)S(1)}, u32[]{:S(2)}, u32[]{:S(2)}) collective-permute-start(f32[2,8,16,256]{3,2,1,0:T(8,128)S(1)} %pair.7), channel_id=1, source_target_pairs={{1,2},{3,4},{5,6},{7,8},{9,10},{11,12},{13,14},{2,1},{4,3},{6,5},{... | collective-permute-start | bytes 786440 | tf_op jit(solution)/shard_map/ppermute | solution.py:547
  39.4 12.8 %copy-start.1 = (f32[16,16384]{1,0:T(8,128)S(1)}, f32[16,16384]{1,0:T(8,128)}, u32[]{:S(2)}) copy-start(f32[16,16384]{1,0:T(8,128)} %model_ref.1) | copy-start | bytes 3145732
  47.3 5.0 %collective-permute-start.11 = (f32[8,16,256]{2,1,0:T(8,128)S(1)}, f32[8,16,256]{2,1,0:T(8,128)S(1)}, u32[]{:S(2)}, u32[]{:S(2)}) collective-permute-start(f32[8,16,256]{2,1,0:T(8,128)S(1)} %get-tuple-element.50.refs_6_), channel_id=1, source_target_pairs={{0,1},{1,0},{2,3},{3,2},{4,5},{5,4},{6,7},{7,6},{8,9},{9,8},{10,11... | collective-permute-start | bytes 393224 | tf_op jit(solution)/shard_map/ppermute | solution.py:543

commit v3 on v2

--- a/solution.py
+++ b/solution.py
@@ -41,47 +41,87 @@
     return jnp.dot(left, right, preferred_element_type=F32)
 
 
-def pack_kernel(offsets_ref, pairs_ref, message_ref):
+def pack_kernel(offsets_any, pairs_any, residual_any, message_ref, residual_ref, offsets_ref, pairs_ref, sent):
+    copies = [
+        pltpu.make_async_copy(offsets_any, offsets_ref, sent.at[0]),
+        pltpu.make_async_copy(pairs_any, pairs_ref, sent.at[1]),
+        pltpu.make_async_copy(residual_any, residual_ref, sent.at[2]),
+    ]
+    for copy in copies:
+        copy.start()
     lines = offsets_ref.shape[1] // LANES
-    message_ref[...] = jnp.zeros_like(message_ref)
+    rows, pairs = pairs_ref.shape
+    message_ref[pl.ds(2 * lines, rows), :] = jnp.zeros((rows, LANES), F32)
+    for copy in copies:
+        copy.wait()
     for i in range(lines):
         at = pl.ds(i * LANES, LANES)
         message_ref[pl.ds(i, 1), :] = offsets_ref[pl.ds(0, 1), at]
         message_ref[pl.ds(lines + i, 1), :] = offsets_ref[pl.ds(1, 1), at]
-    rows, pairs = pairs_ref.shape
     message_ref[pl.ds(2 * lines, rows), pl.ds(0, pairs)] = pairs_ref[...].astype(F32) + 1.0
 
 
-def pack(station_offsets, block_pairs):
+def in_hbm(array):
+    return pltpu.with_memory_space_constraint(array, pltpu.HBM)
+
+
+def pack(station_offsets, block_pairs, residual):
     rows = 2 * station_offsets.shape[1] // LANES + block_pairs.shape[0]
     return pl.pallas_call(
         pack_kernel,
-        out_shape=jax.ShapeDtypeStruct((rows, LANES), F32),
-        in_specs=[VMEM] * 2,
+        out_shape=(jax.ShapeDtypeStruct((rows, LANES), F32), jax.ShapeDtypeStruct(residual.shape, F32)),
+        in_specs=[pl.BlockSpec(memory_space=pl.ANY)] * 3,
+        out_specs=(VMEM, VMEM),
+        scratch_shapes=[
+            pltpu.VMEM(station_offsets.shape, F32),
+            pltpu.VMEM(block_pairs.shape, jnp.int32),
+            pltpu.SemaphoreType.DMA((3,)),
+        ],
+        compiler_params=params(2),
+        name="pack",
+    )(in_hbm(station_offsets), in_hbm(block_pairs), in_hbm(residual))
+
+
+def far_parts_kernel(parts_ref, third_ref, message_ref):
+    message_ref[0] = parts_ref[0] + third_ref[...]
+    message_ref[1] = parts_ref[1]
+
+
+def far_parts(parts, third):
+    return small_call(far_parts_kernel, (2, *third.shape), "far_parts", parts, third)
+
+
+def both_images_kernel(mine_ref, theirs_ref, images_ref):
+    images_ref[0] = mine_ref[0] + theirs_ref[1]
+    images_ref[1] = mine_ref[1] + theirs_ref[0]
+
+
+def both_images(mine, theirs):
+    return small_call(both_images_kernel, mine.shape, "both_images", mine, theirs)
+
+
+def add_kernel(left_ref, right_ref, sum_ref):
+    sum_ref[...] = left_ref[...] + right_ref[...]
+
+
+def pair_kernel(first_ref, second_ref, message_ref):
+    message_ref[0] = first_ref[...]
+    message_ref[1] = second_ref[...]
+
+
+def pair_up(first, second):
+    return small_call(pair_kernel, (2, *first.shape), "pair", first, second)
+
+
+def small_call(kernel, shape, name, *arrays):
+    return pl.pallas_call(
+        kernel,
+        out_shape=jax.ShapeDtypeStruct(shape, F32),
+        in_specs=[VMEM] * len(arrays),
         out_specs=VMEM,
         compiler_params=params(2),
-        name="pack",
-    )(station_offsets, block_pairs)
-
-
-def pair_kernel(*refs):
-    first_ref, second_ref, *added_refs, message_ref = refs
-    first = first_ref[...]
-    for added_ref in added_refs:
-        first = first + added_ref[...]
-    message_ref[0] = first
-    message_ref[1] = second_ref[...]
-
-
-def pair_up(first, second, *added):
-    return pl.pallas_call(
-        pair_kernel,
-        out_shape=jax.ShapeDtypeStruct((2, *first.shape), F32),
-        in_specs=[VMEM] * (2 + len(added)),
-        out_specs=VMEM,
-        compiler_params=params(2),
-        name="pair",
-    )(first, second, *added)
+        name=name,
+    )(*arrays)
 
 
 def prepare_kernel(scale, band_ref, band_row_ref, direction_ref, values_ref, cells_ref, turned_ref):
@@ -123,7 +163,7 @@
             jax.ShapeDtypeStruct((cells // LANES, LANES), F32),
         ),
         in_specs=[
-            VMEM,
+            pl.BlockSpec((cells // LANES, LANES), lambda i: (0, 0)),
             pl.BlockSpec((1, cells // PARTS), lambda i: (0, i)),
             pl.BlockSpec((epochs, cells // PARTS), lambda i: (0, i)),
         ],
@@ -136,9 +176,9 @@
         cost_estimate=pl.CostEstimate(flops=8 * epochs * cells, bytes_accessed=12 * epochs * cells, transcendentals=0),
         name="prepare",
     )(
-        depth_band.reshape(cells // LANES, LANES),
-        depth_band.reshape(1, cells),
-        pltpu.with_memory_space_constraint(direction, pltpu.HBM),
+        in_hbm(depth_band.reshape(cells // LANES, LANES)),
+        in_hbm(depth_band.reshape(1, cells)),
+        in_hbm(direction),
     )
 
 
@@ -219,8 +259,7 @@
     cell_blocks, station_blocks, pairs, epochs, slots = sizes
     messages = refs[:slots]
     values_ref, turned_ref = refs[slots : slots + 2]
-    images = refs[slots + 2 : 2 * slots + 2]
-    list_ref, codes_ref, scalars_ref, sent, *scratch = refs[2 * slots + 2 :]
+    images_ref, list_ref, codes_ref, scalars_ref, sent, *scratch = refs[slots + 2 :]
     across_ref, along_ref, image_ref, gaps_ref, lines_ref, depths_ref = scratch
     copy = send_codes(sizes, first_ref, messages, codes_ref, scalars_ref, sent)
     dummy = slots * station_blocks
@@ -274,7 +313,7 @@
 
     pl.run_scoped(run, *accumulators(2 * epochs))
     for slot in range(slots):
-        images[slot][...] = image_ref[pl.ds(slot * station_blocks, station_blocks)]
+        images_ref[slot] = image_ref[pl.ds(slot * station_blocks, station_blocks)]
 
 
 def forward(sizes, first, shift, messages, values, turned):
@@ -282,9 +321,9 @@
     rows = (slots * station_blocks + 8) // 8 * 8
     return pl.pallas_call(
         functools.partial(forward_kernel, sizes),
-        out_shape=(jax.ShapeDtypeStruct((station_blocks, epochs, SBLOCK), F32),) * slots,
+        out_shape=jax.ShapeDtypeStruct((slots, station_blocks, epochs, SBLOCK), F32),
         in_specs=[SMEM, SMEM] + [VMEM] * (slots + 2),
-        out_specs=(VMEM,) * slots,
+        out_specs=VMEM,
         scratch_shapes=list_scratch(sizes)
         + [
             pltpu.VMEM((rows, SBLOCK), F32),
@@ -295,15 +334,15 @@
             pltpu.VMEM((2, CBLOCK, LANES), F32),
         ],
         compiler_params=params(),
-        cost_estimate=estimate(sizes),
+        cost_estimate=estimate(sizes, 0.1 if slots > 2 else 1),
         name="forward",
     )(first, shift, *messages, values, turned)
 
 
-def estimate(sizes):
+def estimate(sizes, part=1):
     cell_blocks, station_blocks, pairs, epochs, slots = sizes
     entries = station_blocks * pairs * slots // (2 * REACH + 1) * SBLOCK * CBLOCK
-    return pl.CostEstimate(flops=2 * 1200 * entries, bytes_accessed=2**20, transcendentals=entries)
+    return pl.CostEstimate(flops=int(2 * 1200 * entries * part), bytes_accessed=2**20, transcendentals=entries)
 
 
 def adjoint_sums(sizes, first_ref, shift_ref, messages, residuals, images, cells_ref, total_ref, scratch):
@@ -377,10 +416,17 @@
     pl.run_scoped(run, *accumulators(4 * epochs))
 
 
+def slot_refs(slots, refs):
+    messages, refs = refs[:slots], refs[slots:]
+    arrays = slots - 1
+    residuals, images, rest = refs[:arrays], refs[arrays : 2 * arrays], refs[2 * arrays :]
+    return messages, *([pair.at[0], pair.at[1], *single] for pair, *single in (residuals, images)), rest
+
+
 def near_kernel(sizes, first_ref, shift_ref, *refs):
     cell_blocks, station_blocks, pairs, epochs, slots = sizes
-    messages, residuals, images = (refs[i * slots : (i + 1) * slots] for i in range(3))
-    cells_ref, direction_ref, old_ref, total_ref, sums_ref, *scratch = refs[3 * slots :]
+    messages, residuals, images, rest = slot_refs(slots, refs)
+    cells_ref, direction_ref, old_ref, total_ref, sums_ref, *scratch = rest
     adjoint_sums(sizes, first_ref, shift_ref, messages, residuals, images, cells_ref, total_ref, scratch)
 
     def add(w, sums):
@@ -395,8 +441,7 @@
 
 def far_kernel(sizes, first_ref, shift_ref, *refs):
     cell_blocks, station_blocks, pairs, epochs, slots = sizes
-    messages, residuals, images = (refs[i * slots : (i + 1) * slots] for i in range(3))
-    rest = refs[3 * slots :]
+    messages, residuals, images, rest = slot_refs(slots, refs)
     cells_ref, near_ref, sums_ref, model_ref, direction_ref, image_ref = rest[:6]
     constant_ref, slope_ref, stats_ref = rest[6:9]
     total_ref, *scratch = rest[9:]
@@ -424,7 +469,7 @@
         return sums[0] + left * left, sums[1] + left * slope
 
     left_square, left_cross = lax.fori_loop(0, cell_blocks, remainder, (zero, zero), unroll=2)
-    image = image_ref[...]
+    image = image_ref[0]
     stats = [
         sums_ref[pl.ds(0, 1), pl.ds(0, 1)],
         sums_ref[pl.ds(1, 1), pl.ds(0, 1)],
@@ -461,7 +506,7 @@
     return pl.pallas_call(
         functools.partial(kernel, sizes),
         out_shape=tuple(jax.ShapeDtypeStruct(shape, F32) for shape in shapes),
-        in_specs=[SMEM, SMEM] + [VMEM] * (3 * slots + 1 + len(others)),
+        in_specs=[SMEM, SMEM] + [VMEM] * (3 * slots - 1 + len(others)),
         out_specs=(VMEM,) * len(shapes),
         scratch_shapes=scratch,
         compiler_params=params(),
@@ -489,9 +534,9 @@
         copies.append(pltpu.make_async_copy(source.at[:, at], target.at[:, at], sent.at[i]))
         copies[-1].start()
 
-    for q in range(image_ref.shape[0]):
+    for q in range(image_ref.shape[1]):
         at = pl.ds(q * SBLOCK, SBLOCK)
-        new_residual[:, at] = residual_ref[:, at] - step * image_ref[q]
+        new_residual[:, at] = residual_ref[:, at] - step * image_ref[0, q]
     send(0, new_residual, residual_out, pl.ds(0, residual_ref.shape[1]))
     cells = model_ref.shape[1] // FINISH_PARTS
     for part in range(FINISH_PARTS):
@@ -553,37 +598,37 @@
 
     near_slots, far_slots = slots(0, -1), slots(1, 2, -2)
 
-    own = pack(station_offsets, block_pairs)
+    own, residual = pack(station_offsets, block_pairs, residual)
     partner = to_partner(own)
     near = [own, partner]
-    partner_residual = to_partner(after(residual, own))
+    partner_residual = to_partner(residual)
     arrived = across(pair_up(*near))
     values, cell_rows, turned = prepare(2.0 / math.sqrt(cells), after(depth_band, partner), direction)
-    arrived = after(arrived, (values, partner_residual))
+    residuals = pair_up(residual, partner_residual)
+    arrived = after(arrived, (values, residuals))
     far = [arrived[0], arrived[1], to_partner(arrived[0])]
 
-    arrived = across(pair_up(residual, partner_residual))
-    to_first, to_second, to_third = forward(*far_slots, far, values, turned)
-    to_third, arrived = after((to_third, arrived), (arrived, to_third))
-    far_residuals = [arrived[0], arrived[1], to_partner(arrived[0])]
-    returned = to_partner(to_third)
-    given = across(pair_up(to_first, to_second, returned))
-    image, to_return = forward(*near_slots, after(near, (far_residuals[2], returned)), values, turned)
-    given = after(given, image)
-    image = image + given[0] + to_partner(to_return + given[1])
-
-    near_images = [image, to_partner(image)]
-    arrived = across(pair_up(*near_images))
-    near_total, sums = adjoint(
-        *near_slots, near, [residual, partner_residual], near_images, cell_rows, direction, old_grad
-    )
-    arrived = after(arrived, near_total)
-    far_images = [arrived[0], arrived[1], to_partner(arrived[0])]
+    far_residuals = across(residuals)
+    parts = forward(*far_slots, far, values, turned)
+    parts, far_residuals = after((parts, far_residuals), (far_residuals, parts))
+    returned = to_partner(parts[2])
+    given = across(far_parts(parts, returned))
+    mine = forward(*near_slots, after(near, returned), values, turned)
+    given = after(given, mine)
+    mine = small_call(add_kernel, mine.shape, "add", mine, given)
+    images = both_images(mine, to_partner(mine))
+
+    far_images = across(images)
+    third_residual = to_partner(after(far_residuals[0], images))
+    near_total, sums = adjoint(*near_slots, near, [residuals], [images], cell_rows, direction, old_grad)
+    far_images, third_residual = after((far_images, third_residual), near_total)
+    third_image = to_partner(far_images[0])
     constant, slope, stats = adjoint(
-        *far_slots, far, far_residuals, far_images, cell_rows, near_total, sums, model_field, direction, image, ranks=ranks
+        *far_slots, far, [far_residuals, third_residual], [far_images, third_image], cell_rows,
+        near_total, sums, model_field, direction, images, ranks=ranks,
     )
     stats = lax.all_to_all(stats, "tile", 0, 0)
-    return finish(stats, constant, slope, model_field, direction, residual, image)
+    return finish(stats, constant, slope, model_field, direction, residual, images)
 
 
 def solution(mesh):

time: 81.4 us -> 78.8 us (0.968)
  the two profiles are of different devices: /device:TPU:0 before, /device:TPU:2 now
where the time goes in v3:
time: 78.8 us
  Pallas kernels  34.2 us (43%)
  starting transfers between devices  19.6 us (25%)
  blocking collectives  19 us (24%)
  waiting for transfers between devices  4.93 us (6%)
  between operations  0.85 us (1%)
    all_to_all x1, blocking collectives, shards(): stats = lax.all_to_all(stats, 'tile', 0, 0)  19 us
    ppermute x7, starting transfers between devices, to_partner(): return lax.ppermute(array, 'tile', [(i, i ^ 1) for i in range(ranks)])  16.9 us
    pallas_call x2, Pallas kernels, adjoint(): pl.pallas_call(functools.partial(kernel, sizes), out_shape=tuple((jax.Sha...  16.7 us
    pallas_call x2, Pallas kernels, forward(): pl.pallas_call(functools.partial(forward_kernel, sizes), out_shape=jax.Sh...  12.6 us
    ppermute x7, waiting for transfers between devices, to_partner(): return lax.ppermute(array, 'tile', [(i, i ^ 1) for i in range(ranks)])  4.92 us
    ppermute x4, starting transfers between devices, across(): return lax.ppermute(message, 'tile', ends + [(j, i) for i, j in ends])  2.68 us
    pallas_call x1, Pallas kernels, finish(): pl.pallas_call(finish_kernel, out_shape=tuple((jax.ShapeDtypeStruct(shape...  2.22 us
  transfers between devices with their start and end apart: 11, of which 5 were waited for; matrix products, arithmetic and copies ran while one was open for 0% of the time, Pallas kernels for 30%

profile of v3, /device:TPU:2, one launch (start us, length us, event | category | flops | bytes accessed | tf_op | source)
XLA Modules:
  0.0 78.8 jit_solution(6291052679081831747)
XLA Ops:
  0.6 1.0 %pack.1 = (f32[40,128]{1,0:T(8,128)S(1)}, f32[16,2048]{1,0:T(8,128)S(1)}) custom-call(f32[2,2048]{1,0:T(2,128)} %offsets_any.1, s32[8,8]{1,0:T(8,128)} %pairs_any.1, f32[16,2048]{1,0:T(8,128)} %residual_any.1), custom_call_target="tpu_custom_call" | custom-call | tf_op jit(solution)/shard_map/pack/pallas_call | solution.py:70
  1.6 0.1 collective-permute-start
  1.7 0.5 collective-permute-start.2
  2.2 0.7 collective-permute-done.second_ref.refs_1_
  2.9 0.7 collective-permute-start.1
  3.5 0.1 fusion.1
  3.6 1.5 %prepare.1 = (bf16[32,32,512]{2,1,0:T(8,128)(2,1)S(1)}, f32[2,16384]{1,0:T(2,128)S(1)}, f32[128,128]{1,0:T(8,128)S(1)}) custom-call(s32[128,128]{1,0:T(8,128)} %bitcast.16, s32[1,16384]{1,0:T(1,128)} %bitcast.17, f32[16,16384]{1,0:T(8,128)} %direction_ref.3), custom_call_target="tpu_custom_call" | custom-call | flops 2097152 | bytes 3145728 | tf_op jit(solution)/shard_map/prepare/pallas_call | solution.py:157
  5.2 0.0 collective-permute-done.2.second_ref
  5.2 0.7 collective-permute-start.4
  5.9 0.0 collective-permute-done.1
  5.9 4.5 %collective-permute-start.3 = (f32[40,128]{1,0:T(8,128)S(1)}, f32[40,128]{1,0:T(8,128)S(1)}, u32[]{:S(2)}, u32[]{:S(2)}) collective-permute-start(f32[40,128]{1,0:T(8,128)S(1)} %get-tuple-element.46.refs_0_), channel_id=1, source_target_pairs={{0,1},{1,0},{2,3},{3,2},{4,5},{5,4},{6,7},{7,6},{8,9},{9,8},{10,11... | collective-permute-start | bytes 61448 | tf_op jit(solution)/shard_map/ppermute | solution.py:588
  10.4 0.8 %collective-permute-done.3.refs_2_ = f32[40,128]{1,0:T(8,128)S(1)} collective-permute-done((f32[40,128]{1,0:T(8,128)S(1)}, f32[40,128]{1,0:T(8,128)S(1)}, u32[]{:S(2)}, u32[]{:S(2)}) %collective-permute-start.3) | collective-permute-done | bytes 20512 | tf_op jit(solution)/shard_map/ppermute | solution.py:588
  11.2 5.0 %forward.2.parts_ref = f32[3,8,16,256]{3,2,1,0:T(8,128)S(1)} custom-call(s32[3]{0:T(128)S(1)} %multiply_add_fusion.1.first_ref, f32[3]{0:T(128)S(1)} %get-tuple-element.43.shift_ref, f32[40,128]{1,0:T(8,128)S(1)} %get-tuple-element.46.refs_0_, f32[40,128]{1,0:T(8,128)S(1)} %get-tuple-element.45.refs_1_, f32[40,128]{1,0:T(8,128)S(1)} %collective-permute-done.3.refs_2_, ...), custom_call_target="tpu_custom_call" | custom-call | flops 1195376640 | bytes 1048576 | tf_op jit(solution)/shard_map/forward/pallas_call | solution.py:322
  16.2 0.0 collective-permute-done.4.refs_3_
  16.2 1.1 %collective-permute-start.5 = (f32[8,16,256]{2,1,0:T(8,128)S(1)}, f32[8,16,256]{2,1,0:T(8,128)S(1)}, u32[]{:S(2)}, u32[]{:S(2)}) collective-permute-start(f32[8,16,256]{2,1,0:T(8,128)S(1)} %slice_bitcast_fusion.2), channel_id=1, source_target_pairs={{0,1},{1,0},{2,3},{3,2},{4,5},{5,4},{6,7},{7,6},{8,9},{9,8},{10,11... | collective-permute-start | bytes 393224 | tf_op jit(solution)/shard_map/ppermute | solution.py:588
  17.4 0.1 multiply_add_fusion
  17.4 0.9 %collective-permute-done.5.third_ref = f32[8,16,256]{2,1,0:T(8,128)S(1)} collective-permute-done((f32[8,16,256]{2,1,0:T(8,128)S(1)}, f32[8,16,256]{2,1,0:T(8,128)S(1)}, u32[]{:S(2)}, u32[]{:S(2)}) %collective-permute-start.5) | collective-permute-done | bytes 131104 | tf_op jit(solution)/shard_map/ppermute | solution.py:588
  18.4 0.7 collective-permute-start.6
  19.1 0.0 copy-start
  19.1 0.0 copy-start.2
  19.1 7.6 %forward.3.left_ref = f32[2,8,16,256]{3,2,1,0:T(8,128)S(1)} custom-call(s32[2]{0:T(128)S(1)} %get-tuple-element.47.first_ref, f32[2]{0:T(128)S(1)} %get-tuple-element.48.shift_ref, f32[40,128]{1,0:T(8,128)S(1)} %get-tuple-element.31.first_ref.refs_0_, f32[40,128]{1,0:T(8,128)S(1)} %collective-permute-done.second_ref.refs_1_, ...), custom_call_target="tpu_custom_call" | custom-call | flops 7864320000 | bytes 1048576 | tf_op jit(solution)/shard_map/forward/pallas_call | solution.py:322
  26.7 0.0 collective-permute-done.6.right_ref
  26.8 6.5 %collective-permute-start.7 = (f32[2,8,16,256]{3,2,1,0:T(8,128)S(1)}, f32[2,8,16,256]{3,2,1,0:T(8,128)S(1)}, u32[]{:S(2)}, u32[]{:S(2)}) collective-permute-start(f32[2,8,16,256]{3,2,1,0:T(8,128)S(1)} %add.29.mine_ref), channel_id=1, source_target_pairs={{0,1},{1,0},{2,3},{3,2},{4,5},{5,4},{6,7},{7,6},{8,9},{9,8},{10,11... | collective-permute-start | bytes 786440 | tf_op jit(solution)/shard_map/ppermute | solution.py:588
  33.3 1.1 %collective-permute-done.7.theirs_ref = f32[2,8,16,256]{3,2,1,0:T(8,128)S(1)} collective-permute-done((f32[2,8,16,256]{3,2,1,0:T(8,128)S(1)}, f32[2,8,16,256]{3,2,1,0:T(8,128)S(1)}, u32[]{:S(2)}, u32[]{:S(2)}) %collective-permute-start.7) | collective-permute-done | bytes 262176 | tf_op jit(solution)/shard_map/ppermute | solution.py:588
  34.5 0.7 collective-permute-start.8
  35.2 4.2 %collective-permute-start.9 = (f32[16,2048]{1,0:T(8,128)S(1)}, f32[16,2048]{1,0:T(8,128)S(1)}, u32[]{:S(2)}, u32[]{:S(2)}) collective-permute-start(f32[16,2048]{1,0:T(8,128)S(1)} %slice_bitcast_fusion.1), channel_id=1, source_target_pairs={{0,1},{1,0},{2,3},{3,2},{4,5},{5,4},{6,7},{7,6},{8,9},{9,8},{10,11... | collective-permute-start | bytes 393224 | tf_op jit(solution)/shard_map/ppermute | solution.py:588
  39.4 9.6 %near.1 = (f32[32,32,512]{2,1,0:T(8,128)S(1)}, f32[2,128]{1,0:T(2,128)S(1)}) custom-call(s32[2]{0:T(128)S(1)} %get-tuple-element.47.first_ref, f32[2]{0:T(128)S(1)} %get-tuple-element.48.shift_ref, f32[40,128]{1,0:T(8,128)S(1)} %get-tuple-element.31.first_ref.refs_0_, f32[40,128]{1,0:T(8,128)S(1)} %collective-permute-done.second_ref.refs_1_, ...), custom_call_target="tpu_custom_call" | custom-call | flops 7864320000 | bytes 1048576 | tf_op jit(solution)/shard_map/near/pallas_call | solution.py:506
  49.0 0.1 collective-permute-start.10
  49.1 1.3 %collective-permute-done.10.refs_6_ = f32[8,16,256]{2,1,0:T(8,128)S(1)} collective-permute-done((f32[8,16,256]{2,1,0:T(8,128)S(1)}, f32[8,16,256]{2,1,0:T(8,128)S(1)}, u32[]{:S(2)}, u32[]{:S(2)}) %collective-permute-start.10) | collective-permute-done | bytes 131104 | tf_op jit(solution)/shard_map/ppermute | solution.py:588
  50.5 7.1 %far.1 = (f32[16,16384]{1,0:T(8,128)S(1)}, f32[16,16384]{1,0:T(8,128)S(1)}, f32[16,1,128]{2,1,0:T(1,128)S(1)}) custom-call(s32[3]{0:T(128)S(1)} %multiply_add_fusion.1.first_ref, f32[3]{0:T(128)S(1)} %get-tuple-element.43.shift_ref, f32[40,128]{1,0:T(8,128)S(1)} %get-tuple-element.46.refs_0_, f32[40,128]{1,0:T(8,128)S(1)} %get-tuple-element.45.refs_1_, ...), custom_call_target="tpu_custom_call" | custom-call | flops 11953766400 | bytes 1048576 | tf_op jit(solution)/shard_map/far/pallas_call | solution.py:506
  57.6 19.0 %all_to_all.5.stats_ref = f32[16,1,128]{2,1,0:T(1,128)S(1)} all-to-all(f32[16,1,128]{2,1,0:T(1,128)S(1)} %get-tuple-element.40), channel_id=1, replica_groups=mesh['groups'=2,'tile'=16] {'tile'}, dimensions={0} | all-to-all | bytes 16384 | tf_op jit(solution)/shard_map/all_to_all | solution.py:630
  76.5 2.2 %finish.1 = (f32[16,16384]{1,0:T(8,128)}, f32[16,2048]{1,0:T(8,128)}, f32[16,16384]{1,0:T(8,128)}) custom-call(f32[16,1,128]{2,1,0:T(1,128)S(1)} %all_to_all.5.stats_ref, f32[16,16384]{1,0:T(8,128)S(1)} %get-tuple-element.41.constant_ref, f32[16,16384]{1,0:T(8,128)S(1)} %get-tuple-element.42.slope_ref, f32[16,16384]{1,0:T(8,128)S(1)} %copy-done.1, ...), custom_call_target="tpu_custom_call" | custom-call | tf_op jit(solution)/shard_map/finish/pallas_call | solution.py:563
  (16 shorter events, 0.2 us)
Async XLA Ops:
  1.6 1.3 %collective-permute-start = (f32[40,128]{1,0:T(8,128)S(1)}, f32[40,128]{1,0:T(8,128)S(1)}, u32[]{:S(2)}, u32[]{:S(2)}) collective-permute-start(f32[40,128]{1,0:T(8,128)S(1)} %get-tuple-element.31.first_ref.refs_0_), channel_id=1, source_target_pairs={{0,1},{1,0},{2,3},{3,2},{4,5},{5,4},{6,7},{7,6},{8,9},{9,8},{10,11... | collective-permute-start | bytes 61448 | tf_op jit(solution)/shard_map/ppermute | solution.py:588
  1.7 3.5 %collective-permute-start.2 = (f32[16,2048]{1,0:T(8,128)S(1)}, f32[16,2048]{1,0:T(8,128)S(1)}, u32[]{:S(2)}, u32[]{:S(2)}) collective-permute-start(f32[16,2048]{1,0:T(8,128)S(1)} %get-tuple-element.26.first_ref.residual_ref), channel_id=1, source_target_pairs={{0,1},{1,0},{2,3},{3,2},{4,5},{5,4},{6,7},{7,6},{8,9},{9,8},{10,11... | collective-permute-start | bytes 393224 | tf_op jit(solution)/shard_map/ppermute | solution.py:588
  2.9 3.0 %collective-permute-start.1 = (f32[2,40,128]{2,1,0:T(8,128)S(1)}, f32[2,40,128]{2,1,0:T(8,128)S(1)}, u32[]{:S(2)}, u32[]{:S(2)}) collective-permute-start(f32[2,40,128]{2,1,0:T(8,128)S(1)} %pair.2), channel_id=1, source_target_pairs={{1,2},{3,4},{5,6},{7,8},{9,10},{11,12},{13,14},{2,1},{4,3},{6,5},{... | collective-permute-start | bytes 122888 | tf_op jit(solution)/shard_map/ppermute | solution.py:592
  5.2 11.0 %collective-permute-start.4 = (f32[2,16,2048]{2,1,0:T(8,128)S(1)}, f32[2,16,2048]{2,1,0:T(8,128)S(1)}, u32[]{:S(2)}, u32[]{:S(2)}) collective-permute-start(f32[2,16,2048]{2,1,0:T(8,128)S(1)} %pair.3.refs_2_), channel_id=1, source_target_pairs={{1,2},{3,4},{5,6},{7,8},{9,10},{11,12},{13,14},{2,1},{4,3},{6,5},{... | collective-permute-start | bytes 786440 | tf_op jit(solution)/shard_map/ppermute | solution.py:592
  5.9 5.3 %collective-permute-start.3 = (f32[40,128]{1,0:T(8,128)S(1)}, f32[40,128]{1,0:T(8,128)S(1)}, u32[]{:S(2)}, u32[]{:S(2)}) collective-permute-start(f32[40,128]{1,0:T(8,128)S(1)} %get-tuple-element.46.refs_0_), channel_id=1, source_target_pairs={{0,1},{1,0},{2,3},{3,2},{4,5},{5,4},{6,7},{7,6},{8,9},{9,8},{10,11... | collective-permute-start | bytes 61448 | tf_op jit(solution)/shard_map/ppermute | solution.py:588
  16.2 2.1 %collective-permute-start.5 = (f32[8,16,256]{2,1,0:T(8,128)S(1)}, f32[8,16,256]{2,1,0:T(8,128)S(1)}, u32[]{:S(2)}, u32[]{:S(2)}) collective-permute-start(f32[8,16,256]{2,1,0:T(8,128)S(1)} %slice_bitcast_fusion.2), channel_id=1, source_target_pairs={{0,1},{1,0},{2,3},{3,2},{4,5},{5,4},{6,7},{7,6},{8,9},{9,8},{10,11... | collective-permute-start | bytes 393224 | tf_op jit(solution)/shard_map/ppermute | solution.py:588
  18.4 8.4 %collective-permute-start.6 = (f32[2,8,16,256]{3,2,1,0:T(8,128)S(1)}, f32[2,8,16,256]{3,2,1,0:T(8,128)S(1)}, u32[]{:S(2)}, u32[]{:S(2)}) collective-permute-start(f32[2,8,16,256]{3,2,1,0:T(8,128)S(1)} %far_parts.1), channel_id=1, source_target_pairs={{1,2},{3,4},{5,6},{7,8},{9,10},{11,12},{13,14},{2,1},{4,3},{6,5},{... | collective-permute-start | bytes 786440 | tf_op jit(solution)/shard_map/ppermute | solution.py:592
  19.1 20.3 %copy-start = (f32[16,16384]{1,0:T(8,128)S(1)}, f32[16,16384]{1,0:T(8,128)}, u32[]{:S(2)}) copy-start(f32[16,16384]{1,0:T(8,128)} %direction_ref.3) | copy-start | bytes 3145732
  19.1 20.3 %copy-start.2 = (f32[16,16384]{1,0:T(8,128)S(1)}, f32[16,16384]{1,0:T(8,128)}, u32[]{:S(2)}) copy-start(f32[16,16384]{1,0:T(8,128)} %refs_6_.1) | copy-start | bytes 3145732
  26.8 7.7 %collective-permute-start.7 = (f32[2,8,16,256]{3,2,1,0:T(8,128)S(1)}, f32[2,8,16,256]{3,2,1,0:T(8,128)S(1)}, u32[]{:S(2)}, u32[]{:S(2)}) collective-permute-start(f32[2,8,16,256]{3,2,1,0:T(8,128)S(1)} %add.29.mine_ref), channel_id=1, source_target_pairs={{0,1},{1,0},{2,3},{3,2},{4,5},{5,4},{6,7},{7,6},{8,9},{9,8},{10,11... | collective-permute-start | bytes 786440 | tf_op jit(solution)/shard_map/ppermute | solution.py:588
  34.5 14.5 %collective-permute-start.8 = (f32[2,8,16,256]{3,2,1,0:T(8,128)S(1)}, f32[2,8,16,256]{3,2,1,0:T(8,128)S(1)}, u32[]{:S(2)}, u32[]{:S(2)}) collective-permute-start(f32[2,8,16,256]{3,2,1,0:T(8,128)S(1)} %both_images.1.refs_3_.refs_12_.image_ref), channel_id=1, source_target_pairs={{1,2},{3,4},{5,6},{7,8},{9,10},{11,12},{13,14},{2,1},{4,3},{6,5},{... | collective-permute-start | bytes 786440 | tf_op jit(solution)/shard_map/ppermute | solution.py:592
  35.2 13.8 %collective-permute-start.9 = (f32[16,2048]{1,0:T(8,128)S(1)}, f32[16,2048]{1,0:T(8,128)S(1)}, u32[]{:S(2)}, u32[]{:S(2)}) collective-permute-start(f32[16,2048]{1,0:T(8,128)S(1)} %slice_bitcast_fusion.1), channel_id=1, source_target_pairs={{0,1},{1,0},{2,3},{3,2},{4,5},{5,4},{6,7},{7,6},{8,9},{9,8},{10,11... | collective-permute-start | bytes 393224 | tf_op jit(solution)/shard_map/ppermute | solution.py:588
  39.3 11.1 %copy-start.1 = (f32[16,16384]{1,0:T(8,128)S(1)}, f32[16,16384]{1,0:T(8,128)}, u32[]{:S(2)}) copy-start(f32[16,16384]{1,0:T(8,128)} %model_ref.1) | copy-start | bytes 3145732
  49.0 1.4 %collective-permute-start.10 = (f32[8,16,256]{2,1,0:T(8,128)S(1)}, f32[8,16,256]{2,1,0:T(8,128)S(1)}, u32[]{:S(2)}, u32[]{:S(2)}) collective-permute-start(f32[8,16,256]{2,1,0:T(8,128)S(1)} %slice_bitcast_fusion), channel_id=1, source_target_pairs={{0,1},{1,0},{2,3},{3,2},{4,5},{5,4},{6,7},{7,6},{8,9},{9,8},{10,11... | collective-permute-start | bytes 393224 | tf_op jit(solution)/shard_map/ppermute | solution.py:588

commit v4 on v3

--- a/solution.py
+++ b/solution.py
@@ -41,11 +41,11 @@
     return jnp.dot(left, right, preferred_element_type=F32)
 
 
-def pack_kernel(offsets_any, pairs_any, residual_any, message_ref, residual_ref, offsets_ref, pairs_ref, sent):
+def pack_kernel(offsets_any, pairs_any, residual_any, message_ref, residual_ref, offsets_ref, pairs_ref, rows_ref, sent):
     copies = [
         pltpu.make_async_copy(offsets_any, offsets_ref, sent.at[0]),
         pltpu.make_async_copy(pairs_any, pairs_ref, sent.at[1]),
-        pltpu.make_async_copy(residual_any, residual_ref, sent.at[2]),
+        pltpu.make_async_copy(residual_any, rows_ref, sent.at[2]),
     ]
     for copy in copies:
         copy.start()
@@ -59,6 +59,8 @@
         message_ref[pl.ds(i, 1), :] = offsets_ref[pl.ds(0, 1), at]
         message_ref[pl.ds(lines + i, 1), :] = offsets_ref[pl.ds(1, 1), at]
     message_ref[pl.ds(2 * lines, rows), pl.ds(0, pairs)] = pairs_ref[...].astype(F32) + 1.0
+    for q in range(rows):
+        residual_ref[q] = rows_ref[:, pl.ds(q * SBLOCK, SBLOCK)]
 
 
 def in_hbm(array):
@@ -69,12 +71,13 @@
     rows = 2 * station_offsets.shape[1] // LANES + block_pairs.shape[0]
     return pl.pallas_call(
         pack_kernel,
-        out_shape=(jax.ShapeDtypeStruct((rows, LANES), F32), jax.ShapeDtypeStruct(residual.shape, F32)),
+        out_shape=(jax.ShapeDtypeStruct((rows, LANES), F32), jax.ShapeDtypeStruct((block_pairs.shape[0], residual.shape[0], SBLOCK), F32)),
         in_specs=[pl.BlockSpec(memory_space=pl.ANY)] * 3,
         out_specs=(VMEM, VMEM),
         scratch_shapes=[
             pltpu.VMEM(station_offsets.shape, F32),
             pltpu.VMEM(block_pairs.shape, jnp.int32),
+            pltpu.VMEM(residual.shape, F32),
             pltpu.SemaphoreType.DMA((3,)),
         ],
         compiler_params=params(2),
@@ -182,12 +185,16 @@
     )
 
 
-def send_codes(sizes, first_ref, messages, codes_ref, scalars_ref, sent):
-    cell_blocks, station_blocks, pairs, epochs, slots = sizes
+def tile_offset(place):
+    return place * (2 * (lax.axis_index("tile") % 2) - 1)
+
+
+def send_codes(sizes, messages, codes_ref, scalars_ref, sent):
+    cell_blocks, station_blocks, pairs, epochs, places = sizes
     q = lax.broadcasted_iota(jnp.int32, (station_blocks, LANES), 0)
     for slot, message_ref in enumerate(messages):
         codes = message_ref[pl.ds(message_ref.shape[0] - station_blocks, station_blocks), :]
-        within = codes.astype(jnp.int32) - first_ref[slot]
+        within = codes.astype(jnp.int32) - (cell_blocks * (REACH - tile_offset(places[slot])) + 1)
         hit = jnp.logical_and(within >= 0, within < cell_blocks)
         code = (slot * station_blocks + q) * cell_blocks + within
         codes_ref[pl.ds(slot * station_blocks, station_blocks), :] = jnp.where(hit, code, -1)
@@ -197,7 +204,8 @@
 
 
 def list_pairs(sizes, copy, scalars_ref, list_ref):
-    cell_blocks, station_blocks, pairs, epochs, slots = sizes
+    cell_blocks, station_blocks, pairs, epochs, places = sizes
+    slots = len(places)
     copy.wait()
     count = jnp.int32(0)
     for row in range(slots * station_blocks):
@@ -211,7 +219,8 @@
 
 
 def list_scratch(sizes):
-    cell_blocks, station_blocks, pairs, epochs, slots = sizes
+    cell_blocks, station_blocks, pairs, epochs, places = sizes
+    slots = len(places)
     return [
         pltpu.SMEM((slots * station_blocks * pairs + UNROLL + 4,), jnp.int32),
         pltpu.VMEM((slots * station_blocks, LANES), jnp.int32),
@@ -255,13 +264,14 @@
     return lax.rsqrt(squared * squared * squared)
 
 
-def forward_kernel(sizes, first_ref, shift_ref, *refs):
-    cell_blocks, station_blocks, pairs, epochs, slots = sizes
+def forward_kernel(sizes, *refs):
+    cell_blocks, station_blocks, pairs, epochs, places = sizes
+    slots = len(places)
     messages = refs[:slots]
     values_ref, turned_ref = refs[slots : slots + 2]
     images_ref, list_ref, codes_ref, scalars_ref, sent, *scratch = refs[slots + 2 :]
     across_ref, along_ref, image_ref, gaps_ref, lines_ref, depths_ref = scratch
-    copy = send_codes(sizes, first_ref, messages, codes_ref, scalars_ref, sent)
+    copy = send_codes(sizes, messages, codes_ref, scalars_ref, sent)
     dummy = slots * station_blocks
     per_block = SBLOCK // LANES
     lines = station_blocks * per_block
@@ -271,19 +281,21 @@
     for slot in range(slots):
         for i in range(lines):
             place = (pl.ds(slot * station_blocks + i // per_block, 1), pl.ds(i % per_block * LANES, LANES))
-            across_ref[place] = messages[slot][pl.ds(i, 1), :] + shift_ref[slot]
+            across_ref[place] = messages[slot][pl.ds(i, 1), :] + tile_offset(places[slot]).astype(F32)
             along_ref[place] = messages[slot][pl.ds(lines + i, 1), :]
     count = list_pairs(sizes, copy, scalars_ref, list_ref)
     column = lax.broadcasted_iota(jnp.int32, (COL_SIDE, SBLOCK), 0).astype(F32)
     column = (column + 0.5) / COL_SIDE
     rows = CBLOCK // COL_SIDE
+    line = (lax.broadcasted_iota(jnp.int32, (rows, SBLOCK), 0).astype(F32) + 0.5) / COL_SIDE
 
     def stage(i, k):
         code = list_ref[i]
         q, w = code // cell_blocks, code % cell_blocks
         across = across_ref[pl.ds(q, 1), :] - column
         gaps_ref[k] = across * across
-        lines_ref[k] = along_ref[pl.ds(q, 1), :] - (w % 2).astype(F32) * (rows / COL_SIDE)
+        along = along_ref[pl.ds(q, 1), :] - (w % 2).astype(F32) * (rows / COL_SIDE) - line
+        lines_ref[k] = along * along
         turned = pltpu.roll(turned_ref[...], (LANES - w * (CBLOCK // LANES)) % LANES, 1)
         for part in range(CBLOCK // LANES):
             depths_ref[k, pl.ds(part * LANES, LANES), :] = jnp.broadcast_to(turned[:, part : part + 1], (LANES, LANES))
@@ -291,15 +303,14 @@
     def issue(sums, i, k):
         w = list_ref[i] % cell_blocks
         across = gaps_ref[k]
-        along = lines_ref[k]
         for tile in range(CBLOCK // HALF):
             pieces = []
             for at in range(0, HALF, COL_SIDE):
                 y = (tile * HALF + at) // COL_SIDE
                 depth = depths_ref[k, pl.ds(y * COL_SIDE, COL_SIDE), :]
                 depth = jnp.concatenate([depth] * (SBLOCK // LANES), axis=1)
-                gap = along - (y + 0.5) / COL_SIDE
-                pieces.append(split(inverse_cube((across + gap * gap) + depth)))
+                along = lines_ref[k, pl.ds(y, 1), :]
+                pieces.append(split(inverse_cube((across + along) + depth)))
             left = values_ref[w, :, pl.ds(tile * HALF, HALF)]
             multiply_add(sums[2 * k + tile % 2], left, pieces, tile % 2, tile // 2)
 
@@ -316,13 +327,14 @@
         images_ref[slot] = image_ref[pl.ds(slot * station_blocks, station_blocks)]
 
 
-def forward(sizes, first, shift, messages, values, turned):
-    cell_blocks, station_blocks, pairs, epochs, slots = sizes
+def forward(sizes, messages, values, turned):
+    cell_blocks, station_blocks, pairs, epochs, places = sizes
+    slots = len(places)
     rows = (slots * station_blocks + 8) // 8 * 8
     return pl.pallas_call(
         functools.partial(forward_kernel, sizes),
         out_shape=jax.ShapeDtypeStruct((slots, station_blocks, epochs, SBLOCK), F32),
-        in_specs=[SMEM, SMEM] + [VMEM] * (slots + 2),
+        in_specs=[VMEM] * (slots + 2),
         out_specs=VMEM,
         scratch_shapes=list_scratch(sizes)
         + [
@@ -330,25 +342,27 @@
             pltpu.VMEM((rows, SBLOCK), F32),
             pltpu.VMEM((slots * station_blocks + 1, epochs, SBLOCK), F32),
             pltpu.VMEM((2, COL_SIDE, SBLOCK), F32),
-            pltpu.VMEM((2, 1, SBLOCK), F32),
+            pltpu.VMEM((2, CBLOCK // COL_SIDE, SBLOCK), F32),
             pltpu.VMEM((2, CBLOCK, LANES), F32),
         ],
         compiler_params=params(),
         cost_estimate=estimate(sizes, 0.1 if slots > 2 else 1),
         name="forward",
-    )(first, shift, *messages, values, turned)
+    )(*messages, values, turned)
 
 
 def estimate(sizes, part=1):
-    cell_blocks, station_blocks, pairs, epochs, slots = sizes
+    cell_blocks, station_blocks, pairs, epochs, places = sizes
+    slots = len(places)
     entries = station_blocks * pairs * slots // (2 * REACH + 1) * SBLOCK * CBLOCK
     return pl.CostEstimate(flops=int(2 * 1200 * entries * part), bytes_accessed=2**20, transcendentals=entries)
 
 
-def adjoint_sums(sizes, first_ref, shift_ref, messages, residuals, images, cells_ref, total_ref, scratch):
-    cell_blocks, station_blocks, pairs, epochs, slots = sizes
+def adjoint_sums(sizes, messages, residuals, images, cells_ref, total_ref, scratch):
+    cell_blocks, station_blocks, pairs, epochs, places = sizes
+    slots = len(places)
     list_ref, codes_ref, scalars_ref, sent, stations_ref, terms_ref, depths_ref, gaps_ref, lines_ref = scratch
-    copy = send_codes(sizes, first_ref, messages, codes_ref, scalars_ref, sent)
+    copy = send_codes(sizes, messages, codes_ref, scalars_ref, sent)
     dummy = slots * station_blocks
     terms_ref[dummy] = jnp.zeros(terms_ref.shape[1:], BF16)
     stations_ref[slots] = jnp.zeros(stations_ref.shape[1:], F32)
@@ -356,11 +370,12 @@
     per_block = SBLOCK // LANES
     lane_rows = station_blocks * per_block
     for slot in range(slots):
-        places = [messages[slot][pl.ds(0, lane_rows), :] + shift_ref[slot], messages[slot][pl.ds(lane_rows, lane_rows), :]]
-        places.append(jnp.zeros((LANES - 2 * lane_rows, LANES), F32))
-        stations_ref[slot] = jnp.concatenate(places, axis=0).T
+        shift = tile_offset(places[slot]).astype(F32)
+        rows = [messages[slot][pl.ds(0, lane_rows), :] + shift, messages[slot][pl.ds(lane_rows, lane_rows), :]]
+        rows.append(jnp.zeros((LANES - 2 * lane_rows, LANES), F32))
+        stations_ref[slot] = jnp.concatenate(rows, axis=0).T
         for q in range(station_blocks):
-            stacked = jnp.concatenate([residuals[slot][:, pl.ds(q * SBLOCK, SBLOCK)], images[slot][q]], axis=0)
+            stacked = jnp.concatenate([residuals[slot][q], images[slot][q]], axis=0)
             high, low = split(stacked)
             terms_ref[slot * station_blocks + q, pl.ds(0, 2 * epochs), :] = high
             terms_ref[slot * station_blocks + q, pl.ds(2 * epochs, 2 * epochs), :] = low
@@ -370,6 +385,7 @@
     line = ((lane // COL_SIDE).astype(F32) + 0.5) / COL_SIDE
     rows = CBLOCK // COL_SIDE
     chunks = CBLOCK // LANES
+    stride = LANES / COL_SIDE / COL_SIDE
 
     def stage(i, k):
         code = list_ref[i]
@@ -393,12 +409,16 @@
             for at in range(part * LANES, (part + 1) * LANES, 16):
                 across = gaps_ref[k, pl.ds(at, 16), :]
                 along = lines_ref[k, pl.ds(at, 16), :]
+                level = across + along * along
+                slope = stride * stride - 2 * stride * along
                 for unit in range(2):
                     near = []
                     for chunk in range(unit * chunks // 2, (unit + 1) * chunks // 2):
-                        gap = along - chunk * (LANES // COL_SIDE) / COL_SIDE
-                        squared = (across + gap * gap) + depth[:, chunk * LANES : (chunk + 1) * LANES]
+                        squared = level + depth[:, chunk * LANES : (chunk + 1) * LANES]
                         near.append(split(inverse_cube(squared)))
+                        if chunk < chunks - 1:
+                            level = level + slope
+                            slope = slope + 2 * stride * stride
                     pieces[unit].append([jnp.concatenate(terms, axis=1) for terms in zip(*near)])
             left = terms_ref[q, :, pl.ds(part * HALF, HALF)]
             for unit in range(2):
@@ -417,17 +437,21 @@
 
 
 def slot_refs(slots, refs):
-    messages, refs = refs[:slots], refs[slots:]
-    arrays = slots - 1
-    residuals, images, rest = refs[:arrays], refs[arrays : 2 * arrays], refs[2 * arrays :]
-    return messages, *([pair.at[0], pair.at[1], *single] for pair, *single in (residuals, images)), rest
-
-
-def near_kernel(sizes, first_ref, shift_ref, *refs):
-    cell_blocks, station_blocks, pairs, epochs, slots = sizes
+    messages, (residuals, images), rest = refs[:slots], refs[slots : slots + 2], refs[slots + 2 :]
+    residuals, images = [residuals.at[0], residuals.at[1]], [images.at[0], images.at[1]]
+    if slots == 3:
+        third, *rest = rest
+        residuals.append(third.at[0])
+        images.append(third.at[1])
+    return messages, residuals, images, rest
+
+
+def near_kernel(sizes, *refs):
+    cell_blocks, station_blocks, pairs, epochs, places = sizes
+    slots = len(places)
     messages, residuals, images, rest = slot_refs(slots, refs)
     cells_ref, direction_ref, old_ref, total_ref, sums_ref, *scratch = rest
-    adjoint_sums(sizes, first_ref, shift_ref, messages, residuals, images, cells_ref, total_ref, scratch)
+    adjoint_sums(sizes, messages, residuals, images, cells_ref, total_ref, scratch)
 
     def add(w, sums):
         at = pl.ds(pl.multiple_of(w * CBLOCK, CBLOCK), CBLOCK)
@@ -439,13 +463,14 @@
         sums_ref[pl.ds(i, 1), :] = jnp.broadcast_to(jnp.sum(total).reshape(1, 1), (1, LANES))
 
 
-def far_kernel(sizes, first_ref, shift_ref, *refs):
-    cell_blocks, station_blocks, pairs, epochs, slots = sizes
+def far_kernel(sizes, *refs):
+    cell_blocks, station_blocks, pairs, epochs, places = sizes
+    slots = len(places)
     messages, residuals, images, rest = slot_refs(slots, refs)
     cells_ref, near_ref, sums_ref, model_ref, direction_ref, image_ref = rest[:6]
     constant_ref, slope_ref, stats_ref = rest[6:9]
     total_ref, *scratch = rest[9:]
-    adjoint_sums(sizes, first_ref, shift_ref, messages, residuals, images, cells_ref, total_ref, scratch)
+    adjoint_sums(sizes, messages, residuals, images, cells_ref, total_ref, scratch)
     zero = jnp.zeros((epochs, CBLOCK), F32)
 
     def combine(w, sums):
@@ -487,8 +512,9 @@
         stats_ref[i] = row
 
 
-def adjoint(sizes, first, shift, messages, residuals, images, cell_rows, *others, ranks=None):
-    cell_blocks, station_blocks, pairs, epochs, slots = sizes
+def adjoint(sizes, messages, terms, cell_rows, *others, ranks=None):
+    cell_blocks, station_blocks, pairs, epochs, places = sizes
+    slots = len(places)
     total = (cell_blocks, 2 * epochs, CBLOCK)
     scratch = list_scratch(sizes) + [
         pltpu.VMEM((slots + 1, LANES, LANES), F32),
@@ -506,13 +532,13 @@
     return pl.pallas_call(
         functools.partial(kernel, sizes),
         out_shape=tuple(jax.ShapeDtypeStruct(shape, F32) for shape in shapes),
-        in_specs=[SMEM, SMEM] + [VMEM] * (3 * slots - 1 + len(others)),
+        in_specs=[VMEM] * (slots + len(terms) + 1 + len(others)),
         out_specs=(VMEM,) * len(shapes),
         scratch_shapes=scratch,
         compiler_params=params(),
         cost_estimate=estimate(sizes),
         name="near" if ranks is None else "far",
-    )(first, shift, *messages, *residuals, *images, cell_rows, *others)
+    )(*messages, *terms, cell_rows, *others)
 
 
 def finish_kernel(
@@ -536,8 +562,8 @@
 
     for q in range(image_ref.shape[1]):
         at = pl.ds(q * SBLOCK, SBLOCK)
-        new_residual[:, at] = residual_ref[:, at] - step * image_ref[0, q]
-    send(0, new_residual, residual_out, pl.ds(0, residual_ref.shape[1]))
+        new_residual[:, at] = residual_ref[q] - step * image_ref[0, q]
+    send(0, new_residual, residual_out, pl.ds(0, new_residual.shape[1]))
     cells = model_ref.shape[1] // FINISH_PARTS
     for part in range(FINISH_PARTS):
 
@@ -559,7 +585,8 @@
 
 
 def finish(stats, constant, slope, model_field, direction, residual, image):
-    outs = (model_field.shape, residual.shape, direction.shape)
+    blocks, epochs, _ = residual.shape
+    outs = (model_field.shape, (epochs, blocks * SBLOCK), direction.shape)
     return pl.pallas_call(
         finish_kernel,
         out_shape=tuple(jax.ShapeDtypeStruct(shape, F32) for shape in outs),
@@ -578,11 +605,9 @@
 
 def shards(model_field, direction, old_grad, residual, block_pairs, depth_band, station_offsets):
     ranks = lax.axis_size("tile")
-    tile_id = lax.axis_index("tile")
     epochs, cells = model_field.shape
     station_blocks, pairs = block_pairs.shape
     cell_blocks = cells // CBLOCK
-    side = 2 * (tile_id % 2) - 1
 
     def to_partner(array):
         return lax.ppermute(array, "tile", [(i, i ^ 1) for i in range(ranks)])
@@ -591,12 +616,8 @@
         ends = [(i, i + 1) for i in range(1, ranks - 1, 2)]
         return lax.ppermute(message, "tile", ends + [(j, i) for i, j in ends])
 
-    def slots(*places):
-        offsets = jnp.stack([multiple * side for multiple in places]).astype(jnp.int32)
-        sizes = (cell_blocks, station_blocks, pairs, epochs, len(places))
-        return sizes, cell_blocks * (REACH - offsets) + 1, offsets.astype(F32)
-
-    near_slots, far_slots = slots(0, -1), slots(1, 2, -2)
+    sizes = (cell_blocks, station_blocks, pairs, epochs)
+    near_slots, far_slots = (*sizes, (0, -1)), (*sizes, (1, 2, -2))
 
     own, residual = pack(station_offsets, block_pairs, residual)
     partner = to_partner(own)
@@ -609,22 +630,21 @@
     far = [arrived[0], arrived[1], to_partner(arrived[0])]
 
     far_residuals = across(residuals)
-    parts = forward(*far_slots, far, values, turned)
+    parts = forward(far_slots, far, values, turned)
     parts, far_residuals = after((parts, far_residuals), (far_residuals, parts))
     returned = to_partner(parts[2])
     given = across(far_parts(parts, returned))
-    mine = forward(*near_slots, after(near, returned), values, turned)
+    mine = forward(near_slots, after(near, returned), values, turned)
     given = after(given, mine)
     mine = small_call(add_kernel, mine.shape, "add", mine, given)
     images = both_images(mine, to_partner(mine))
 
     far_images = across(images)
-    third_residual = to_partner(after(far_residuals[0], images))
-    near_total, sums = adjoint(*near_slots, near, [residuals], [images], cell_rows, direction, old_grad)
-    far_images, third_residual = after((far_images, third_residual), near_total)
-    third_image = to_partner(far_images[0])
+    near_total, sums = adjoint(near_slots, near, [residuals, images], cell_rows, direction, old_grad)
+    far_images = after(far_images, near_total)
+    thirds = to_partner(pair_up(far_residuals[0], far_images[0]))
     constant, slope, stats = adjoint(
-        *far_slots, far, [far_residuals, third_residual], [far_images, third_image], cell_rows,
+        far_slots, far, [far_residuals, far_images, thirds], cell_rows,
         near_total, sums, model_field, direction, images, ranks=ranks,
     )
     stats = lax.all_to_all(stats, "tile", 0, 0)

time: 78.8 us -> 76.5 us (0.971)
  the two profiles are of different devices: /device:TPU:2 before, /device:TPU:0 now
where the time goes in v4:
time: 76.5 us; the launch traced here: 75.8 us
  Pallas kernels  26.7 us (35%)
  starting transfers between devices  22 us (29%)
  blocking collectives  21 us (27%)
  waiting for transfers between devices  5.27 us (7%)
  between operations  0.85 us (1%)
    all_to_all x1, blocking collectives, shards(): stats = lax.all_to_all(stats, 'tile', 0, 0)  21 us
    ppermute x6, starting transfers between devices, to_partner(): return lax.ppermute(array, 'tile', [(i, i ^ 1) for i in range(ranks)])  19.1 us
    pallas_call x2, Pallas kernels, adjoint(): pl.pallas_call(functools.partial(kernel, sizes), out_shape=tuple((jax.Sha...  12.5 us
    pallas_call x2, Pallas kernels, forward(): pl.pallas_call(functools.partial(forward_kernel, sizes), out_shape=jax.Sh...  9.28 us
    ppermute x6, waiting for transfers between devices, to_partner(): return lax.ppermute(array, 'tile', [(i, i ^ 1) for i in range(ranks)])  5.26 us
    ppermute x4, starting transfers between devices, across(): return lax.ppermute(message, 'tile', ends + [(j, i) for i, j in ends])  2.82 us
    pallas_call x1, Pallas kernels, finish(): pl.pallas_call(finish_kernel, out_shape=tuple((jax.ShapeDtypeStruct(shape...  2.22 us
    pallas_call x1, Pallas kernels, prepare(): pl.pallas_call(functools.partial(prepare_kernel, scale), grid=(PARTS,), o...  1.56 us
  transfers between devices with their start and end apart: 10, of which 5 were waited for; matrix products, arithmetic and copies ran while one was open for 0% of the time, Pallas kernels for 25%

profile of v4, /device:TPU:0, one launch (start us, length us, event | category | flops | bytes accessed | tf_op | source)
XLA Modules:
  0.0 75.8 jit_solution(10940242189484217310)
XLA Ops:
  0.6 1.0 %pack.1 = (f32[40,128]{1,0:T(8,128)S(1)}, f32[8,16,256]{2,1,0:T(8,128)S(1)}) custom-call(f32[2,2048]{1,0:T(2,128)} %offsets_any.1, s32[8,8]{1,0:T(8,128)} %pairs_any.1, f32[16,2048]{1,0:T(8,128)} %residual_any.1), custom_call_target="tpu_custom_call" | custom-call | tf_op jit(solution)/shard_map/pack/pallas_call | solution.py:72
  1.6 0.5 collective-permute-start.2
  2.1 0.1 collective-permute-start
  2.2 1.1 %collective-permute-done.second_ref.refs_1_ = f32[40,128]{1,0:T(8,128)S(1)} collective-permute-done((f32[40,128]{1,0:T(8,128)S(1)}, f32[40,128]{1,0:T(8,128)S(1)}, u32[]{:S(2)}, u32[]{:S(2)}) %collective-permute-start) | collective-permute-done | bytes 20512 | tf_op jit(solution)/shard_map/ppermute | solution.py:613
  3.3 0.7 collective-permute-start.1
  4.0 1.6 %prepare.1 = (bf16[32,32,512]{2,1,0:T(8,128)(2,1)S(1)}, f32[2,16384]{1,0:T(2,128)S(1)}, f32[128,128]{1,0:T(8,128)S(1)}) custom-call(s32[128,128]{1,0:T(8,128)} %bitcast.12, s32[1,16384]{1,0:T(1,128)} %bitcast.13, f32[16,16384]{1,0:T(8,128)} %direction_ref.3), custom_call_target="tpu_custom_call" | custom-call | flops 2097152 | bytes 3145728 | tf_op jit(solution)/shard_map/prepare/pallas_call | solution.py:160
  5.6 0.0 collective-permute-done.2.second_ref
  5.6 0.7 collective-permute-start.4
  6.3 0.0 collective-permute-done.1
  6.3 5.4 %collective-permute-start.3 = (f32[40,128]{1,0:T(8,128)S(1)}, f32[40,128]{1,0:T(8,128)S(1)}, u32[]{:S(2)}, u32[]{:S(2)}) collective-permute-start(f32[40,128]{1,0:T(8,128)S(1)} %get-tuple-element.40.refs_0_), channel_id=1, source_target_pairs={{0,1},{1,0},{2,3},{3,2},{4,5},{5,4},{6,7},{7,6},{8,9},{9,8},{10,11... | collective-permute-start | bytes 61448 | tf_op jit(solution)/shard_map/ppermute | solution.py:613
  11.7 0.8 %collective-permute-done.3.refs_2_ = f32[40,128]{1,0:T(8,128)S(1)} collective-permute-done((f32[40,128]{1,0:T(8,128)S(1)}, f32[40,128]{1,0:T(8,128)S(1)}, u32[]{:S(2)}, u32[]{:S(2)}) %collective-permute-start.3) | collective-permute-done | bytes 20512 | tf_op jit(solution)/shard_map/ppermute | solution.py:613
  12.5 3.0 %forward.2.parts_ref = f32[3,8,16,256]{3,2,1,0:T(8,128)S(1)} custom-call(f32[40,128]{1,0:T(8,128)S(1)} %get-tuple-element.40.refs_0_, f32[40,128]{1,0:T(8,128)S(1)} %get-tuple-element.39.refs_1_, f32[40,128]{1,0:T(8,128)S(1)} %collective-permute-done.3.refs_2_, bf16[32,32,512]{2,1,0:T(8,128)(2,1)S(1)} %get-tuple-element.23.refs_3_.refs_2_, ...), custom_call_target="tpu_custom_call" | custom-call | flops 1195376640 | bytes 1048576 | tf_op jit(solution)/shard_map/forward/pallas_call | solution.py:334
  15.5 0.0 collective-permute-done.4.refs_3_
  15.5 3.2 %collective-permute-start.5 = (f32[8,16,256]{2,1,0:T(8,128)S(1)}, f32[8,16,256]{2,1,0:T(8,128)S(1)}, u32[]{:S(2)}, u32[]{:S(2)}) collective-permute-start(f32[8,16,256]{2,1,0:T(8,128)S(1)} %slice_bitcast_fusion.2), channel_id=1, source_target_pairs={{0,1},{1,0},{2,3},{3,2},{4,5},{5,4},{6,7},{7,6},{8,9},{9,8},{10,11... | collective-permute-start | bytes 393224 | tf_op jit(solution)/shard_map/ppermute | solution.py:613
  18.8 1.0 %collective-permute-done.5.third_ref = f32[8,16,256]{2,1,0:T(8,128)S(1)} collective-permute-done((f32[8,16,256]{2,1,0:T(8,128)S(1)}, f32[8,16,256]{2,1,0:T(8,128)S(1)}, u32[]{:S(2)}, u32[]{:S(2)}) %collective-permute-start.5) | collective-permute-done | bytes 131104 | tf_op jit(solution)/shard_map/ppermute | solution.py:613
  19.8 0.0 copy-start
  19.8 0.0 copy-start.2
  19.8 0.8 %collective-permute-start.6 = (f32[2,8,16,256]{3,2,1,0:T(8,128)S(1)}, f32[2,8,16,256]{3,2,1,0:T(8,128)S(1)}, u32[]{:S(2)}, u32[]{:S(2)}) collective-permute-start(f32[2,8,16,256]{3,2,1,0:T(8,128)S(1)} %far_parts.1), channel_id=1, source_target_pairs={{1,2},{3,4},{5,6},{7,8},{9,10},{11,12},{13,14},{2,1},{4,3},{6,5},{... | collective-permute-start | bytes 786440 | tf_op jit(solution)/shard_map/ppermute | solution.py:617
  20.6 6.3 %forward.3.left_ref = f32[2,8,16,256]{3,2,1,0:T(8,128)S(1)} custom-call(f32[40,128]{1,0:T(8,128)S(1)} %get-tuple-element.29.first_ref.refs_0_, f32[40,128]{1,0:T(8,128)S(1)} %collective-permute-done.second_ref.refs_1_, bf16[32,32,512]{2,1,0:T(8,128)(2,1)S(1)} %get-tuple-element.23.refs_3_.refs_2_, f32[128,128]{1,0:T(8,128)S(1)} %get-tuple-element.26.refs_4_.refs_3_), custom_call_target="tpu_custom_call" | custom-call | flops 7864320000 | bytes 1048576 | tf_op jit(solution)/shard_map/forward/pallas_call | solution.py:334
  26.9 0.0 collective-permute-done.6.right_ref
  27.0 7.6 %collective-permute-start.7 = (f32[2,8,16,256]{3,2,1,0:T(8,128)S(1)}, f32[2,8,16,256]{3,2,1,0:T(8,128)S(1)}, u32[]{:S(2)}, u32[]{:S(2)}) collective-permute-start(f32[2,8,16,256]{3,2,1,0:T(8,128)S(1)} %add.1.mine_ref), channel_id=1, source_target_pairs={{0,1},{1,0},{2,3},{3,2},{4,5},{5,4},{6,7},{7,6},{8,9},{9,8},{10,11... | collective-permute-start | bytes 786440 | tf_op jit(solution)/shard_map/ppermute | solution.py:613
  34.6 1.1 %collective-permute-done.7.theirs_ref = f32[2,8,16,256]{3,2,1,0:T(8,128)S(1)} collective-permute-done((f32[2,8,16,256]{3,2,1,0:T(8,128)S(1)}, f32[2,8,16,256]{3,2,1,0:T(8,128)S(1)}, u32[]{:S(2)}, u32[]{:S(2)}) %collective-permute-start.7) | collective-permute-done | bytes 262176 | tf_op jit(solution)/shard_map/ppermute | solution.py:613
  35.8 0.7 collective-permute-start.8
  36.5 0.0 copy-start.1
  36.5 8.0 %near.1 = (f32[32,32,512]{2,1,0:T(8,128)S(1)}, f32[2,128]{1,0:T(2,128)S(1)}) custom-call(f32[40,128]{1,0:T(8,128)S(1)} %get-tuple-element.29.first_ref.refs_0_, f32[40,128]{1,0:T(8,128)S(1)} %collective-permute-done.second_ref.refs_1_, f32[2,8,16,256]{3,2,1,0:T(8,128)S(1)} %pair.4.refs_2_, f32[2,8,16,256]{3,2,1,0:T(8,128)S(1)} %both_images.1.refs_3_.refs_11_.image_ref, ...), custom_call_target="tpu_custom_call" | custom-call | flops 7864320000 | bytes 1048576 | tf_op jit(solution)/shard_map/near/pallas_call | solution.py:532
  44.4 0.0 collective-permute-done.8.refs_4_
  44.5 2.4 %collective-permute-start.9 = (f32[2,8,16,256]{3,2,1,0:T(8,128)S(1)}, f32[2,8,16,256]{3,2,1,0:T(8,128)S(1)}, u32[]{:S(2)}, u32[]{:S(2)}) collective-permute-start(f32[2,8,16,256]{3,2,1,0:T(8,128)S(1)} %pair.5), channel_id=1, source_target_pairs={{0,1},{1,0},{2,3},{3,2},{4,5},{5,4},{6,7},{7,6},{8,9},{9,8},{10,11... | collective-permute-start | bytes 786440 | tf_op jit(solution)/shard_map/ppermute | solution.py:613
  46.9 1.2 %collective-permute-done.9.refs_5_ = f32[2,8,16,256]{3,2,1,0:T(8,128)S(1)} collective-permute-done((f32[2,8,16,256]{3,2,1,0:T(8,128)S(1)}, f32[2,8,16,256]{3,2,1,0:T(8,128)S(1)}, u32[]{:S(2)}, u32[]{:S(2)}) %collective-permute-start.9) | collective-permute-done | bytes 262176 | tf_op jit(solution)/shard_map/ppermute | solution.py:613
  48.0 0.0 copy-done.1
  48.0 4.5 %far.1 = (f32[16,16384]{1,0:T(8,128)S(1)}, f32[16,16384]{1,0:T(8,128)S(1)}, f32[16,1,128]{2,1,0:T(1,128)S(1)}) custom-call(f32[40,128]{1,0:T(8,128)S(1)} %get-tuple-element.40.refs_0_, f32[40,128]{1,0:T(8,128)S(1)} %get-tuple-element.39.refs_1_, f32[40,128]{1,0:T(8,128)S(1)} %collective-permute-done.3.refs_2_, ...), custom_call_target="tpu_custom_call" | custom-call | flops 11953766400 | bytes 1048576 | tf_op jit(solution)/shard_map/far/pallas_call | solution.py:532
  52.6 21.0 %all_to_all.5.stats_ref = f32[16,1,128]{2,1,0:T(1,128)S(1)} all-to-all(f32[16,1,128]{2,1,0:T(1,128)S(1)} %get-tuple-element.36), channel_id=1, replica_groups=mesh['groups'=2,'tile'=16] {'tile'}, dimensions={0} | all-to-all | bytes 16384 | tf_op jit(solution)/shard_map/all_to_all | solution.py:650
  73.6 2.2 %finish.1 = (f32[16,16384]{1,0:T(8,128)}, f32[16,2048]{1,0:T(8,128)}, f32[16,16384]{1,0:T(8,128)}) custom-call(f32[16,1,128]{2,1,0:T(1,128)S(1)} %all_to_all.5.stats_ref, f32[16,16384]{1,0:T(8,128)S(1)} %get-tuple-element.37.constant_ref, f32[16,16384]{1,0:T(8,128)S(1)} %get-tuple-element.38.slope_ref, f32[16,16384]{1,0:T(8,128)S(1)} %copy-done.1, ...), custom_call_target="tpu_custom_call" | custom-call | tf_op jit(solution)/shard_map/finish/pallas_call | solution.py:590
  (12 shorter events, 0.2 us)
Async XLA Ops:
  1.6 3.9 %collective-permute-start.2 = (f32[8,16,256]{2,1,0:T(8,128)S(1)}, f32[8,16,256]{2,1,0:T(8,128)S(1)}, u32[]{:S(2)}, u32[]{:S(2)}) collective-permute-start(f32[8,16,256]{2,1,0:T(8,128)S(1)} %get-tuple-element.24.first_ref.residual_ref), channel_id=1, source_target_pairs={{0,1},{1,0},{2,3},{3,2},{4,5},{5,4},{6,7},{7,6},{8,9},{9,8},{10,11... | collective-permute-start | bytes 393224 | tf_op jit(solution)/shard_map/ppermute | solution.py:613
  2.1 1.2 %collective-permute-start = (f32[40,128]{1,0:T(8,128)S(1)}, f32[40,128]{1,0:T(8,128)S(1)}, u32[]{:S(2)}, u32[]{:S(2)}) collective-permute-start(f32[40,128]{1,0:T(8,128)S(1)} %get-tuple-element.29.first_ref.refs_0_), channel_id=1, source_target_pairs={{0,1},{1,0},{2,3},{3,2},{4,5},{5,4},{6,7},{7,6},{8,9},{9,8},{10,11... | collective-permute-start | bytes 61448 | tf_op jit(solution)/shard_map/ppermute | solution.py:613
  3.3 3.0 %collective-permute-start.1 = (f32[2,40,128]{2,1,0:T(8,128)S(1)}, f32[2,40,128]{2,1,0:T(8,128)S(1)}, u32[]{:S(2)}, u32[]{:S(2)}) collective-permute-start(f32[2,40,128]{2,1,0:T(8,128)S(1)} %pair.3), channel_id=1, source_target_pairs={{1,2},{3,4},{5,6},{7,8},{9,10},{11,12},{13,14},{2,1},{4,3},{6,5},{... | collective-permute-start | bytes 122888 | tf_op jit(solution)/shard_map/ppermute | solution.py:617
  5.6 9.9 %collective-permute-start.4 = (f32[2,8,16,256]{3,2,1,0:T(8,128)S(1)}, f32[2,8,16,256]{3,2,1,0:T(8,128)S(1)}, u32[]{:S(2)}, u32[]{:S(2)}) collective-permute-start(f32[2,8,16,256]{3,2,1,0:T(8,128)S(1)} %pair.4.refs_2_), channel_id=1, source_target_pairs={{1,2},{3,4},{5,6},{7,8},{9,10},{11,12},{13,14},{2,1},{4,3},{6,5},{... | collective-permute-start | bytes 786440 | tf_op jit(solution)/shard_map/ppermute | solution.py:617
  6.3 6.2 %collective-permute-start.3 = (f32[40,128]{1,0:T(8,128)S(1)}, f32[40,128]{1,0:T(8,128)S(1)}, u32[]{:S(2)}, u32[]{:S(2)}) collective-permute-start(f32[40,128]{1,0:T(8,128)S(1)} %get-tuple-element.40.refs_0_), channel_id=1, source_target_pairs={{0,1},{1,0},{2,3},{3,2},{4,5},{5,4},{6,7},{7,6},{8,9},{9,8},{10,11... | collective-permute-start | bytes 61448 | tf_op jit(solution)/shard_map/ppermute | solution.py:613
  15.5 4.2 %collective-permute-start.5 = (f32[8,16,256]{2,1,0:T(8,128)S(1)}, f32[8,16,256]{2,1,0:T(8,128)S(1)}, u32[]{:S(2)}, u32[]{:S(2)}) collective-permute-start(f32[8,16,256]{2,1,0:T(8,128)S(1)} %slice_bitcast_fusion.2), channel_id=1, source_target_pairs={{0,1},{1,0},{2,3},{3,2},{4,5},{5,4},{6,7},{7,6},{8,9},{9,8},{10,11... | collective-permute-start | bytes 393224 | tf_op jit(solution)/shard_map/ppermute | solution.py:613
  19.8 16.6 %copy-start = (f32[16,16384]{1,0:T(8,128)S(1)}, f32[16,16384]{1,0:T(8,128)}, u32[]{:S(2)}) copy-start(f32[16,16384]{1,0:T(8,128)} %direction_ref.3) | copy-start | bytes 3145732
  19.8 16.6 %copy-start.2 = (f32[16,16384]{1,0:T(8,128)S(1)}, f32[16,16384]{1,0:T(8,128)}, u32[]{:S(2)}) copy-start(f32[16,16384]{1,0:T(8,128)} %refs_6_.1) | copy-start | bytes 3145732
  19.8 7.1 %collective-permute-start.6 = (f32[2,8,16,256]{3,2,1,0:T(8,128)S(1)}, f32[2,8,16,256]{3,2,1,0:T(8,128)S(1)}, u32[]{:S(2)}, u32[]{:S(2)}) collective-permute-start(f32[2,8,16,256]{3,2,1,0:T(8,128)S(1)} %far_parts.1), channel_id=1, source_target_pairs={{1,2},{3,4},{5,6},{7,8},{9,10},{11,12},{13,14},{2,1},{4,3},{6,5},{... | collective-permute-start | bytes 786440 | tf_op jit(solution)/shard_map/ppermute | solution.py:617
  27.0 8.7 %collective-permute-start.7 = (f32[2,8,16,256]{3,2,1,0:T(8,128)S(1)}, f32[2,8,16,256]{3,2,1,0:T(8,128)S(1)}, u32[]{:S(2)}, u32[]{:S(2)}) collective-permute-start(f32[2,8,16,256]{3,2,1,0:T(8,128)S(1)} %add.1.mine_ref), channel_id=1, source_target_pairs={{0,1},{1,0},{2,3},{3,2},{4,5},{5,4},{6,7},{7,6},{8,9},{9,8},{10,11... | collective-permute-start | bytes 786440 | tf_op jit(solution)/shard_map/ppermute | solution.py:613
  35.8 8.7 %collective-permute-start.8 = (f32[2,8,16,256]{3,2,1,0:T(8,128)S(1)}, f32[2,8,16,256]{3,2,1,0:T(8,128)S(1)}, u32[]{:S(2)}, u32[]{:S(2)}) collective-permute-start(f32[2,8,16,256]{3,2,1,0:T(8,128)S(1)} %both_images.1.refs_3_.refs_11_.image_ref), channel_id=1, source_target_pairs={{1,2},{3,4},{5,6},{7,8},{9,10},{11,12},{13,14},{2,1},{4,3},{6,5},{... | collective-permute-start | bytes 786440 | tf_op jit(solution)/shard_map/ppermute | solution.py:617
  36.5 11.6 %copy-start.1 = (f32[16,16384]{1,0:T(8,128)S(1)}, f32[16,16384]{1,0:T(8,128)}, u32[]{:S(2)}) copy-start(f32[16,16384]{1,0:T(8,128)} %model_ref.1) | copy-start | bytes 3145732
  44.5 3.5 %collective-permute-start.9 = (f32[2,8,16,256]{3,2,1,0:T(8,128)S(1)}, f32[2,8,16,256]{3,2,1,0:T(8,128)S(1)}, u32[]{:S(2)}, u32[]{:S(2)}) collective-permute-start(f32[2,8,16,256]{3,2,1,0:T(8,128)S(1)} %pair.5), channel_id=1, source_target_pairs={{0,1},{1,0},{2,3},{3,2},{4,5},{5,4},{6,7},{7,6},{8,9},{9,8},{10,11... | collective-permute-start | bytes 786440 | tf_op jit(solution)/shard_map/ppermute | solution.py:613

commit v5 on v4

--- a/solution.py
+++ b/solution.py
@@ -30,6 +30,11 @@
 
 def params(mebibytes=16):
     return pltpu.CompilerParams(vmem_limit_bytes=mebibytes * 2**20)
+
+
+def parts_of(number, size):
+    assert size & (size - 1) == 0
+    return number >> (size.bit_length() - 1), number & (size - 1)
 
 
 def split(values):
@@ -186,7 +191,7 @@
 
 
 def tile_offset(place):
-    return place * (2 * (lax.axis_index("tile") % 2) - 1)
+    return place * (2 * (lax.axis_index("tile") & 1) - 1)
 
 
 def send_codes(sizes, messages, codes_ref, scalars_ref, sent):
@@ -213,7 +218,7 @@
             code = scalars_ref[row, i]
             list_ref[count] = code
             count = count + (code >= 0).astype(jnp.int32)
-    for i in range(UNROLL + 4):
+    for i in range(2 * UNROLL):
         list_ref[count + i] = slots * station_blocks * cell_blocks
     return count
 
@@ -222,7 +227,7 @@
     cell_blocks, station_blocks, pairs, epochs, places = sizes
     slots = len(places)
     return [
-        pltpu.SMEM((slots * station_blocks * pairs + UNROLL + 4,), jnp.int32),
+        pltpu.SMEM((slots * station_blocks * pairs + 2 * UNROLL,), jnp.int32),
         pltpu.VMEM((slots * station_blocks, LANES), jnp.int32),
         pltpu.SMEM((slots * station_blocks, LANES), jnp.int32),
         pltpu.SemaphoreType.DMA(()),
@@ -239,10 +244,10 @@
 
     def step(j, unused):
         for k in range(UNROLL):
-            i, now, later = UNROLL * j + k, k % 2, 1 - k % 2
-            issue(i + 1, later)
-            stage(i + 2, now)
-            collect(i, now)
+            i = UNROLL * j + k
+            issue(i + 1, (k + 1) % 2)
+            stage(i + 2, k % 2)
+            collect(i, k % 2)
         return 0
 
     rounds = (count + UNROLL - 2) // UNROLL
@@ -291,17 +296,17 @@
 
     def stage(i, k):
         code = list_ref[i]
-        q, w = code // cell_blocks, code % cell_blocks
+        q, w = parts_of(code, cell_blocks)
         across = across_ref[pl.ds(q, 1), :] - column
         gaps_ref[k] = across * across
-        along = along_ref[pl.ds(q, 1), :] - (w % 2).astype(F32) * (rows / COL_SIDE) - line
+        along = along_ref[pl.ds(q, 1), :] - (w & 1).astype(F32) * (rows / COL_SIDE) - line
         lines_ref[k] = along * along
-        turned = pltpu.roll(turned_ref[...], (LANES - w * (CBLOCK // LANES)) % LANES, 1)
+        turned = pltpu.roll(turned_ref[...], (LANES - w * (CBLOCK // LANES)) & (LANES - 1), 1)
         for part in range(CBLOCK // LANES):
             depths_ref[k, pl.ds(part * LANES, LANES), :] = jnp.broadcast_to(turned[:, part : part + 1], (LANES, LANES))
 
     def issue(sums, i, k):
-        w = list_ref[i] % cell_blocks
+        w = list_ref[i] & (cell_blocks - 1)
         across = gaps_ref[k]
         for tile in range(CBLOCK // HALF):
             pieces = []
@@ -315,7 +320,7 @@
             multiply_add(sums[2 * k + tile % 2], left, pieces, tile % 2, tile // 2)
 
     def collect(sums, i, k):
-        q = list_ref[i] // cell_blocks
+        q, _ = parts_of(list_ref[i], cell_blocks)
         both = pltpu.matmul_pop(sums[2 * k]) + pltpu.matmul_pop(sums[2 * k + 1])
         image_ref[q] += both[:epochs] + both[epochs:]
 
@@ -358,15 +363,13 @@
     return pl.CostEstimate(flops=int(2 * 1200 * entries * part), bytes_accessed=2**20, transcendentals=entries)
 
 
-def adjoint_sums(sizes, messages, residuals, images, cells_ref, total_ref, scratch):
+def adjoint_sums(sizes, messages, residuals, images, cells_ref, total_ref, scratch, clear):
     cell_blocks, station_blocks, pairs, epochs, places = sizes
     slots = len(places)
     list_ref, codes_ref, scalars_ref, sent, stations_ref, terms_ref, depths_ref, gaps_ref, lines_ref = scratch
     copy = send_codes(sizes, messages, codes_ref, scalars_ref, sent)
     dummy = slots * station_blocks
-    terms_ref[dummy] = jnp.zeros(terms_ref.shape[1:], BF16)
     stations_ref[slots] = jnp.zeros(stations_ref.shape[1:], F32)
-    total_ref[...] = jnp.zeros_like(total_ref)
     per_block = SBLOCK // LANES
     lane_rows = station_blocks * per_block
     for slot in range(slots):
@@ -374,12 +377,16 @@
         rows = [messages[slot][pl.ds(0, lane_rows), :] + shift, messages[slot][pl.ds(lane_rows, lane_rows), :]]
         rows.append(jnp.zeros((LANES - 2 * lane_rows, LANES), F32))
         stations_ref[slot] = jnp.concatenate(rows, axis=0).T
+    if clear:
+        total_ref[...] = jnp.zeros_like(total_ref)
+    count = list_pairs(sizes, copy, scalars_ref, list_ref)
+    terms_ref[dummy] = jnp.zeros(terms_ref.shape[1:], BF16)
+    for slot in range(slots):
         for q in range(station_blocks):
             stacked = jnp.concatenate([residuals[slot][q], images[slot][q]], axis=0)
             high, low = split(stacked)
             terms_ref[slot * station_blocks + q, pl.ds(0, 2 * epochs), :] = high
             terms_ref[slot * station_blocks + q, pl.ds(2 * epochs, 2 * epochs), :] = low
-    count = list_pairs(sizes, copy, scalars_ref, list_ref)
     lane = lax.broadcasted_iota(jnp.int32, (1, LANES), 1)
     column = ((lane % COL_SIDE).astype(F32) + 0.5) / COL_SIDE
     line = ((lane // COL_SIDE).astype(F32) + 0.5) / COL_SIDE
@@ -389,11 +396,11 @@
 
     def stage(i, k):
         code = list_ref[i]
-        q, w = code // cell_blocks, code % cell_blocks
-        slot, within = q // station_blocks, q % station_blocks
+        q, w = parts_of(code, cell_blocks)
+        slot, within = parts_of(q, station_blocks)
         depths_ref[k] = cells_ref[pl.ds(0, 1), pl.ds(pl.multiple_of(w * CBLOCK, CBLOCK), CBLOCK)]
-        lines = line + (w % 2).astype(F32) * (rows / COL_SIDE)
-        places = pltpu.roll(stations_ref[slot], (LANES - within * per_block) % LANES, 1)
+        lines = line + (w & 1).astype(F32) * (rows / COL_SIDE)
+        places = pltpu.roll(stations_ref[slot], (LANES - within * per_block) & (LANES - 1), 1)
         for part in range(per_block):
             at = pl.ds(part * LANES, LANES)
             across = jnp.broadcast_to(places[:, part : part + 1], (LANES, LANES)) - column
@@ -402,7 +409,7 @@
             lines_ref[k, at, :] = along - lines
 
     def issue(sums, i, k):
-        q = list_ref[i] // cell_blocks
+        q, _ = parts_of(list_ref[i], cell_blocks)
         depth = depths_ref[k]
         for part in range(per_block):
             pieces = ([], [])
@@ -425,7 +432,7 @@
                 multiply_add(sums[2 * k + unit], left, pieces[unit], unit, part)
 
     def collect(sums, i, k):
-        w = list_ref[i] % cell_blocks
+        w = list_ref[i] & (cell_blocks - 1)
         for unit in range(2):
             both = pltpu.matmul_pop(sums[2 * k + unit])
             total_ref[w, :, pl.ds(unit * TILE, TILE)] += both[: 2 * epochs] + both[2 * epochs :]
@@ -451,7 +458,7 @@
     slots = len(places)
     messages, residuals, images, rest = slot_refs(slots, refs)
     cells_ref, direction_ref, old_ref, total_ref, sums_ref, *scratch = rest
-    adjoint_sums(sizes, messages, residuals, images, cells_ref, total_ref, scratch)
+    adjoint_sums(sizes, messages, residuals, images, cells_ref, total_ref, scratch, True)
 
     def add(w, sums):
         at = pl.ds(pl.multiple_of(w * CBLOCK, CBLOCK), CBLOCK)
@@ -467,15 +474,14 @@
     cell_blocks, station_blocks, pairs, epochs, places = sizes
     slots = len(places)
     messages, residuals, images, rest = slot_refs(slots, refs)
-    cells_ref, near_ref, sums_ref, model_ref, direction_ref, image_ref = rest[:6]
-    constant_ref, slope_ref, stats_ref = rest[6:9]
-    total_ref, *scratch = rest[9:]
-    adjoint_sums(sizes, messages, residuals, images, cells_ref, total_ref, scratch)
+    cells_ref, _, sums_ref, model_ref, direction_ref, image_ref = rest[:6]
+    constant_ref, slope_ref, stats_ref, total_ref, *scratch = rest[6:]
+    adjoint_sums(sizes, messages, residuals, images, cells_ref, total_ref, scratch, False)
     zero = jnp.zeros((epochs, CBLOCK), F32)
 
     def combine(w, sums):
         at = pl.ds(pl.multiple_of(w * CBLOCK, CBLOCK), CBLOCK)
-        total = (near_ref[w] + total_ref[w]) * cells_ref[pl.ds(1, 1), at]
+        total = total_ref[w] * cells_ref[pl.ds(1, 1), at]
         constant = total[:epochs] - DAMPING * model_ref[:, at]
         slope = total[epochs:] + DAMPING * direction_ref[:, at]
         constant_ref[:, at] = constant
@@ -524,17 +530,18 @@
         pltpu.VMEM((2, SBLOCK, LANES), F32),
     ]
     if ranks is None:
-        kernel, shapes = near_kernel, [total, (2, LANES)]
+        kernel, shapes, aliases = near_kernel, [total, (2, LANES)], {}
     else:
         kernel, cells = far_kernel, (epochs, cell_blocks * CBLOCK)
-        shapes = [cells, cells, (ranks, 1, LANES)]
-        scratch = [pltpu.VMEM(total, F32)] + scratch
+        shapes = [cells, cells, (ranks, 1, LANES), total]
+        aliases = {slots + len(terms) + 1: 3}
     return pl.pallas_call(
         functools.partial(kernel, sizes),
         out_shape=tuple(jax.ShapeDtypeStruct(shape, F32) for shape in shapes),
         in_specs=[VMEM] * (slots + len(terms) + 1 + len(others)),
         out_specs=(VMEM,) * len(shapes),
         scratch_shapes=scratch,
+        input_output_aliases=aliases,
         compiler_params=params(),
         cost_estimate=estimate(sizes),
         name="near" if ranks is None else "far",
@@ -623,10 +630,10 @@
     partner = to_partner(own)
     near = [own, partner]
     partner_residual = to_partner(residual)
-    arrived = across(pair_up(*near))
-    values, cell_rows, turned = prepare(2.0 / math.sqrt(cells), after(depth_band, partner), direction)
+    values, cell_rows, turned = prepare(2.0 / math.sqrt(cells), after(depth_band, own), direction)
+    arrived = across(pair_up(own, after(partner, values)))
     residuals = pair_up(residual, partner_residual)
-    arrived = after(arrived, (values, residuals))
+    arrived = after(arrived, residuals)
     far = [arrived[0], arrived[1], to_partner(arrived[0])]
 
     far_residuals = across(residuals)
@@ -643,7 +650,7 @@
     near_total, sums = adjoint(near_slots, near, [residuals, images], cell_rows, direction, old_grad)
     far_images = after(far_images, near_total)
     thirds = to_partner(pair_up(far_residuals[0], far_images[0]))
-    constant, slope, stats = adjoint(
+    constant, slope, stats, _ = adjoint(
         far_slots, far, [far_residuals, far_images, thirds], cell_rows,
         near_total, sums, model_field, direction, images, ranks=ranks,
     )

time: 76.5 us -> 75 us (0.980)
  starting transfers between devices: 22 us -> 25.3 us
  blocking collectives: 21 us -> 18.4 us
  Pallas kernels: 26.7 us -> 24.9 us
  waiting for transfers between devices: 5.27 us -> 4.16 us
    ppermute x6, starting transfers between devices: 19.1 us -> 22.5 us  [to_partner(): return lax.ppermute(array, 'tile', [(i, i ^ 1) for i in range(ranks)])]
    all_to_all x1, blocking collectives: 21 us -> 18.4 us  [shards(): stats = lax.all_to_all(stats, 'tile', 0, 0)]
    ppermute x6, waiting for transfers between devices: 5.26 us -> 4.15 us  [to_partner(): return lax.ppermute(array, 'tile', [(i, i ^ 1) for i in range(ranks)])]
    pallas_call x2, Pallas kernels: 12.5 us -> 11.5 us  [adjoint(): pl.pallas_call(functools.partial(kernel, sizes), out_shape=tuple((jax.Sha...]
    pallas_call x2, Pallas kernels: 9.28 us -> 8.5 us  [forward(): pl.pallas_call(functools.partial(forward_kernel, sizes), out_shape=jax.Sh...]
  transfers between devices with their start and end apart: 10 -> 10, of which waited for: 5 -> 4; matrix products, arithmetic and copies ran while one was open for 0% -> 0% of each run, Pallas kernels for 25% -> 22%
where the time goes in v5:
time: 75 us; the launch traced here: 73.7 us
  starting transfers between devices  25.3 us (34%)
  Pallas kernels  24.9 us (33%)
  blocking collectives  18.4 us (25%)
  waiting for transfers between devices  4.16 us (6%)
  between operations  0.87 us (1%)
    ppermute x6, starting transfers between devices, to_partner(): return lax.ppermute(array, 'tile', [(i, i ^ 1) for i in range(ranks)])  22.5 us
    all_to_all x1, blocking collectives, shards(): stats = lax.all_to_all(stats, 'tile', 0, 0)  18.4 us
    pallas_call x2, Pallas kernels, adjoint(): pl.pallas_call(functools.partial(kernel, sizes), out_shape=tuple((jax.Sha...  11.5 us
    pallas_call x2, Pallas kernels, forward(): pl.pallas_call(functools.partial(forward_kernel, sizes), out_shape=jax.Sh...  8.5 us
    ppermute x6, waiting for transfers between devices, to_partner(): return lax.ppermute(array, 'tile', [(i, i ^ 1) for i in range(ranks)])  4.15 us
    ppermute x4, starting transfers between devices, across(): return lax.ppermute(message, 'tile', ends + [(j, i) for i, j in ends])  2.83 us
    pallas_call x1, Pallas kernels, finish(): pl.pallas_call(finish_kernel, out_shape=tuple((jax.ShapeDtypeStruct(shape...  2.22 us
    pallas_call x1, Pallas kernels, prepare(): pl.pallas_call(functools.partial(prepare_kernel, scale), grid=(PARTS,), o...  1.54 us
  transfers between devices with their start and end apart: 10, of which 4 were waited for; matrix products, arithmetic and copies ran while one was open for 0% of the time, Pallas kernels for 22%

profile of v5, /device:TPU:0, one launch (start us, length us, event | category | flops | bytes accessed | tf_op | source)
XLA Modules:
  0.0 73.7 jit_solution(10101448304729013098)
XLA Ops:
  0.6 1.0 %pack.1 = (f32[40,128]{1,0:T(8,128)S(1)}, f32[8,16,256]{2,1,0:T(8,128)S(1)}) custom-call(f32[2,2048]{1,0:T(2,128)} %offsets_any.1, s32[8,8]{1,0:T(8,128)} %pairs_any.1, f32[16,2048]{1,0:T(8,128)} %residual_any.1), custom_call_target="tpu_custom_call" | custom-call | tf_op jit(solution)/shard_map/pack/pallas_call | solution.py:77
  1.6 0.5 collective-permute-start.2
  2.1 0.1 collective-permute-start
  2.2 1.5 %prepare.1 = (bf16[32,32,512]{2,1,0:T(8,128)(2,1)S(1)}, f32[2,16384]{1,0:T(2,128)S(1)}, f32[128,128]{1,0:T(8,128)S(1)}) custom-call(s32[128,128]{1,0:T(8,128)} %bitcast.12, s32[1,16384]{1,0:T(1,128)} %bitcast.13, f32[16,16384]{1,0:T(8,128)} %direction_ref.3), custom_call_target="tpu_custom_call" | custom-call | flops 2097152 | bytes 3145728 | tf_op jit(solution)/shard_map/prepare/pallas_call | solution.py:165
  3.8 0.0 collective-permute-done.second_ref.refs_1_
  3.8 0.7 collective-permute-start.1
  4.5 0.0 collective-permute-done.2.second_ref
  4.5 0.7 collective-permute-start.4
  5.2 0.0 collective-permute-done.1
  5.2 5.6 %collective-permute-start.3 = (f32[40,128]{1,0:T(8,128)S(1)}, f32[40,128]{1,0:T(8,128)S(1)}, u32[]{:S(2)}, u32[]{:S(2)}) collective-permute-start(f32[40,128]{1,0:T(8,128)S(1)} %get-tuple-element.42.refs_0_), channel_id=1, source_target_pairs={{0,1},{1,0},{2,3},{3,2},{4,5},{5,4},{6,7},{7,6},{8,9},{9,8},{10,11... | collective-permute-start | bytes 61448 | tf_op jit(solution)/shard_map/ppermute | solution.py:620
  10.8 0.8 %collective-permute-done.3.refs_2_ = f32[40,128]{1,0:T(8,128)S(1)} collective-permute-done((f32[40,128]{1,0:T(8,128)S(1)}, f32[40,128]{1,0:T(8,128)S(1)}, u32[]{:S(2)}, u32[]{:S(2)}) %collective-permute-start.3) | collective-permute-done | bytes 20512 | tf_op jit(solution)/shard_map/ppermute | solution.py:620
  11.7 3.7 %forward.2.parts_ref = f32[3,8,16,256]{3,2,1,0:T(8,128)S(1)} custom-call(f32[40,128]{1,0:T(8,128)S(1)} %get-tuple-element.42.refs_0_, f32[40,128]{1,0:T(8,128)S(1)} %get-tuple-element.41.refs_1_, f32[40,128]{1,0:T(8,128)S(1)} %collective-permute-done.3.refs_2_, bf16[32,32,512]{2,1,0:T(8,128)(2,1)S(1)} %get-tuple-element.24.refs_3_.refs_2_, ...), custom_call_target="tpu_custom_call" | custom-call | flops 1195376640 | bytes 1048576 | tf_op jit(solution)/shard_map/forward/pallas_call | solution.py:339
  15.3 0.0 collective-permute-done.4.refs_3_
  15.4 2.5 %collective-permute-start.5 = (f32[8,16,256]{2,1,0:T(8,128)S(1)}, f32[8,16,256]{2,1,0:T(8,128)S(1)}, u32[]{:S(2)}, u32[]{:S(2)}) collective-permute-start(f32[8,16,256]{2,1,0:T(8,128)S(1)} %slice_bitcast_fusion.2), channel_id=1, source_target_pairs={{0,1},{1,0},{2,3},{3,2},{4,5},{5,4},{6,7},{7,6},{8,9},{9,8},{10,11... | collective-permute-start | bytes 393224 | tf_op jit(solution)/shard_map/ppermute | solution.py:620
  17.9 1.0 %collective-permute-done.5.third_ref = f32[8,16,256]{2,1,0:T(8,128)S(1)} collective-permute-done((f32[8,16,256]{2,1,0:T(8,128)S(1)}, f32[8,16,256]{2,1,0:T(8,128)S(1)}, u32[]{:S(2)}, u32[]{:S(2)}) %collective-permute-start.5) | collective-permute-done | bytes 131104 | tf_op jit(solution)/shard_map/ppermute | solution.py:620
  18.9 0.0 copy-start
  18.9 0.0 copy-start.2
  18.9 0.8 %collective-permute-start.6 = (f32[2,8,16,256]{3,2,1,0:T(8,128)S(1)}, f32[2,8,16,256]{3,2,1,0:T(8,128)S(1)}, u32[]{:S(2)}, u32[]{:S(2)}) collective-permute-start(f32[2,8,16,256]{3,2,1,0:T(8,128)S(1)} %far_parts.1), channel_id=1, source_target_pairs={{1,2},{3,4},{5,6},{7,8},{9,10},{11,12},{13,14},{2,1},{4,3},{6,5},{... | collective-permute-start | bytes 786440 | tf_op jit(solution)/shard_map/ppermute | solution.py:624
  19.7 4.8 %forward.3.left_ref = f32[2,8,16,256]{3,2,1,0:T(8,128)S(1)} custom-call(f32[40,128]{1,0:T(8,128)S(1)} %get-tuple-element.31.first_ref.refs_0_, f32[40,128]{1,0:T(8,128)S(1)} %collective-permute-done.second_ref.refs_1_, bf16[32,32,512]{2,1,0:T(8,128)(2,1)S(1)} %get-tuple-element.24.refs_3_.refs_2_, f32[128,128]{1,0:T(8,128)S(1)} %get-tuple-element.28.refs_4_.refs_3_), custom_call_target="tpu_custom_call" | custom-call | flops 7864320000 | bytes 1048576 | tf_op jit(solution)/shard_map/forward/pallas_call | solution.py:339
  24.6 0.0 collective-permute-done.6.right_ref
  24.6 8.7 %collective-permute-start.7 = (f32[2,8,16,256]{3,2,1,0:T(8,128)S(1)}, f32[2,8,16,256]{3,2,1,0:T(8,128)S(1)}, u32[]{:S(2)}, u32[]{:S(2)}) collective-permute-start(f32[2,8,16,256]{3,2,1,0:T(8,128)S(1)} %add.1.mine_ref), channel_id=1, source_target_pairs={{0,1},{1,0},{2,3},{3,2},{4,5},{5,4},{6,7},{7,6},{8,9},{9,8},{10,11... | collective-permute-start | bytes 786440 | tf_op jit(solution)/shard_map/ppermute | solution.py:620
  33.4 1.1 %collective-permute-done.7.theirs_ref = f32[2,8,16,256]{3,2,1,0:T(8,128)S(1)} collective-permute-done((f32[2,8,16,256]{3,2,1,0:T(8,128)S(1)}, f32[2,8,16,256]{3,2,1,0:T(8,128)S(1)}, u32[]{:S(2)}, u32[]{:S(2)}) %collective-permute-start.7) | collective-permute-done | bytes 262176 | tf_op jit(solution)/shard_map/ppermute | solution.py:620
  34.6 0.7 collective-permute-start.8
  35.3 0.0 copy-start.1
  35.3 6.2 %near.1 = (f32[32,32,512]{2,1,0:T(8,128)S(1)}, f32[2,128]{1,0:T(2,128)S(1)}) custom-call(f32[40,128]{1,0:T(8,128)S(1)} %get-tuple-element.31.first_ref.refs_0_, f32[40,128]{1,0:T(8,128)S(1)} %collective-permute-done.second_ref.refs_1_, f32[2,8,16,256]{3,2,1,0:T(8,128)S(1)} %pair.4.refs_2_, f32[2,8,16,256]{3,2,1,0:T(8,128)S(1)} %both_images.1.refs_3_.refs_11_.image_ref, ...), custom_call_target="tpu_custom_call" | custom-call | flops 7864320000 | bytes 1048576 | tf_op jit(solution)/shard_map/near/pallas_call | solution.py:538
  41.5 0.0 collective-permute-done.8.refs_4_
  41.5 5.0 %collective-permute-start.9 = (f32[2,8,16,256]{3,2,1,0:T(8,128)S(1)}, f32[2,8,16,256]{3,2,1,0:T(8,128)S(1)}, u32[]{:S(2)}, u32[]{:S(2)}) collective-permute-start(f32[2,8,16,256]{3,2,1,0:T(8,128)S(1)} %pair.5), channel_id=1, source_target_pairs={{0,1},{1,0},{2,3},{3,2},{4,5},{5,4},{6,7},{7,6},{8,9},{9,8},{10,11... | collective-permute-start | bytes 786440 | tf_op jit(solution)/shard_map/ppermute | solution.py:620
  46.5 1.2 %collective-permute-done.9.refs_5_ = f32[2,8,16,256]{3,2,1,0:T(8,128)S(1)} collective-permute-done((f32[2,8,16,256]{3,2,1,0:T(8,128)S(1)}, f32[2,8,16,256]{3,2,1,0:T(8,128)S(1)}, u32[]{:S(2)}, u32[]{:S(2)}) %collective-permute-start.9) | collective-permute-done | bytes 262176 | tf_op jit(solution)/shard_map/ppermute | solution.py:620
  47.7 0.0 copy-done.1
  47.7 5.4 %far.1 = (f32[16,16384]{1,0:T(8,128)S(1)}, f32[16,16384]{1,0:T(8,128)S(1)}, f32[16,1,128]{2,1,0:T(1,128)S(1)}, f32[32,32,512]{2,1,0:T(8,128)S(1)}) custom-call(f32[40,128]{1,0:T(8,128)S(1)} %get-tuple-element.42.refs_0_, f32[40,128]{1,0:T(8,128)S(1)} %get-tuple-element.41.refs_1_, ...), custom_call_target="tpu_custom_call", output_to_operand_aliasing={{3}: (7, {})} | custom-call | flops 11953766400 | bytes 1048576 | tf_op jit(solution)/shard_map/far/pallas_call | solution.py:538
  53.1 18.4 %all_to_all.5.stats_ref = f32[16,1,128]{2,1,0:T(1,128)S(1)} all-to-all(f32[16,1,128]{2,1,0:T(1,128)S(1)} %get-tuple-element.38), channel_id=1, replica_groups=mesh['groups'=2,'tile'=16] {'tile'}, dimensions={0} | all-to-all | bytes 16384 | tf_op jit(solution)/shard_map/all_to_all | solution.py:657
  71.4 2.2 %finish.1 = (f32[16,16384]{1,0:T(8,128)}, f32[16,2048]{1,0:T(8,128)}, f32[16,16384]{1,0:T(8,128)}) custom-call(f32[16,1,128]{2,1,0:T(1,128)S(1)} %all_to_all.5.stats_ref, f32[16,16384]{1,0:T(8,128)S(1)} %get-tuple-element.39.constant_ref, f32[16,16384]{1,0:T(8,128)S(1)} %get-tuple-element.40.slope_ref, f32[16,16384]{1,0:T(8,128)S(1)} %copy-done.1, ...), custom_call_target="tpu_custom_call" | custom-call | tf_op jit(solution)/shard_map/finish/pallas_call | solution.py:597
  (12 shorter events, 0.2 us)
Async XLA Ops:
  1.6 2.8 %collective-permute-start.2 = (f32[8,16,256]{2,1,0:T(8,128)S(1)}, f32[8,16,256]{2,1,0:T(8,128)S(1)}, u32[]{:S(2)}, u32[]{:S(2)}) collective-permute-start(f32[8,16,256]{2,1,0:T(8,128)S(1)} %get-tuple-element.26.first_ref.residual_ref), channel_id=1, source_target_pairs={{0,1},{1,0},{2,3},{3,2},{4,5},{5,4},{6,7},{7,6},{8,9},{9,8},{10,11... | collective-permute-start | bytes 393224 | tf_op jit(solution)/shard_map/ppermute | solution.py:620
  2.1 1.6 %collective-permute-start = (f32[40,128]{1,0:T(8,128)S(1)}, f32[40,128]{1,0:T(8,128)S(1)}, u32[]{:S(2)}, u32[]{:S(2)}) collective-permute-start(f32[40,128]{1,0:T(8,128)S(1)} %get-tuple-element.31.first_ref.refs_0_), channel_id=1, source_target_pairs={{0,1},{1,0},{2,3},{3,2},{4,5},{5,4},{6,7},{7,6},{8,9},{9,8},{10,11... | collective-permute-start | bytes 61448 | tf_op jit(solution)/shard_map/ppermute | solution.py:620
  3.8 1.4 %collective-permute-start.1 = (f32[2,40,128]{2,1,0:T(8,128)S(1)}, f32[2,40,128]{2,1,0:T(8,128)S(1)}, u32[]{:S(2)}, u32[]{:S(2)}) collective-permute-start(f32[2,40,128]{2,1,0:T(8,128)S(1)} %pair.3), channel_id=1, source_target_pairs={{1,2},{3,4},{5,6},{7,8},{9,10},{11,12},{13,14},{2,1},{4,3},{6,5},{... | collective-permute-start | bytes 122888 | tf_op jit(solution)/shard_map/ppermute | solution.py:624
  4.5 10.8 %collective-permute-start.4 = (f32[2,8,16,256]{3,2,1,0:T(8,128)S(1)}, f32[2,8,16,256]{3,2,1,0:T(8,128)S(1)}, u32[]{:S(2)}, u32[]{:S(2)}) collective-permute-start(f32[2,8,16,256]{3,2,1,0:T(8,128)S(1)} %pair.4.refs_2_), channel_id=1, source_target_pairs={{1,2},{3,4},{5,6},{7,8},{9,10},{11,12},{13,14},{2,1},{4,3},{6,5},{... | collective-permute-start | bytes 786440 | tf_op jit(solution)/shard_map/ppermute | solution.py:624
  5.2 6.5 %collective-permute-start.3 = (f32[40,128]{1,0:T(8,128)S(1)}, f32[40,128]{1,0:T(8,128)S(1)}, u32[]{:S(2)}, u32[]{:S(2)}) collective-permute-start(f32[40,128]{1,0:T(8,128)S(1)} %get-tuple-element.42.refs_0_), channel_id=1, source_target_pairs={{0,1},{1,0},{2,3},{3,2},{4,5},{5,4},{6,7},{7,6},{8,9},{9,8},{10,11... | collective-permute-start | bytes 61448 | tf_op jit(solution)/shard_map/ppermute | solution.py:620
  15.4 3.5 %collective-permute-start.5 = (f32[8,16,256]{2,1,0:T(8,128)S(1)}, f32[8,16,256]{2,1,0:T(8,128)S(1)}, u32[]{:S(2)}, u32[]{:S(2)}) collective-permute-start(f32[8,16,256]{2,1,0:T(8,128)S(1)} %slice_bitcast_fusion.2), channel_id=1, source_target_pairs={{0,1},{1,0},{2,3},{3,2},{4,5},{5,4},{6,7},{7,6},{8,9},{9,8},{10,11... | collective-permute-start | bytes 393224 | tf_op jit(solution)/shard_map/ppermute | solution.py:620
  18.9 16.4 %copy-start = (f32[16,16384]{1,0:T(8,128)S(1)}, f32[16,16384]{1,0:T(8,128)}, u32[]{:S(2)}) copy-start(f32[16,16384]{1,0:T(8,128)} %direction_ref.3) | copy-start | bytes 3145732
  18.9 16.4 %copy-start.2 = (f32[16,16384]{1,0:T(8,128)S(1)}, f32[16,16384]{1,0:T(8,128)}, u32[]{:S(2)}) copy-start(f32[16,16384]{1,0:T(8,128)} %refs_6_.1) | copy-start | bytes 3145732
  18.9 5.7 %collective-permute-start.6 = (f32[2,8,16,256]{3,2,1,0:T(8,128)S(1)}, f32[2,8,16,256]{3,2,1,0:T(8,128)S(1)}, u32[]{:S(2)}, u32[]{:S(2)}) collective-permute-start(f32[2,8,16,256]{3,2,1,0:T(8,128)S(1)} %far_parts.1), channel_id=1, source_target_pairs={{1,2},{3,4},{5,6},{7,8},{9,10},{11,12},{13,14},{2,1},{4,3},{6,5},{... | collective-permute-start | bytes 786440 | tf_op jit(solution)/shard_map/ppermute | solution.py:624
  24.6 9.9 %collective-permute-start.7 = (f32[2,8,16,256]{3,2,1,0:T(8,128)S(1)}, f32[2,8,16,256]{3,2,1,0:T(8,128)S(1)}, u32[]{:S(2)}, u32[]{:S(2)}) collective-permute-start(f32[2,8,16,256]{3,2,1,0:T(8,128)S(1)} %add.1.mine_ref), channel_id=1, source_target_pairs={{0,1},{1,0},{2,3},{3,2},{4,5},{5,4},{6,7},{7,6},{8,9},{9,8},{10,11... | collective-permute-start | bytes 786440 | tf_op jit(solution)/shard_map/ppermute | solution.py:620
  34.6 6.9 %collective-permute-start.8 = (f32[2,8,16,256]{3,2,1,0:T(8,128)S(1)}, f32[2,8,16,256]{3,2,1,0:T(8,128)S(1)}, u32[]{:S(2)}, u32[]{:S(2)}) collective-permute-start(f32[2,8,16,256]{3,2,1,0:T(8,128)S(1)} %both_images.1.refs_3_.refs_11_.image_ref), channel_id=1, source_target_pairs={{1,2},{3,4},{5,6},{7,8},{9,10},{11,12},{13,14},{2,1},{4,3},{6,5},{... | collective-permute-start | bytes 786440 | tf_op jit(solution)/shard_map/ppermute | solution.py:624
  35.3 12.4 %copy-start.1 = (f32[16,16384]{1,0:T(8,128)S(1)}, f32[16,16384]{1,0:T(8,128)}, u32[]{:S(2)}) copy-start(f32[16,16384]{1,0:T(8,128)} %model_ref.1) | copy-start | bytes 3145732
  41.5 6.2 %collective-permute-start.9 = (f32[2,8,16,256]{3,2,1,0:T(8,128)S(1)}, f32[2,8,16,256]{3,2,1,0:T(8,128)S(1)}, u32[]{:S(2)}, u32[]{:S(2)}) collective-permute-start(f32[2,8,16,256]{3,2,1,0:T(8,128)S(1)} %pair.5), channel_id=1, source_target_pairs={{0,1},{1,0},{2,3},{3,2},{4,5},{5,4},{6,7},{7,6},{8,9},{9,8},{10,11... | collective-permute-start | bytes 786440 | tf_op jit(solution)/shard_map/ppermute | solution.py:620

commit v6 on v5

--- a/solution.py
+++ b/solution.py
@@ -23,6 +23,7 @@
 LANES = 128
 TILE = 256
 HALF = TILE // 2
+GROUP = HALF // 2
 
 SMEM = pl.BlockSpec(memory_space=pltpu.SMEM)
 VMEM = pl.BlockSpec(memory_space=pltpu.VMEM)
@@ -242,23 +243,37 @@
     stage(1, 1)
     issue(0, 0)
 
-    def step(j, unused):
-        for k in range(UNROLL):
-            i = UNROLL * j + k
-            issue(i + 1, (k + 1) % 2)
-            stage(i + 2, k % 2)
-            collect(i, k % 2)
-        return 0
-
-    rounds = (count + UNROLL - 2) // UNROLL
-    lax.fori_loop(0, rounds, step, 0)
-    collect(UNROLL * rounds, 0)
-
-
-def multiply_add(sums_ref, left, pieces, unit, register):
-    high, low = zip(*pieces)
-    pltpu.matmul_push_rhs(jnp.concatenate(high + low, axis=0), register, unit)
-    pltpu.matmul_acc_lhs(sums_ref, jnp.concatenate([left, left], axis=1), load_staged_rhs=register)
+    def rounds(first, number, size):
+        def step(j, unused):
+            for k in range(size):
+                i = first + size * j + k
+                issue(i + 1, (k + 1) % 2)
+                stage(i + 2, k % 2)
+                collect(i, k % 2)
+            return 0
+
+        lax.fori_loop(0, number, step, 0)
+        return first + size * number
+
+    whole = count // UNROLL
+    done = rounds(0, whole, UNROLL)
+    done = rounds(done, (count > 1 + done).astype(jnp.int32), UNROLL // 2)
+    collect(done, 0)
+
+
+def doubled(array, group):
+    groups = [array[:, i : i + group] for i in range(0, array.shape[1], group)]
+    return jnp.concatenate([group for group in groups for _ in range(2)], axis=1)
+
+
+def multiply_add(sums_ref, left, pieces, group, unit, register):
+    rows = pieces[0][0].shape[0]
+    tile = []
+    for i in range(0, len(pieces), group // rows):
+        high, low = zip(*pieces[i : i + group // rows])
+        tile += high + low
+    pltpu.matmul_push_rhs(jnp.concatenate(tile, axis=0), register, unit)
+    pltpu.matmul_acc_lhs(sums_ref, left, load_staged_rhs=register)
 
 
 def accumulators(rows):
@@ -316,8 +331,8 @@
                 depth = jnp.concatenate([depth] * (SBLOCK // LANES), axis=1)
                 along = lines_ref[k, pl.ds(y, 1), :]
                 pieces.append(split(inverse_cube((across + along) + depth)))
-            left = values_ref[w, :, pl.ds(tile * HALF, HALF)]
-            multiply_add(sums[2 * k + tile % 2], left, pieces, tile % 2, tile // 2)
+            left = doubled(values_ref[w, :, pl.ds(tile * HALF, HALF)], HALF)
+            multiply_add(sums[2 * k + tile % 2], left, pieces, HALF, tile % 2, tile // 2)
 
     def collect(sums, i, k):
         q, _ = parts_of(list_ref[i], cell_blocks)
@@ -383,7 +398,7 @@
     terms_ref[dummy] = jnp.zeros(terms_ref.shape[1:], BF16)
     for slot in range(slots):
         for q in range(station_blocks):
-            stacked = jnp.concatenate([residuals[slot][q], images[slot][q]], axis=0)
+            stacked = doubled(jnp.concatenate([residuals[slot][q], images[slot][q]], axis=0), GROUP)
             high, low = split(stacked)
             terms_ref[slot * station_blocks + q, pl.ds(0, 2 * epochs), :] = high
             terms_ref[slot * station_blocks + q, pl.ds(2 * epochs, 2 * epochs), :] = low
@@ -427,9 +442,9 @@
                             level = level + slope
                             slope = slope + 2 * stride * stride
                     pieces[unit].append([jnp.concatenate(terms, axis=1) for terms in zip(*near)])
-            left = terms_ref[q, :, pl.ds(part * HALF, HALF)]
+            left = terms_ref[q, :, pl.ds(part * TILE, TILE)]
             for unit in range(2):
-                multiply_add(sums[2 * k + unit], left, pieces[unit], unit, part)
+                multiply_add(sums[2 * k + unit], left, pieces[unit], GROUP, unit, part)
 
     def collect(sums, i, k):
         w = list_ref[i] & (cell_blocks - 1)
@@ -457,16 +472,20 @@
     cell_blocks, station_blocks, pairs, epochs, places = sizes
     slots = len(places)
     messages, residuals, images, rest = slot_refs(slots, refs)
-    cells_ref, direction_ref, old_ref, total_ref, sums_ref, *scratch = rest
+    cells_ref, total_ref, *scratch = rest
     adjoint_sums(sizes, messages, residuals, images, cells_ref, total_ref, scratch, True)
+
+
+def squares_kernel(old_ref, direction_ref, sums_ref):
+    epochs, cells = direction_ref.shape
 
     def add(w, sums):
         at = pl.ds(pl.multiple_of(w * CBLOCK, CBLOCK), CBLOCK)
-        direction, old = direction_ref[:, at], old_ref[:, at]
+        old, direction = old_ref[:, at], direction_ref[:, at]
         return sums[0] + old * old, sums[1] + direction * direction
 
     zero = jnp.zeros((epochs, CBLOCK), F32)
-    for i, total in enumerate(lax.fori_loop(0, cell_blocks, add, (zero, zero), unroll=4)):
+    for i, total in enumerate(lax.fori_loop(0, cells // CBLOCK, add, (zero, zero), unroll=4)):
         sums_ref[pl.ds(i, 1), :] = jnp.broadcast_to(jnp.sum(total).reshape(1, 1), (1, LANES))
 
 
@@ -524,13 +543,13 @@
     total = (cell_blocks, 2 * epochs, CBLOCK)
     scratch = list_scratch(sizes) + [
         pltpu.VMEM((slots + 1, LANES, LANES), F32),
-        pltpu.VMEM((slots * station_blocks + 1, 4 * epochs, SBLOCK), BF16),
+        pltpu.VMEM((slots * station_blocks + 1, 4 * epochs, 2 * SBLOCK), BF16),
         pltpu.VMEM((2, 1, CBLOCK), F32),
         pltpu.VMEM((2, SBLOCK, LANES), F32),
         pltpu.VMEM((2, SBLOCK, LANES), F32),
     ]
     if ranks is None:
-        kernel, shapes, aliases = near_kernel, [total, (2, LANES)], {}
+        kernel, shapes, aliases = near_kernel, [total], {}
     else:
         kernel, cells = far_kernel, (epochs, cell_blocks * CBLOCK)
         shapes = [cells, cells, (ranks, 1, LANES), total]
@@ -642,12 +661,13 @@
     returned = to_partner(parts[2])
     given = across(far_parts(parts, returned))
     mine = forward(near_slots, after(near, returned), values, turned)
-    given = after(given, mine)
+    sums = small_call(squares_kernel, (2, LANES), "squares", *after((old_grad, direction), mine))
+    given = after(given, (mine, sums))
     mine = small_call(add_kernel, mine.shape, "add", mine, given)
     images = both_images(mine, to_partner(mine))
 
     far_images = across(images)
-    near_total, sums = adjoint(near_slots, near, [residuals, images], cell_rows, direction, old_grad)
+    (near_total,) = adjoint(near_slots, near, [residuals, images], cell_rows)
     far_images = after(far_images, near_total)
     thirds = to_partner(pair_up(far_residuals[0], far_images[0]))
     constant, slope, stats, _ = adjoint(

time: 75 us -> 75.1 us (level); the launches traced: 73.7 us -> 75.6 us
  blocking collectives: 18.4 us -> 20.7 us
  starting transfers between devices: 25.3 us -> 24.5 us
    all_to_all x1, blocking collectives: 18.4 us -> 20.7 us  [shards(): stats = lax.all_to_all(stats, 'tile', 0, 0)]
    ppermute x6, starting transfers between devices: 22.5 us -> 21.7 us  [to_partner(): return lax.ppermute(array, 'tile', [(i, i ^ 1) for i in range(ranks)])]
  transfers between devices with their start and end apart: 10 -> 10, of which waited for: 4 -> 4; matrix products, arithmetic and copies ran while one was open for 0% -> 0% of each run, Pallas kernels for 22% -> 23%
where the time goes in v6:
time: 75.1 us; the launch traced here: 75.6 us
  Pallas kernels  25.2 us (34%)
  starting transfers between devices  24.5 us (33%)
  blocking collectives  20.7 us (28%)
  waiting for transfers between devices  4.16 us (6%)
  between operations  0.88 us (1%)
    ppermute x6, starting transfers between devices, to_partner(): return lax.ppermute(array, 'tile', [(i, i ^ 1) for i in range(ranks)])  21.7 us
    all_to_all x1, blocking collectives, shards(): stats = lax.all_to_all(stats, 'tile', 0, 0)  20.7 us
    pallas_call x2, Pallas kernels, adjoint(): pl.pallas_call(functools.partial(kernel, sizes), out_shape=tuple((jax.Sha...  11.2 us
    pallas_call x2, Pallas kernels, forward(): pl.pallas_call(functools.partial(forward_kernel, sizes), out_shape=jax.Sh...  8.86 us
    ppermute x6, waiting for transfers between devices, to_partner(): return lax.ppermute(array, 'tile', [(i, i ^ 1) for i in range(ranks)])  4.15 us
    ppermute x4, starting transfers between devices, across(): return lax.ppermute(message, 'tile', ends + [(j, i) for i, j in ends])  2.83 us
    pallas_call x1, Pallas kernels, finish(): pl.pallas_call(finish_kernel, out_shape=tuple((jax.ShapeDtypeStruct(shape...  2.22 us
    pallas_call x1, Pallas kernels, prepare(): pl.pallas_call(functools.partial(prepare_kernel, scale), grid=(PARTS,), o...  1.54 us
  transfers between devices with their start and end apart: 10, of which 4 were waited for; matrix products, arithmetic and copies ran while one was open for 0% of the time, Pallas kernels for 23%

profile of v6, /device:TPU:0, one launch (start us, length us, event | category | flops | bytes accessed | tf_op | source)
XLA Modules:
  0.0 75.6 jit_solution(11613222038646721615)
XLA Ops:
  0.6 1.0 %pack.1 = (f32[40,128]{1,0:T(8,128)S(1)}, f32[8,16,256]{2,1,0:T(8,128)S(1)}) custom-call(f32[2,2048]{1,0:T(2,128)} %offsets_any.1, s32[8,8]{1,0:T(8,128)} %pairs_any.1, f32[16,2048]{1,0:T(8,128)} %residual_any.1), custom_call_target="tpu_custom_call" | custom-call | tf_op jit(solution)/shard_map/pack/pallas_call | solution.py:78
  1.6 0.5 collective-permute-start.2
  2.1 0.1 collective-permute-start
  2.2 1.5 %prepare.1 = (bf16[32,32,512]{2,1,0:T(8,128)(2,1)S(1)}, f32[2,16384]{1,0:T(2,128)S(1)}, f32[128,128]{1,0:T(8,128)S(1)}) custom-call(s32[128,128]{1,0:T(8,128)} %bitcast.12, s32[1,16384]{1,0:T(1,128)} %bitcast.13, f32[16,16384]{1,0:T(8,128)} %direction_ref.4), custom_call_target="tpu_custom_call" | custom-call | flops 2097152 | bytes 3145728 | tf_op jit(solution)/shard_map/prepare/pallas_call | solution.py:166
  3.8 0.0 collective-permute-done.second_ref.refs_1_
  3.8 0.7 collective-permute-start.1
  4.5 0.0 collective-permute-done.2.second_ref
  4.5 0.7 collective-permute-start.4
  5.2 0.0 collective-permute-done.1
  5.2 5.6 %collective-permute-start.3 = (f32[40,128]{1,0:T(8,128)S(1)}, f32[40,128]{1,0:T(8,128)S(1)}, u32[]{:S(2)}, u32[]{:S(2)}) collective-permute-start(f32[40,128]{1,0:T(8,128)S(1)} %get-tuple-element.42.refs_0_), channel_id=1, source_target_pairs={{0,1},{1,0},{2,3},{3,2},{4,5},{5,4},{6,7},{7,6},{8,9},{9,8},{10,11... | collective-permute-start | bytes 61448 | tf_op jit(solution)/shard_map/ppermute | solution.py:639
  10.8 0.8 %collective-permute-done.3.refs_2_ = f32[40,128]{1,0:T(8,128)S(1)} collective-permute-done((f32[40,128]{1,0:T(8,128)S(1)}, f32[40,128]{1,0:T(8,128)S(1)}, u32[]{:S(2)}, u32[]{:S(2)}) %collective-permute-start.3) | collective-permute-done | bytes 20512 | tf_op jit(solution)/shard_map/ppermute | solution.py:639
  11.7 3.0 %forward.2.parts_ref = f32[3,8,16,256]{3,2,1,0:T(8,128)S(1)} custom-call(f32[40,128]{1,0:T(8,128)S(1)} %get-tuple-element.42.refs_0_, f32[40,128]{1,0:T(8,128)S(1)} %get-tuple-element.41.refs_1_, f32[40,128]{1,0:T(8,128)S(1)} %collective-permute-done.3.refs_2_, bf16[32,32,512]{2,1,0:T(8,128)(2,1)S(1)} %get-tuple-element.24.refs_3_.refs_2_, ...), custom_call_target="tpu_custom_call" | custom-call | flops 1195376640 | bytes 1048576 | tf_op jit(solution)/shard_map/forward/pallas_call | solution.py:354
  14.6 0.0 collective-permute-done.4.refs_3_
  14.7 3.6 %collective-permute-start.5 = (f32[8,16,256]{2,1,0:T(8,128)S(1)}, f32[8,16,256]{2,1,0:T(8,128)S(1)}, u32[]{:S(2)}, u32[]{:S(2)}) collective-permute-start(f32[8,16,256]{2,1,0:T(8,128)S(1)} %slice_bitcast_fusion.2), channel_id=1, source_target_pairs={{0,1},{1,0},{2,3},{3,2},{4,5},{5,4},{6,7},{7,6},{8,9},{9,8},{10,11... | collective-permute-start | bytes 393224 | tf_op jit(solution)/shard_map/ppermute | solution.py:639
  18.2 1.0 %collective-permute-done.5.third_ref = f32[8,16,256]{2,1,0:T(8,128)S(1)} collective-permute-done((f32[8,16,256]{2,1,0:T(8,128)S(1)}, f32[8,16,256]{2,1,0:T(8,128)S(1)}, u32[]{:S(2)}, u32[]{:S(2)}) %collective-permute-start.5) | collective-permute-done | bytes 131104 | tf_op jit(solution)/shard_map/ppermute | solution.py:639
  19.2 0.0 copy-start
  19.3 0.0 copy-start.1
  19.3 0.8 %collective-permute-start.6 = (f32[2,8,16,256]{3,2,1,0:T(8,128)S(1)}, f32[2,8,16,256]{3,2,1,0:T(8,128)S(1)}, u32[]{:S(2)}, u32[]{:S(2)}) collective-permute-start(f32[2,8,16,256]{3,2,1,0:T(8,128)S(1)} %far_parts.1), channel_id=1, source_target_pairs={{1,2},{3,4},{5,6},{7,8},{9,10},{11,12},{13,14},{2,1},{4,3},{6,5},{... | collective-permute-start | bytes 786440 | tf_op jit(solution)/shard_map/ppermute | solution.py:643
  20.1 5.9 %forward.3.left_ref = f32[2,8,16,256]{3,2,1,0:T(8,128)S(1)} custom-call(f32[40,128]{1,0:T(8,128)S(1)} %get-tuple-element.31.first_ref.refs_0_, f32[40,128]{1,0:T(8,128)S(1)} %collective-permute-done.second_ref.refs_1_, bf16[32,32,512]{2,1,0:T(8,128)(2,1)S(1)} %get-tuple-element.24.refs_3_.refs_2_, f32[128,128]{1,0:T(8,128)S(1)} %get-tuple-element.28.refs_4_.refs_3_), custom_call_target="tpu_custom_call" | custom-call | flops 7864320000 | bytes 1048576 | tf_op jit(solution)/shard_map/forward/pallas_call | solution.py:354
  26.0 0.3 squares.1.refs_8_
  26.3 0.0 collective-permute-done.6.right_ref
  26.4 6.4 %collective-permute-start.7 = (f32[2,8,16,256]{3,2,1,0:T(8,128)S(1)}, f32[2,8,16,256]{3,2,1,0:T(8,128)S(1)}, u32[]{:S(2)}, u32[]{:S(2)}) collective-permute-start(f32[2,8,16,256]{3,2,1,0:T(8,128)S(1)} %add.1.mine_ref), channel_id=1, source_target_pairs={{0,1},{1,0},{2,3},{3,2},{4,5},{5,4},{6,7},{7,6},{8,9},{9,8},{10,11... | collective-permute-start | bytes 786440 | tf_op jit(solution)/shard_map/ppermute | solution.py:639
  32.8 1.1 %collective-permute-done.7.theirs_ref = f32[2,8,16,256]{3,2,1,0:T(8,128)S(1)} collective-permute-done((f32[2,8,16,256]{3,2,1,0:T(8,128)S(1)}, f32[2,8,16,256]{3,2,1,0:T(8,128)S(1)}, u32[]{:S(2)}, u32[]{:S(2)}) %collective-permute-start.7) | collective-permute-done | bytes 262176 | tf_op jit(solution)/shard_map/ppermute | solution.py:639
  34.0 0.7 collective-permute-start.8
  34.7 0.0 copy-start.2
  34.7 6.8 %near.1.refs_7_ = f32[32,32,512]{2,1,0:T(8,128)S(1)} custom-call(f32[40,128]{1,0:T(8,128)S(1)} %get-tuple-element.31.first_ref.refs_0_, f32[40,128]{1,0:T(8,128)S(1)} %collective-permute-done.second_ref.refs_1_, f32[2,8,16,256]{3,2,1,0:T(8,128)S(1)} %pair.4.refs_2_, f32[2,8,16,256]{3,2,1,0:T(8,128)S(1)} %both_images.1.refs_3_.refs_11_.image_ref, ...), custom_call_target="tpu_custom_call" | custom-call | flops 7864320000 | bytes 1048576 | tf_op jit(solution)/shard_map/near/pallas_call | solution.py:557
  41.5 0.0 collective-permute-done.8.refs_4_
  41.6 5.5 %collective-permute-start.9 = (f32[2,8,16,256]{3,2,1,0:T(8,128)S(1)}, f32[2,8,16,256]{3,2,1,0:T(8,128)S(1)}, u32[]{:S(2)}, u32[]{:S(2)}) collective-permute-start(f32[2,8,16,256]{3,2,1,0:T(8,128)S(1)} %pair.5), channel_id=1, source_target_pairs={{0,1},{1,0},{2,3},{3,2},{4,5},{5,4},{6,7},{7,6},{8,9},{9,8},{10,11... | collective-permute-start | bytes 786440 | tf_op jit(solution)/shard_map/ppermute | solution.py:639
  47.1 1.2 %collective-permute-done.9.refs_5_ = f32[2,8,16,256]{3,2,1,0:T(8,128)S(1)} collective-permute-done((f32[2,8,16,256]{3,2,1,0:T(8,128)S(1)}, f32[2,8,16,256]{3,2,1,0:T(8,128)S(1)}, u32[]{:S(2)}, u32[]{:S(2)}) %collective-permute-start.9) | collective-permute-done | bytes 262176 | tf_op jit(solution)/shard_map/ppermute | solution.py:639
  48.2 4.4 %far.1 = (f32[16,16384]{1,0:T(8,128)S(1)}, f32[16,16384]{1,0:T(8,128)S(1)}, f32[16,1,128]{2,1,0:T(1,128)S(1)}, f32[32,32,512]{2,1,0:T(8,128)S(1)}) custom-call(f32[40,128]{1,0:T(8,128)S(1)} %get-tuple-element.42.refs_0_, f32[40,128]{1,0:T(8,128)S(1)} %get-tuple-element.41.refs_1_, ...), custom_call_target="tpu_custom_call", output_to_operand_aliasing={{3}: (7, {})} | custom-call | flops 11953766400 | bytes 1048576 | tf_op jit(solution)/shard_map/far/pallas_call | solution.py:557
  52.6 20.7 %all_to_all.5.stats_ref = f32[16,1,128]{2,1,0:T(1,128)S(1)} all-to-all(f32[16,1,128]{2,1,0:T(1,128)S(1)} %get-tuple-element.38), channel_id=1, replica_groups=mesh['groups'=2,'tile'=16] {'tile'}, dimensions={0} | all-to-all | bytes 16384 | tf_op jit(solution)/shard_map/all_to_all | solution.py:677
  73.3 2.2 %finish.1 = (f32[16,16384]{1,0:T(8,128)}, f32[16,2048]{1,0:T(8,128)}, f32[16,16384]{1,0:T(8,128)}) custom-call(f32[16,1,128]{2,1,0:T(1,128)S(1)} %all_to_all.5.stats_ref, f32[16,16384]{1,0:T(8,128)S(1)} %get-tuple-element.39.constant_ref, f32[16,16384]{1,0:T(8,128)S(1)} %get-tuple-element.40.slope_ref, f32[16,16384]{1,0:T(8,128)S(1)} %copy-done.2, ...), custom_call_target="tpu_custom_call" | custom-call | tf_op jit(solution)/shard_map/finish/pallas_call | solution.py:616
  (13 shorter events, 0.2 us)
Async XLA Ops:
  1.6 2.8 %collective-permute-start.2 = (f32[8,16,256]{2,1,0:T(8,128)S(1)}, f32[8,16,256]{2,1,0:T(8,128)S(1)}, u32[]{:S(2)}, u32[]{:S(2)}) collective-permute-start(f32[8,16,256]{2,1,0:T(8,128)S(1)} %get-tuple-element.26.first_ref.residual_ref), channel_id=1, source_target_pairs={{0,1},{1,0},{2,3},{3,2},{4,5},{5,4},{6,7},{7,6},{8,9},{9,8},{10,11... | collective-permute-start | bytes 393224 | tf_op jit(solution)/shard_map/ppermute | solution.py:639
  2.1 1.6 %collective-permute-start = (f32[40,128]{1,0:T(8,128)S(1)}, f32[40,128]{1,0:T(8,128)S(1)}, u32[]{:S(2)}, u32[]{:S(2)}) collective-permute-start(f32[40,128]{1,0:T(8,128)S(1)} %get-tuple-element.31.first_ref.refs_0_), channel_id=1, source_target_pairs={{0,1},{1,0},{2,3},{3,2},{4,5},{5,4},{6,7},{7,6},{8,9},{9,8},{10,11... | collective-permute-start | bytes 61448 | tf_op jit(solution)/shard_map/ppermute | solution.py:639
  3.8 1.4 %collective-permute-start.1 = (f32[2,40,128]{2,1,0:T(8,128)S(1)}, f32[2,40,128]{2,1,0:T(8,128)S(1)}, u32[]{:S(2)}, u32[]{:S(2)}) collective-permute-start(f32[2,40,128]{2,1,0:T(8,128)S(1)} %pair.3), channel_id=1, source_target_pairs={{1,2},{3,4},{5,6},{7,8},{9,10},{11,12},{13,14},{2,1},{4,3},{6,5},{... | collective-permute-start | bytes 122888 | tf_op jit(solution)/shard_map/ppermute | solution.py:643
  4.5 10.1 %collective-permute-start.4 = (f32[2,8,16,256]{3,2,1,0:T(8,128)S(1)}, f32[2,8,16,256]{3,2,1,0:T(8,128)S(1)}, u32[]{:S(2)}, u32[]{:S(2)}) collective-permute-start(f32[2,8,16,256]{3,2,1,0:T(8,128)S(1)} %pair.4.refs_2_), channel_id=1, source_target_pairs={{1,2},{3,4},{5,6},{7,8},{9,10},{11,12},{13,14},{2,1},{4,3},{6,5},{... | collective-permute-start | bytes 786440 | tf_op jit(solution)/shard_map/ppermute | solution.py:643
  5.2 6.5 %collective-permute-start.3 = (f32[40,128]{1,0:T(8,128)S(1)}, f32[40,128]{1,0:T(8,128)S(1)}, u32[]{:S(2)}, u32[]{:S(2)}) collective-permute-start(f32[40,128]{1,0:T(8,128)S(1)} %get-tuple-element.42.refs_0_), channel_id=1, source_target_pairs={{0,1},{1,0},{2,3},{3,2},{4,5},{5,4},{6,7},{7,6},{8,9},{9,8},{10,11... | collective-permute-start | bytes 61448 | tf_op jit(solution)/shard_map/ppermute | solution.py:639
  14.7 4.6 %collective-permute-start.5 = (f32[8,16,256]{2,1,0:T(8,128)S(1)}, f32[8,16,256]{2,1,0:T(8,128)S(1)}, u32[]{:S(2)}, u32[]{:S(2)}) collective-permute-start(f32[8,16,256]{2,1,0:T(8,128)S(1)} %slice_bitcast_fusion.2), channel_id=1, source_target_pairs={{0,1},{1,0},{2,3},{3,2},{4,5},{5,4},{6,7},{7,6},{8,9},{9,8},{10,11... | collective-permute-start | bytes 393224 | tf_op jit(solution)/shard_map/ppermute | solution.py:639
  19.2 6.8 %copy-start = (f32[16,16384]{1,0:T(8,128)S(1)}, f32[16,16384]{1,0:T(8,128)}, u32[]{:S(2)}) copy-start(f32[16,16384]{1,0:T(8,128)} %direction_ref.4) | copy-start | bytes 3145732
  19.3 6.7 %copy-start.1 = (f32[16,16384]{1,0:T(8,128)S(1)}, f32[16,16384]{1,0:T(8,128)}, u32[]{:S(2)}) copy-start(f32[16,16384]{1,0:T(8,128)} %old_ref) | copy-start | bytes 3145732
  19.3 7.1 %collective-permute-start.6 = (f32[2,8,16,256]{3,2,1,0:T(8,128)S(1)}, f32[2,8,16,256]{3,2,1,0:T(8,128)S(1)}, u32[]{:S(2)}, u32[]{:S(2)}) collective-permute-start(f32[2,8,16,256]{3,2,1,0:T(8,128)S(1)} %far_parts.1), channel_id=1, source_target_pairs={{1,2},{3,4},{5,6},{7,8},{9,10},{11,12},{13,14},{2,1},{4,3},{6,5},{... | collective-permute-start | bytes 786440 | tf_op jit(solution)/shard_map/ppermute | solution.py:643
  26.4 7.6 %collective-permute-start.7 = (f32[2,8,16,256]{3,2,1,0:T(8,128)S(1)}, f32[2,8,16,256]{3,2,1,0:T(8,128)S(1)}, u32[]{:S(2)}, u32[]{:S(2)}) collective-permute-start(f32[2,8,16,256]{3,2,1,0:T(8,128)S(1)} %add.1.mine_ref), channel_id=1, source_target_pairs={{0,1},{1,0},{2,3},{3,2},{4,5},{5,4},{6,7},{7,6},{8,9},{9,8},{10,11... | collective-permute-start | bytes 786440 | tf_op jit(solution)/shard_map/ppermute | solution.py:639
  34.0 7.5 %collective-permute-start.8 = (f32[2,8,16,256]{3,2,1,0:T(8,128)S(1)}, f32[2,8,16,256]{3,2,1,0:T(8,128)S(1)}, u32[]{:S(2)}, u32[]{:S(2)}) collective-permute-start(f32[2,8,16,256]{3,2,1,0:T(8,128)S(1)} %both_images.1.refs_3_.refs_11_.image_ref), channel_id=1, source_target_pairs={{1,2},{3,4},{5,6},{7,8},{9,10},{11,12},{13,14},{2,1},{4,3},{6,5},{... | collective-permute-start | bytes 786440 | tf_op jit(solution)/shard_map/ppermute | solution.py:643
  34.7 13.6 %copy-start.2 = (f32[16,16384]{1,0:T(8,128)S(1)}, f32[16,16384]{1,0:T(8,128)}, u32[]{:S(2)}) copy-start(f32[16,16384]{1,0:T(8,128)} %model_ref.1) | copy-start | bytes 3145732
  41.6 6.7 %collective-permute-start.9 = (f32[2,8,16,256]{3,2,1,0:T(8,128)S(1)}, f32[2,8,16,256]{3,2,1,0:T(8,128)S(1)}, u32[]{:S(2)}, u32[]{:S(2)}) collective-permute-start(f32[2,8,16,256]{3,2,1,0:T(8,128)S(1)} %pair.5), channel_id=1, source_target_pairs={{0,1},{1,0},{2,3},{3,2},{4,5},{5,4},{6,7},{7,6},{8,9},{9,8},{10,11... | collective-permute-start | bytes 786440 | tf_op jit(solution)/shard_map/ppermute | solution.py:639
